TPU v7x, 768 devices: a whole 4x8x12 slice. The times are simulated.
768 devices in a mesh: gx: 96 (over y, z), gy: 8 (over x, core).
Axes of the slice: x: 4, y: 8, z: 12, core: 2. Of those that a mesh axis runs over, the one named last changes fastest.
Arguments:
- state: bfloat16 [6, 125, 393216], P(None, None, ('gx', 'gy')), may hold values from -6 to 6
- forcing: bfloat16 [6, 125, 393216], P(None, None, ('gx', 'gy')), may hold values from -6 to 6
- volume_flux_matrix: bfloat16 [125, 125], replicated, may hold values from -0.5 to 0.5
- viscous_matrix: bfloat16 [125, 125], replicated, may hold values from -0.5 to 0.5
- linear_flux_matrix: float32 [6, 6], replicated, may hold values from -2.5 to 2.5
- viscosity: float32 [393216], P(('gx', 'gy')), may hold values from 0.1 to 1
- lift: bfloat16 [6, 125, 25], replicated, may hold values from -0.5 to 0.5
- wall_flags: int32 [393216], P(('gx', 'gy')), may hold values 0 or 1
- restriction_weight: float32 [8, 125], replicated, may hold values from -0.1875 to 0.1875
- owner: int32 [393216, 1], P(('gx', 'gy')), may hold values from 0 to 7; in each aligned block of 512 rows (0 to 511, 512 to 1023, ...) at most 256 rows name the same one
- slot: int32 [393216], P(('gx', 'gy')), may hold values from 0 to 31
- coarse_inverse: float32 [48, 48, 24576], P(None, None, ('gx', 'gy')), as said below
- coupling: float32 [48, 48], replicated, may hold values from -0.4375 to 0.4375
- prolongation_weight: float32 [125, 8], replicated, may hold values from -2 to 2
Outputs:
- residual: bfloat16 [6, 125, 393216], P(None, None, ('gx', 'gy'))
- correction: bfloat16 [6, 125, 393216], P(None, None, ('gx', 'gy'))
Inputs may be any that keep to these rules, and one draw needn't show every extreme that they name: `owner`: from the elements of one device at most 256 name one member, and some device gives exactly 256 elements to some member. `coarse_inverse`: one 48 x 48 block for each agglomerate.
All inputs are finite; a program needn't handle non-finite values. No bound on the sum of `wall_flags` on one device may be relied on, other than what follows from the above.
Results may differ from a plain program's by a relative error of at most 0.004.
Values may be sent and summed in bfloat16 or wider, within the bound.
No kernel may reach another device: no remote copies, remote signals or barrier semaphores. Data moves between devices by JAX's collectives and lax.ppermute only.
A program may use at most 64 MiB of HBM per device.

v0:
```python
import jax
import jax.numpy as jnp
from jax import lax
from jax.sharding import PartitionSpec as P

AX = 2
ASLOT = 32
SWEEPS = 3


relaxation = 0.7
wall_rate = 2.0
finest_level = lax.Precision.HIGHEST


def padded_2(value, sides, width):
    for axis, dim in sides:
        size, length = (lax.axis_size(axis), value.shape[dim])
        up = [(i, (i + 1) % size) for i in range(size)]
        down = [(j, i) for i, j in up]
        last = lax.slice_in_dim(value, length - width, length, axis=dim)
        first = lax.slice_in_dim(value, 0, width, axis=dim)
        before = lax.ppermute(last, axis, up)
        after = lax.ppermute(first, axis, down)
        value = jnp.concatenate([before, value, after], axis=dim)
    return value


def per_device(
    state,
    forcing,
    volume_flux_matrix,
    viscous_matrix,
    linear_flux_matrix,
    viscosity,
    lift,
    wall_flags,
    restriction_weight,
    owner,
    slot,
    coarse_inverse,
    coupling,
    prolongation_weight,
):
    element_rows = state.shape[2]
    z_cells = element_rows // AX
    nodal_vals = state.reshape(6, 5, 5, 5, AX, z_cells)

    def face_trace(face_nodes):
        return face_nodes.reshape(6, 25, AX, z_cells)

    owned = [
        face_trace(nodal_vals[:, 0]),
        face_trace(nodal_vals[:, 4]),
        face_trace(nodal_vals[:, :, 0]),
        face_trace(nodal_vals[:, :, 4]),
        face_trace(nodal_vals[:, :, :, 0]),
        face_trace(nodal_vals[:, :, :, 4]),
    ]
    padded = padded_2(state.reshape(6, 125, AX, 1, z_cells), (("gx", 2), ("gy", 3)), 1)
    rim_cells = padded.reshape(6, 5, 5, 5, AX + 2, 3, z_cells)
    near_low_x = rim_cells[:, 4, :, :, 0:AX, 1].reshape(6, 25, AX, z_cells)
    near_high_x = rim_cells[:, 0, :, :, 2 : AX + 2, 1].reshape(6, 25, AX, z_cells)
    near_low_y = rim_cells[:, :, 4, :, 1 : AX + 1, 0].reshape(6, 25, AX, z_cells)
    near_high_y = rim_cells[:, :, 0, :, 1 : AX + 1, 2].reshape(6, 25, AX, z_cells)
    wall_zero = jnp.zeros_like(owned[0][..., :1])
    near_low_z = jnp.concatenate([wall_zero, owned[5][..., :-1]], axis=3)
    near_high_z = jnp.concatenate([owned[4][..., 1:], wall_zero], axis=3)
    nearby = [near_low_x, near_high_x, near_low_y, near_high_y, near_low_z, near_high_z]
    interface_jumps = jnp.stack(
        [
            (nearby[face_no].astype(jnp.float32) - owned[face_no].astype(jnp.float32)).reshape(
                6, 25, element_rows
            )
            for face_no in range(6)
        ]
    ).astype(jnp.bfloat16)
    lifted_values = jnp.einsum(
        "poc,pbcj->boj", lift, interface_jumps, preferred_element_type=jnp.float32
    )
    stiffness_matrix = jnp.einsum(
        "sz,izy->isy", volume_flux_matrix, state, preferred_element_type=jnp.float32
    )
    flux_contribution = jnp.einsum(
        "qk,kgs->qgs", linear_flux_matrix, stiffness_matrix, precision=finest_level
    )
    viscous_update = jnp.einsum(
        "sz,izy->isy", viscous_matrix, state, preferred_element_type=jnp.float32
    )
    marker = (jnp.arange(6) == 5).astype(jnp.float32)[:, None, None]
    wall_term = (
        wall_rate
        * marker
        * wall_flags.astype(jnp.float32)[None, None, :]
        * state.astype(jnp.float32)
    )
    complete_residual = (
        forcing.astype(jnp.float32)
        - flux_contribution
        - viscosity[None, None, :] * viscous_update
        - wall_term
        + lifted_values
    )
    restricted_values = jnp.einsum(
        "wo,xoi->xwi", restriction_weight, complete_residual, precision=finest_level
    ).reshape(48, element_rows)
    members = lax.axis_size("gy")
    target = owner[:, 0]
    agg_keys = target * ASLOT + slot
    spread = (agg_keys[:, None] == jnp.arange(members * ASLOT, dtype=jnp.int32)[None, :]).astype(
        jnp.float32
    )
    partial_sums = jnp.dot(restricted_values, spread, precision=finest_level)
    totals = lax.psum_scatter(partial_sums, "gy", scatter_dimension=1, tiled=True)
    coarse = relaxation * jnp.einsum("ija,ja->ia", coarse_inverse, totals, precision=finest_level)
    for sweep_no in range(SWEEPS - 1):
        loop_view = padded_2(coarse[None], (("gx", 0),), 1)
        beside_all = loop_view[0] + loop_view[2]
        source = totals - jnp.dot(coupling, beside_all, precision=finest_level)
        coarse = (1.0 - relaxation) * coarse + relaxation * jnp.einsum(
            "ija,ja->ia", coarse_inverse, source, precision=finest_level
        )
    everything = lax.all_gather(coarse, "gy", axis=1, tiled=True)
    chosen_rows = jnp.take(everything, target * ASLOT + slot, axis=1).reshape(6, 8, element_rows)
    correction = jnp.einsum("az,tzl->tal", prolongation_weight, chosen_rows, precision=finest_level)
    return (complete_residual.astype(jnp.bfloat16), correction.astype(jnp.bfloat16))


def solution(mesh):
    return jax.shard_map(
        per_device,
        mesh=mesh,
        in_specs=(
            P(None, None, ("gx", "gy")),
            P(None, None, ("gx", "gy")),
            P(),
            P(),
            P(),
            P(("gx", "gy")),
            P(),
            P(("gx", "gy")),
            P(),
            P(("gx", "gy"), None),
            P(("gx", "gy")),
            P(None, None, ("gx", "gy")),
            P(),
            P(),
        ),
        out_specs=(P(None, None, ("gx", "gy")), P(None, None, ("gx", "gy"))),
        check_vma=False,
    )
```

profile of v0, /device:TPU:1, one launch (start us, length us, event | category | flops | bytes accessed | tf_op | source)
XLA Modules:
  0.0 194.3 jit_solution(15694739512195333340)
XLA Ops:
  7.2 1.5 copy.146
  8.8 1.0 copy.148
  9.8 4.8 %collective-permute-start = (bf16[6,125,1,1,256]{4,1,3,2,0:T(8,128)(2,1)}, bf16[6,125,1,1,256]{4,1,3,2,0:T(8,128)(2,1)}, u32[]{:S(2)}, u32[]{:S(2)}) collective-permute-start(bf16[6,125,1,1,256]{4,1,3,2,0:T(8,128)(2,1)} %copy.148), channel_id=1, source_target_pairs={{0,8},{8,16},{16,24},{24,32},{32,40},{40,48},{48,56},{56,64},{64,7... | collective-permute-start | bytes 1152008 | tf_op jit(solution)/shard_map/ppermute | solution.py:23
  14.6 1.0 copy.149
  15.6 15.1 %collective-permute-start.1 = (bf16[6,125,1,1,256]{4,1,3,2,0:T(8,128)(2,1)}, bf16[6,125,1,1,256]{4,1,3,2,0:T(8,128)(2,1)}, u32[]{:S(2)}, u32[]{:S(2)}) collective-permute-start(bf16[6,125,1,1,256]{4,1,3,2,0:T(8,128)(2,1)} %copy.149), channel_id=1, source_target_pairs={{8,0},{16,8},{24,16},{32,24},{40,32},{48,40},{56,48},{64,56},{72,6... | collective-permute-start | bytes 1152008 | tf_op jit(solution)/shard_map/ppermute | solution.py:24
  30.7 0.3 reshape.179
  31.0 1.1 fusion.12
  32.1 0.2 fusion.10
  32.3 0.2 fusion.31
  32.5 0.3 subtract_convert_fusion.5
  32.9 0.2 slice.71
  33.1 2.0 %reshape.212 = f32[1,6,25,512]{3,2,0,1:T(8,128)} reshape(f32[6,1,5,5,2,256]{5,4,1,3,2,0:T(2,128)} %get-tuple-element.27) | data formatting | bytes 614400 | tf_op jit(solution)/shard_map/convert_element_type | solution.py:72
  35.1 1.0 reshape.214
  36.1 1.0 reshape.216
  37.1 1.0 reshape.218
  38.1 0.8 stack_reshape.12
  38.9 0.4 convolution_bitcast_fusion
  39.3 1.9 copy.150
  41.2 1.9 copy.151
  43.2 2.6 %pad_maximum_fusion.1 = bf16[6,125,4,1,256]{1,4,2,0,3:T(8,128)(2,1)} fusion(bf16[6,125,1,1,256]{1,4,2,0,3:T(8,128)(2,1)} %copy.151, bf16[6,125,2,1,256]{1,4,2,0,3:T(8,128)(2,1)S(1)} %bitcast.142, bf16[6,125,1,1,256]{1,4,2,0,3:T(8,128)(2,1)} %copy.150), kind=kLoop, calls=%fused_computation.2 | loop fusion | flops 1536000 | bytes 3072000 | tf_op jit(solution)/shard_map/concatenate | solution.py:25
  45.8 3.7 %copy.152 = bf16[6,125,4,1,256]{4,2,3,1,0:T(4,128)(2,1)} copy(bf16[6,125,4,1,256]{1,4,2,0,3:T(8,128)(2,1)} %pad_maximum_fusion.1) | data formatting | bytes 3072000 | tf_op jit(solution)/shard_map/concatenate | solution.py:25
  49.5 2.1 %collective-permute-start.2 = (bf16[6,125,4,1,256]{4,2,3,1,0:T(4,128)(2,1)}, bf16[6,125,4,1,256]{4,2,3,1,0:T(4,128)(2,1)}, u32[]{:S(2)}, u32[]{:S(2)}) collective-permute-start(bf16[6,125,4,1,256]{4,2,3,1,0:T(4,128)(2,1)} %copy.152), channel_id=1, source_target_pairs={{0,1},{1,2},{2,3},{3,4},{4,5},{5,6},{6,7},{7,0},{8,9},{9,10},{10,1... | collective-permute-start | bytes 4608008 | tf_op jit(solution)/shard_map/ppermute | solution.py:23
  51.6 0.9 subtract_convert_fusion.4
  52.5 1.7 stack_reshape.13
  54.2 2.0 %copy.143 = f32[6,125,512]{2,0,1:T(8,128)} copy(f32[6,125,512]{1,2,0:T(8,128)S(1)} %convolution_bitcast_fusion) | data formatting | bytes 3072000 | tf_op jit(solution)/shard_map/sz,izy->isy/transpose | solution.py:81
  56.1 4.9 %fusion.27 = f32[125,512,6]{1,2,0:T(8,128)} fusion(f32[6,125,512]{2,0,1:T(8,128)} %copy.143, f32[6,6]{1,0:T(8,128)S(1)} %copy-done.19), kind=kOutput, calls=%fused_computation.63 | convolution fusion | flops 27648000 | bytes 3072144 | tf_op jit(solution)/shard_map/qk,kgs->qgs/dot_general | solution.py:84
  61.1 1.9 copy.144
  63.0 2.3 %copy.141 = bf16[6,125,512]{1,2,0:T(8,128)(2,1)} copy(bf16[6,125,512]{2,1,0:T(8,128)(2,1)} %param.15) | data formatting | bytes 1536000 | tf_op args[1]
  65.4 1.6 fusion.17
  67.0 1.9 collective-permute-done.2
  68.9 3.7 %copy.154 = bf16[6,125,4,1,256]{1,4,2,0,3:T(8,128)(2,1)} copy(bf16[6,125,4,1,256]{4,2,3,1,0:T(4,128)(2,1)} %collective-permute-done.2) | data formatting | bytes 3072000 | tf_op jit(solution)/shard_map/ppermute | solution.py:23
  72.6 3.8 %copy.155 = bf16[6,125,4,1,256]{1,4,2,0,3:T(8,128)(2,1)} copy(bf16[6,125,4,1,256]{4,2,3,1,0:T(4,128)(2,1)} %collective-permute-done.3) | data formatting | bytes 3072000 | tf_op jit(solution)/shard_map/ppermute | solution.py:24
  76.4 5.2 %pad_maximum_fusion = bf16[6,125,4,3,256]{1,4,2,0,3:T(8,128)(2,1)} fusion(bf16[6,125,4,1,256]{1,4,2,0,3:T(8,128)(2,1)} %copy.155, bf16[6,125,1,1,256]{1,4,2,0,3:T(8,128)(2,1)S(1)} %copy-done.4, bf16[6,125,2,1,256]{1,4,2,0,3:T(8,128)(2,1)S(1)} %bitcast.143, bf16[6,125,1,1,256]{1,4,2,0,3:T(8,128)(2,1)S(1)} %copy-done.3, bf16[6,125,4,1,256]{1,4,2,0,3:T(8,128)(2,1)} %copy.154), kind=kLoop, calls=%fused_computation.1 | loop fusion | flops 9216000 | bytes 9216000 | tf_op jit(solution)/shard_map/concatenate | solution.py:25
  81.6 8.5 %copy.156 = bf16[6,125,4,3,256]{4,2,3,1,0:T(4,128)(2,1)} copy(bf16[6,125,4,3,256]{1,4,2,0,3:T(8,128)(2,1)} %pad_maximum_fusion) | data formatting | bytes 9216000 | tf_op jit(solution)/shard_map/concatenate | solution.py:25
  90.1 2.0 %slice_convert_fusion.2 = (f32[6,1,5,5,2,1,256]{6,4,5,3,2,1,0:T(2,128)S(1)}, f32[6,1,5,5,2,1,256]{6,4,5,3,2,1,0:T(2,128)}) fusion(bf16[6,5,5,5,4,3,256]{6,4,5,3,2,1,0:T(4,128)(2,1)} %bitcast.144), kind=kLoop, calls=%fused_computation.36 | loop fusion | flops 153600 | bytes 921600 | tf_op jit(solution)/shard_map/convert_element_type | solution.py:72
  92.1 2.1 %slice_convert_fusion = (f32[6,5,1,5,2,1,256]{6,4,5,3,2,1,0:T(2,128)S(1)}, f32[6,5,1,5,2,1,256]{6,4,5,3,2,1,0:T(2,128)}) fusion(bf16[6,5,5,5,4,3,256]{6,4,5,3,2,1,0:T(4,128)(2,1)} %bitcast.145), kind=kLoop, calls=%fused_computation.30 | loop fusion | flops 153600 | bytes 921600 | tf_op jit(solution)/shard_map/convert_element_type | solution.py:72
  94.2 2.0 %reshape.211 = f32[1,6,25,512]{3,2,0,1:T(8,128)} reshape(f32[6,1,5,5,2,1,256]{6,4,5,3,2,1,0:T(2,128)} %get-tuple-element.19) | data formatting | bytes 614400 | tf_op jit(solution)/shard_map/convert_element_type | solution.py:72
  96.2 1.0 reshape.213
  97.2 2.0 %reshape.215 = f32[1,6,25,512]{3,2,0,1:T(8,128)} reshape(f32[6,5,1,5,2,1,256]{6,4,5,3,2,1,0:T(2,128)} %get-tuple-element.17) | data formatting | bytes 614400 | tf_op jit(solution)/shard_map/convert_element_type | solution.py:72
  99.2 1.0 reshape.217
  100.2 1.1 fusion.6
  101.3 1.2 fusion.7
  102.8 1.2 copy-done.2
  104.0 0.2 copy-done.5
  104.2 1.5 fusion.32
  105.7 1.5 convolution_bitcast_fusion.1
  107.2 1.4 fusion.4
  108.6 0.5 copy.178
  109.0 32.1 %reduce-scatter.2.cloned.1.call-done = f32[48,32]{0,1:T(8,128)} async-done(((f32[48,256]{0,1:T(8,128)}), f32[48,32]{0,1:T(8,128)}) %reduce-scatter.2.cloned.1.call-update) | async-done | bytes 6160 | tf_op jit(solution)/shard_map/reduce_scatter | solution.py:114
  141.1 1.5 fusion.33
  142.7 1.9 collective-permute-start.4
  144.6 6.9 %collective-permute-start.5 = (f32[1,48,32]{1,2,0:T(8,128)S(1)}, f32[1,48,32]{1,2,0:T(8,128)S(1)}, u32[]{:S(2)}, u32[]{:S(2)}) collective-permute-start(f32[1,48,32]{1,2,0:T(8,128)S(1)} %multiply_bitcast_fusion), channel_id=1, source_target_pairs={{8,0},{16,8},{24,16},{32,24},{40,32},{48,40},{56,48},{64,56},{72,6... | collective-permute-start | bytes 18440 | tf_op jit(solution)/shard_map/ppermute | solution.py:24
  151.5 0.8 collective-permute-done.5
  152.3 0.9 fusion.3
  153.2 0.7 fusion.34
  153.9 1.9 collective-permute-start.6
  155.9 7.2 %collective-permute-start.7 = (f32[1,48,32]{1,2,0:T(8,128)S(1)}, f32[1,48,32]{1,2,0:T(8,128)S(1)}, u32[]{:S(2)}, u32[]{:S(2)}) collective-permute-start(f32[1,48,32]{1,2,0:T(8,128)S(1)} %fusion.24), channel_id=1, source_target_pairs={{8,0},{16,8},{24,16},{32,24},{40,32},{48,40},{56,48},{64,56},{72,6... | collective-permute-start | bytes 18440 | tf_op jit(solution)/shard_map/ppermute | solution.py:24
  163.1 1.2 copy.171
  164.3 0.2 fusion.2
  164.5 0.7 fusion.35
  165.3 17.2 %all_gather.3 = f32[48,256]{0,1:T(8,128)S(1)} all-gather(f32[48,32]{0,1:T(8,128)S(1)} %bitcast_add_fusion.1), channel_id=1, replica_groups=mesh['gx'=96,'gy'=8] {'gy'}, dimensions={1}, use_global_device_ids=true | all-gather | bytes 55296 | tf_op jit(solution)/shard_map/all_gather | solution.py:123
  182.5 1.0 gather_fusion
  183.6 2.6 %fusion.1 = bf16[6,125,512]{1,2,0:T(8,128)(2,1)S(1)} fusion(f32[48,512]{1,0:T(8,128)S(1)} %copy.170, pred[512]{0:T(512)(128)(4,1)S(1)} %get-tuple-element.14, f32[125,8]{0,1:T(8,128)S(1)} %copy-done.21), kind=kOutput, calls=%fused_computation.9 | convolution fusion | flops 37272576 | bytes 870816 | tf_op jit(solution)/shard_map/az,tzl->tal/dot_general | solution.py:125
  186.3 1.2 copy.172
  (75 shorter events, 0.6 us)
Async XLA Ops:
  7.2 95.7 %copy-start = (bf16[6,125,25]{1,2,0:T(8,128)(2,1)S(1)}, bf16[6,125,25]{1,2,0:T(8,128)(2,1)}, u32[]{:S(2)}) copy-start(bf16[6,125,25]{1,2,0:T(8,128)(2,1)} %param.20) | copy-start | bytes 112504
  7.2 133.9 %reduce-scatter.2.cloned.1.call-start = ((), (), s32[]{:S(2)}) async-start(), calls=%async_computation.1 | async-start | bytes 147456 | tf_op jit(solution)/shard_map/reduce_scatter | solution.py:114
  8.8 22.0 %copy-start.1 = (bf16[6,125,512]{2,1,0:T(8,128)(2,1)S(1)}, bf16[6,125,512]{2,1,0:T(8,128)(2,1)}, u32[]{:S(2)}) copy-start(bf16[6,125,512]{2,1,0:T(8,128)(2,1)} %param.14) | copy-start | bytes 2304004
  9.8 29.5 %collective-permute-start = (bf16[6,125,1,1,256]{4,1,3,2,0:T(8,128)(2,1)}, bf16[6,125,1,1,256]{4,1,3,2,0:T(8,128)(2,1)}, u32[]{:S(2)}, u32[]{:S(2)}) collective-permute-start(bf16[6,125,1,1,256]{4,1,3,2,0:T(8,128)(2,1)} %copy.148), channel_id=1, source_target_pairs={{0,8},{8,16},{16,24},{24,32},{32,40},{40,48},{48,56},{56,64},{64,7... | collective-permute-start | bytes 1152008 | tf_op jit(solution)/shard_map/ppermute | solution.py:23
  15.6 25.6 %collective-permute-start.1 = (bf16[6,125,1,1,256]{4,1,3,2,0:T(8,128)(2,1)}, bf16[6,125,1,1,256]{4,1,3,2,0:T(8,128)(2,1)}, u32[]{:S(2)}, u32[]{:S(2)}) collective-permute-start(bf16[6,125,1,1,256]{4,1,3,2,0:T(8,128)(2,1)} %copy.149), channel_id=1, source_target_pairs={{8,0},{16,8},{24,16},{32,24},{40,32},{48,40},{56,48},{64,56},{72,6... | collective-permute-start | bytes 1152008 | tf_op jit(solution)/shard_map/ppermute | solution.py:24
  32.5 2.6 %copy-start.11 = (f32[6,1,5,5,2,256]{5,4,1,3,2,0:T(2,128)S(1)}, f32[6,1,5,5,2,256]{5,4,1,3,2,0:T(2,128)}, u32[]{:S(2)}) copy-start(f32[6,1,5,5,2,256]{5,4,1,3,2,0:T(2,128)} %get-tuple-element.26) | copy-start | bytes 921604
  33.1 5.8 %copy-start.17 = (bf16[125,125]{1,0:T(8,128)(2,1)S(1)}, bf16[125,125]{1,0:T(8,128)(2,1)}, u32[]{:S(2)}) copy-start(bf16[125,125]{1,0:T(8,128)(2,1)} %param.16) | copy-start | bytes 93754
  49.5 19.3 %collective-permute-start.2 = (bf16[6,125,4,1,256]{4,2,3,1,0:T(4,128)(2,1)}, bf16[6,125,4,1,256]{4,2,3,1,0:T(4,128)(2,1)}, u32[]{:S(2)}, u32[]{:S(2)}) collective-permute-start(bf16[6,125,4,1,256]{4,2,3,1,0:T(4,128)(2,1)} %copy.152), channel_id=1, source_target_pairs={{0,1},{1,2},{2,3},{3,4},{4,5},{5,6},{6,7},{7,0},{8,9},{9,10},{10,1... | collective-permute-start | bytes 4608008 | tf_op jit(solution)/shard_map/ppermute | solution.py:23
  51.6 21.0 %collective-permute-start.3 = (bf16[6,125,4,1,256]{4,2,3,1,0:T(4,128)(2,1)}, bf16[6,125,4,1,256]{4,2,3,1,0:T(4,128)(2,1)}, u32[]{:S(2)}, u32[]{:S(2)}) collective-permute-start(bf16[6,125,4,1,256]{4,2,3,1,0:T(4,128)(2,1)} %copy.152), channel_id=1, source_target_pairs={{1,0},{2,1},{3,2},{4,3},{5,4},{6,5},{7,6},{0,7},{9,8},{10,9},{11,1... | collective-permute-start | bytes 4608008 | tf_op jit(solution)/shard_map/ppermute | solution.py:24
  54.2 2.0 %copy-start.19 = (f32[6,6]{1,0:T(8,128)S(1)}, f32[6,6]{1,0:T(8,128)}, u32[]{:S(2)}) copy-start(f32[6,6]{1,0:T(8,128)} %param.18) | copy-start | bytes 436
  62.9 2.4 %copy-start.23 = (s32[512]{0:T(512)S(1)}, s32[512]{0:T(512)}, u32[]{:S(2)}) copy-start(s32[512]{0:T(512)} %param.21) | copy-start | bytes 6148
  62.9 2.4 %copy-start.24 = (s32[512,1]{0,1:T(1,128)S(1)}, s32[512,1]{0,1:T(1,128)}, u32[]{:S(2)}) copy-start(s32[512,1]{0,1:T(1,128)} %param.23) | copy-start | bytes 6148
  62.9 2.4 %copy-start.25 = (s32[512]{0:T(512)S(1)}, s32[512]{0:T(512)}, u32[]{:S(2)}) copy-start(s32[512]{0:T(512)} %param.24) | copy-start | bytes 6148
  63.0 2.5 %copy-start.18 = (bf16[125,125]{1,0:T(8,128)(2,1)S(1)}, bf16[125,125]{1,0:T(8,128)(2,1)}, u32[]{:S(2)}) copy-start(bf16[125,125]{1,0:T(8,128)(2,1)} %param.17) | copy-start | bytes 93754
  72.6 3.8 %copy-start.3 = (bf16[6,125,1,1,256]{1,4,2,0,3:T(8,128)(2,1)S(1)}, bf16[6,125,1,1,256]{1,4,2,0,3:T(8,128)(2,1)}, u32[]{:S(2)}) copy-start(bf16[6,125,1,1,256]{1,4,2,0,3:T(8,128)(2,1)} %copy.150) | copy-start | bytes 1152004
  72.6 3.8 %copy-start.4 = (bf16[6,125,1,1,256]{1,4,2,0,3:T(8,128)(2,1)S(1)}, bf16[6,125,1,1,256]{1,4,2,0,3:T(8,128)(2,1)}, u32[]{:S(2)}) copy-start(bf16[6,125,1,1,256]{1,4,2,0,3:T(8,128)(2,1)} %copy.151) | copy-start | bytes 1152004
  94.2 6.0 %copy-start.8 = (f32[1,6,25,512]{3,2,0,1:T(8,128)S(1)}, f32[1,6,25,512]{3,2,0,1:T(8,128)}, u32[]{:S(2)}) copy-start(f32[1,6,25,512]{3,2,0,1:T(8,128)} %reshape.212) | copy-start | bytes 921604
  97.2 5.4 %copy-start.7 = (f32[1,6,25,512]{3,2,0,1:T(8,128)S(1)}, f32[1,6,25,512]{3,2,0,1:T(8,128)}, u32[]{:S(2)}) copy-start(f32[1,6,25,512]{3,2,0,1:T(8,128)} %reshape.216) | copy-start | bytes 921604
  100.2 2.4 %copy-start.10 = (f32[1,6,25,512]{3,2,0,1:T(8,128)S(1)}, f32[1,6,25,512]{3,2,0,1:T(8,128)}, u32[]{:S(2)}) copy-start(f32[1,6,25,512]{3,2,0,1:T(8,128)} %reshape.215) | copy-start | bytes 921604
  100.2 2.5 %copy-start.6 = (f32[1,6,25,512]{3,2,0,1:T(8,128)S(1)}, f32[1,6,25,512]{3,2,0,1:T(8,128)}, u32[]{:S(2)}) copy-start(f32[1,6,25,512]{3,2,0,1:T(8,128)} %reshape.218) | copy-start | bytes 921604
  100.2 2.5 %copy-start.9 = (f32[1,6,25,512]{3,2,0,1:T(8,128)S(1)}, f32[1,6,25,512]{3,2,0,1:T(8,128)}, u32[]{:S(2)}) copy-start(f32[1,6,25,512]{3,2,0,1:T(8,128)} %reshape.217) | copy-start | bytes 921604
  101.3 1.4 copy-start.13
  101.3 1.5 copy-start.14
  102.6 1.4 copy-start.2
  102.6 1.6 copy-start.5
  102.6 1.6 copy-start.22
  104.2 1.5 copy-start.20
  105.7 2.9 %copy-start.12 = (f32[48,48,32]{1,2,0:T(8,128)S(1)}, f32[48,48,32]{1,2,0:T(8,128)}, u32[]{:S(2)}) copy-start(f32[48,48,32]{1,2,0:T(8,128)} %param.25) | copy-start | bytes 884740
  107.2 45.1 %copy-start.16 = (f32[48,48]{1,0:T(8,128)S(1)}, f32[48,48]{1,0:T(8,128)}, u32[]{:S(2)}) copy-start(f32[48,48]{1,0:T(8,128)} %param.26) | copy-start | bytes 27652
  141.1 23.2 %copy-start.15 = (f32[48,32]{0,1:T(8,128)S(1)}, f32[48,32]{0,1:T(8,128)}, u32[]{:S(2)}) copy-start(f32[48,32]{0,1:T(8,128)} %reduce-scatter.2.cloned.1.call-done) | copy-start | bytes 18436
  142.7 8.8 %collective-permute-start.4 = (f32[1,48,32]{1,2,0:T(8,128)S(1)}, f32[1,48,32]{1,2,0:T(8,128)S(1)}, u32[]{:S(2)}, u32[]{:S(2)}) collective-permute-start(f32[1,48,32]{1,2,0:T(8,128)S(1)} %multiply_bitcast_fusion), channel_id=1, source_target_pairs={{0,8},{8,16},{16,24},{24,32},{32,40},{40,48},{48,56},{56,64},{64,7... | collective-permute-start | bytes 18440 | tf_op jit(solution)/shard_map/ppermute | solution.py:23
  144.6 7.7 %collective-permute-start.5 = (f32[1,48,32]{1,2,0:T(8,128)S(1)}, f32[1,48,32]{1,2,0:T(8,128)S(1)}, u32[]{:S(2)}, u32[]{:S(2)}) collective-permute-start(f32[1,48,32]{1,2,0:T(8,128)S(1)} %multiply_bitcast_fusion), channel_id=1, source_target_pairs={{8,0},{16,8},{24,16},{32,24},{40,32},{48,40},{56,48},{64,56},{72,6... | collective-permute-start | bytes 18440 | tf_op jit(solution)/shard_map/ppermute | solution.py:24
  153.9 10.4 %collective-permute-start.6 = (f32[1,48,32]{1,2,0:T(8,128)S(1)}, f32[1,48,32]{1,2,0:T(8,128)S(1)}, u32[]{:S(2)}, u32[]{:S(2)}) collective-permute-start(f32[1,48,32]{1,2,0:T(8,128)S(1)} %fusion.24), channel_id=1, source_target_pairs={{0,8},{8,16},{16,24},{24,32},{32,40},{40,48},{48,56},{56,64},{64,7... | collective-permute-start | bytes 18440 | tf_op jit(solution)/shard_map/ppermute | solution.py:23
  155.9 8.4 %collective-permute-start.7 = (f32[1,48,32]{1,2,0:T(8,128)S(1)}, f32[1,48,32]{1,2,0:T(8,128)S(1)}, u32[]{:S(2)}, u32[]{:S(2)}) collective-permute-start(f32[1,48,32]{1,2,0:T(8,128)S(1)} %fusion.24), channel_id=1, source_target_pairs={{8,0},{16,8},{24,16},{32,24},{40,32},{48,40},{56,48},{64,56},{72,6... | collective-permute-start | bytes 18440 | tf_op jit(solution)/shard_map/ppermute | solution.py:24
  164.3 19.3 %copy-start.21 = (f32[125,8]{0,1:T(8,128)S(1)}, f32[125,8]{0,1:T(8,128)}, u32[]{:S(2)}) copy-start(f32[125,8]{0,1:T(8,128)} %param.27) | copy-start | bytes 12004
Sparse Core Ops, SparseCore 0:
  108.7 32.3 reduce-scatter.1
where the time goes:
time: 196 us; the launch traced here: 194 us
  local copies, waits for them, and re-layouts  53 us (27%)
  starting transfers between devices  39.9 us (20%)
  waiting for transfers between devices  34.8 us (18%)
  matrix products  17.8 us (9%)
  blocking collectives  17.2 us (9%)
  other arithmetic  17 us (9%)
  between operations  14.5 us (7%)
    reduce_scatter x1, waiting for transfers between devices, per_device(): lax.psum_scatter(partial_sums, 'gy', scatter_dimension=1, tiled=True)  32.1 us
    ppermute x4, starting transfers between devices, padded_2(): after = lax.ppermute(first, axis, down)  29.2 us
    all_gather x1, blocking collectives, per_device(): everything = lax.all_gather(coarse, 'gy', axis=1, tiled=True)  17.2 us
    concatenate x2, local copies, waits for them, and re-layouts, padded_2(): value = jnp.concatenate([before, value, after], axis=dim)  12.2 us
    ppermute x4, starting transfers between devices, padded_2(): before = lax.ppermute(last, axis, up)  10.7 us
    unnamed x58, local copies, waits for them, and re-layouts  8.29 us
    concatenate x2, other arithmetic, padded_2(): value = jnp.concatenate([before, value, after], axis=dim)  7.81 us
    convert_element_type x4, local copies, waits for them, and re-layouts, per_device(): nearby[face_no].astype(jnp.float32) - owned[face_no].astype(jnp.float32)  6 us
  transfers between devices with their start and end apart: 9, of which 3 were waited for; matrix products, arithmetic and copies ran while one was open for 17% of the time, Pallas kernels for 0%

commit v1 on v0

v1 whole, which is shorter than its diff:
```python
import jax
import jax.numpy as jnp
import numpy as np
from jax import lax
from jax.experimental import pallas as pl
from jax.experimental.pallas import tpu as pltpu
from jax.sharding import PartitionSpec as P

NV = 6
NN = 125
NF = 25
FR = 32
ASLOT = 32
MEMBERS = 8
RELAX = 0.7
WALL = 2.0
BF = jnp.bfloat16
F32 = jnp.float32
TOP = lax.Precision.HIGHEST
VMEM = pl.BlockSpec(memory_space=pltpu.VMEM)
SMEM = pl.BlockSpec(memory_space=pltpu.SMEM)


def face_nodes(face):
    p, q, r = np.meshgrid(np.arange(5), np.arange(5), np.arange(5), indexing="ij")
    axis, end = (p, q, r)[face // 2], 4 * (face % 2)
    return ((p * 5 + q) * 5 + r)[axis == end]


def picker(faces):
    rows = np.zeros((FR * len(faces), NN), np.float32)
    for k, face in enumerate(faces):
        rows[FR * k + np.arange(NF), face_nodes(face)] = 1.0
    return rows


def dot(a, b, **kw):
    return jnp.dot(a, b, preferred_element_type=F32, **kw)


def split(x):
    high = x.astype(BF)
    return high, (x - high.astype(F32)).astype(BF)


def call(kernel, outs, *args, scratch=(), smem=(), flops=10**8, nbytes=10**6):
    return pl.pallas_call(
        kernel,
        out_shape=outs,
        in_specs=[SMEM if i in smem else VMEM for i in range(len(args))],
        out_specs=jax.tree.map(lambda _: VMEM, outs),
        scratch_shapes=list(scratch),
        compiler_params=pltpu.CompilerParams(vmem_limit_bytes=40 * 2**20),
        cost_estimate=pl.CostEstimate(flops=flops, bytes_accessed=nbytes, transcendentals=0),
    )(*args)


def faces_kernel(state, pick, low_x, high_x, low_y, high_y):
    half = state.shape[2] // 2
    for v in range(NV):
        found = dot(pick[...], state[v]).astype(BF)
        low_x[v] = found[:FR, :half]
        high_x[v] = found[FR : 2 * FR, half:]
        low_y[v] = found[2 * FR : 3 * FR]
        high_y[v] = found[3 * FR :]


def prepare_kernel(inverse, lift_t, restrict, grid_inverse, lift_near, lift_far, r_parts, rl_parts):
    lanes = grid_inverse.shape[2]
    rows = inverse.shape[0] // 3
    modes = inverse.shape[2]
    blank = jnp.zeros((lanes - 3 * ASLOT, modes), F32)
    for r in range(rows):
        stacked = jnp.concatenate([inverse[r], inverse[rows + r], inverse[2 * rows + r], blank], axis=0)
        grid_inverse[r] = RELAX * stacked.T
    r_high, r_low = split(restrict[...])
    r_parts[...] = jnp.concatenate([r_high, r_low], axis=0)
    gap = jnp.zeros((FR - NF, NN), F32)
    lifts = [jnp.concatenate([lift_t[f].astype(F32), gap], axis=0).T for f in range(6)]
    for a in range(2):
        lift_near[a] = jnp.concatenate([lifts[1 - a], lifts[4], lifts[5]], axis=1).astype(BF)
        far = jnp.concatenate([lifts[a], lifts[2], lifts[3]], axis=1)
        lift_far[a] = far.astype(BF)
        high, low = split(dot(restrict[...], far, precision=TOP))
        rl_parts[a] = jnp.concatenate([high, low], axis=0)


def volume_kernel(
    mix, state, forcing, volume, viscous, viscosity, flags, pick, lift_near, r_parts, partial, restricted, flux
):
    half = state.shape[2] // 2
    lanes = state.shape[2]
    place = lax.broadcasted_iota(jnp.int32, (FR, lanes), 1) % half
    first, last = place == 0, place == half - 1
    visc = viscosity[...]
    for v in range(NV):
        own = state[v]
        flux[v] = dot(volume[...], own)
        traces = dot(pick[...], own)
        t0, t1, t4, t5 = (traces[FR * k : FR * (k + 1)] for k in range(4))
        below = jnp.where(first, 0.0, pltpu.roll(t5, 1, 1))
        above = jnp.where(last, 0.0, pltpu.roll(t4, lanes - 1, 1))
        j4 = below - t4
        j5 = above - t5
        across = t0[:, half:] - t1[:, :half]
        parts = []
        for a in range(2):
            cut = slice(a * half, (a + 1) * half)
            jumps = jnp.concatenate([across if a == 0 else -across, j4[:, cut], j5[:, cut]], axis=0)
            parts.append(dot(lift_near[a], jumps.astype(BF)))
        lifted = jnp.concatenate(parts, axis=1)
        local = forcing[v].astype(F32) - visc * dot(viscous[...], own) + lifted
        if v == NV - 1:
            local = local - (WALL * flags[...].astype(F32)) * own.astype(F32)
        partial[v] = local
    for low in range(0, NN, 8):
        rows = slice(low, min(low + 8, NN))
        pieces = [flux[k, rows] for k in range(NV)]
        for q in range(NV):
            total = mix[q, 0] * pieces[0]
            for k in range(1, NV):
                total = total + mix[q, k] * pieces[k]
            partial[q, rows] = partial[q, rows] - total
    for v in range(NV):
        high, low = split(partial[v])
        both = dot(r_parts[...], high)
        restricted[8 * v : 8 * v + 8] = both[:8] + both[8:] + dot(r_parts[:8], low)


def far_jumps(v, a, half, near, own):
    cut = slice(a * half, (a + 1) * half)
    nx, ny_low, ny_high = near[a][v], near[2][v][:, cut], near[3][v][:, cut]
    ox, oy_low, oy_high = own[a][v], own[2][v][:, cut], own[3][v][:, cut]
    pairs = ((nx, ox), (ny_low, oy_low), (ny_high, oy_high))
    return jnp.concatenate([n.astype(F32) - o.astype(F32) for n, o in pairs], axis=0).astype(BF)


def keys_of(owner, slot):
    return owner[...] * ASLOT + slot[...]


def one_hot(keys):
    groups = MEMBERS * ASLOT
    return (lax.broadcasted_iota(jnp.int32, (groups, keys.shape[1]), 0) == keys).astype(F32).astype(BF)


def sums_kernel(n0, n1, n2, n3, o0, o1, o2, o3, rl_parts, restricted, owner, slot, blocks):
    near, own = (n0, n1, n2, n3), (o0, o1, o2, o3)
    half = owner.shape[1] // 2
    highs, lows = [], []
    for v in range(NV):
        parts = []
        for a in range(2):
            both = dot(rl_parts[a], far_jumps(v, a, half, near, own))
            parts.append(both[:8] + both[8:])
        high, low = split(restricted[8 * v : 8 * v + 8] + jnp.concatenate(parts, axis=1))
        highs.append(high.astype(F32))
        lows.append(low.astype(F32))
    stacked = jnp.concatenate(highs + lows, axis=0).astype(BF)
    spread = one_hot(keys_of(owner, slot))
    both = lax.dot_general(stacked, spread, (((1,), (1,)), ((), ())), preferred_element_type=F32)
    sums = both[: 8 * NV] + both[8 * NV :]
    group = lax.broadcasted_iota(jnp.int32, (16, 128), 1) // ASLOT
    for m in range(MEMBERS):
        block = jnp.zeros((16, 128), F32)
        for k in range(3):
            piece = sums[16 * k : 16 * k + 16, (m // 4) * 128 : (m // 4 + 1) * 128]
            turn = ((k - m % 4) * ASLOT) % 128
            piece = pltpu.roll(piece, turn, 1) if turn else piece
            block = jnp.where(group == k, piece, block)
        blocks[m] = block


def residual_kernel(n0, n1, n2, n3, o0, o1, o2, o3, lift_far, partial, residual):
    near, own = (n0, n1, n2, n3), (o0, o1, o2, o3)
    half = partial.shape[2] // 2
    for v in range(NV):
        for a in range(2):
            cut = slice(a * half, (a + 1) * half)
            lifted = dot(lift_far[a], far_jumps(v, a, half, near, own))
            residual[v, :, cut] = (partial[v, :, cut] + lifted).astype(BF)


def opened(packed):
    group = lax.broadcasted_iota(jnp.int32, (16, 128), 1) // ASLOT
    rows = []
    for k in range(3):
        only = jnp.where(group == k, packed, 0.0)
        two = only + pltpu.roll(only, 32, 1)
        rows.append(two + pltpu.roll(two, 64, 1))
    return jnp.concatenate(rows, axis=0)


def solve(grid_inverse, source, out):
    for r in range(16):
        out[r : r + 1] = jnp.sum(grid_inverse[r] * source, axis=0, keepdims=True)


def first_kernel(blocks, grid_inverse, totals, coarse):
    packed = jnp.sum(blocks[...], axis=0)
    source = opened(packed)
    totals[...] = source
    solve(grid_inverse, source, coarse)


def sweep_kernel(up, down, totals, coupling, before, grid_inverse, coarse):
    beside = opened(up[...] + down[...])
    source = totals[...] - dot(coupling[...], beside, precision=TOP)
    solve(grid_inverse, source, coarse)
    coarse[...] = (1.0 - RELAX) * before[...] + coarse[...]


def last_sweep_kernel(up, down, totals, coupling, before, grid_inverse, blocks, scratch):
    sweep_kernel(up, down, totals, coupling, before, grid_inverse, scratch)
    for m in range(MEMBERS):
        blocks[m] = scratch[...]


def correction_kernel(blocks, prolong_t, owner, slot, correction):
    weights = prolong_t[...].T
    select = one_hot(keys_of(owner, slot))
    group = lax.broadcasted_iota(jnp.int32, (8, 128), 1) // ASLOT
    for v in range(NV):
        k, rows = v // 2, slice(8 * (v % 2), 8 * (v % 2) + 8)
        halves = []
        for h in range(MEMBERS // 4):
            value = jnp.zeros((8, 128), F32)
            for w in range(4):
                turn = ((w - k) * ASLOT) % 128
                piece = blocks[4 * h + w, rows]
                piece = pltpu.roll(piece, turn, 1) if turn else piece
                value = jnp.where(group == w, piece, value)
            halves.append(value)
        wide = dot(weights, jnp.concatenate(halves, axis=1), precision=TOP).astype(BF)
        correction[v] = dot(wide, select).astype(BF)


def shifted(value, axis, by):
    size = lax.axis_size(axis)
    return lax.ppermute(value, axis, [(i, (i + by) % size) for i in range(size)])


def struct(shape, dtype):
    return jax.ShapeDtypeStruct(shape, dtype)


def per_device(
    state,
    forcing,
    volume_flux_matrix,
    viscous_matrix,
    linear_flux_matrix,
    viscosity,
    lift,
    wall_flags,
    restriction_weight,
    owner,
    slot,
    coarse_inverse,
    coupling,
    prolongation_weight,
):
    elems = state.shape[2]
    half = elems // 2
    owner, slot = owner.reshape(1, elems), slot.reshape(1, elems)
    viscosity, flags = viscosity.reshape(1, elems), wall_flags.reshape(1, elems)
    pick_far = jnp.asarray(picker((0, 1, 2, 3)), BF)
    pick_near = jnp.asarray(picker((0, 1, 4, 5)), BF)
    x_face, y_face = struct((NV, FR, half), BF), struct((NV, FR, elems), BF)
    own = call(faces_kernel, (x_face, x_face, y_face, y_face), state, pick_far)
    near = (
        shifted(own[1], "gx", 1),
        shifted(own[0], "gx", -1),
        shifted(own[3], "gy", 1),
        shifted(own[2], "gy", -1),
    )
    inverse, lift_t, _ = lax.optimization_barrier(
        (jnp.transpose(coarse_inverse, (0, 2, 1)), jnp.transpose(lift, (0, 2, 1)), own[0])
    )
    grid_inverse, lift_near, lift_far, r_parts, rl_parts = call(
        prepare_kernel,
        (
            struct((16, 48, 128), F32),
            struct((2, NN, 3 * FR), BF),
            struct((2, NN, 3 * FR), BF),
            struct((16, NN), BF),
            struct((2, 16, 3 * FR), BF),
        ),
        inverse,
        lift_t,
        restriction_weight,
    )
    partial, restricted = call(
        volume_kernel,
        (struct((NV, NN, elems), F32), struct((48, elems), F32)),
        linear_flux_matrix,
        state,
        forcing,
        volume_flux_matrix,
        viscous_matrix,
        viscosity,
        flags,
        pick_near,
        lift_near,
        r_parts,
        scratch=[pltpu.VMEM((NV, NN, elems), F32)],
        smem=(0,),
        flops=10**9,
        nbytes=4 * 10**6,
    )
    blocks = call(
        sums_kernel, struct((MEMBERS, 16, 128), F32), *near, *own, rl_parts, restricted, owner, slot
    )
    blocks = lax.all_to_all(blocks, "gy", 0, 0, tiled=True)
    totals, coarse = call(
        first_kernel, (struct((48, 128), F32), struct((16, 128), F32)), blocks, grid_inverse
    )
    partial, _ = lax.optimization_barrier((partial, coarse))
    up, down = shifted(coarse, "gx", 1), shifted(coarse, "gx", -1)
    residual = call(
        residual_kernel, struct((NV, NN, elems), BF), *near, *own, lift_far, partial,
        flops=10**9, nbytes=4 * 10**6,
    )
    coarse = call(
        sweep_kernel, struct((16, 128), F32), up, down, totals, coupling, coarse, grid_inverse
    )
    up, down = shifted(coarse, "gx", 1), shifted(coarse, "gx", -1)
    blocks = call(
        last_sweep_kernel,
        struct((MEMBERS, 16, 128), F32),
        up,
        down,
        totals,
        coupling,
        coarse,
        grid_inverse,
        scratch=[pltpu.VMEM((16, 128), F32)],
    )
    blocks = lax.all_to_all(blocks, "gy", 0, 0, tiled=True)
    correction = call(
        correction_kernel,
        struct((NV, NN, elems), BF),
        blocks,
        jnp.transpose(prolongation_weight),
        owner,
        slot,
    )
    return residual, correction


def solution(mesh):
    split_last = P(None, None, ("gx", "gy"))
    flat = P(("gx", "gy"))
    return jax.shard_map(
        per_device,
        mesh=mesh,
        in_specs=(
            split_last,
            split_last,
            P(),
            P(),
            P(),
            flat,
            P(),
            flat,
            P(),
            P(("gx", "gy"), None),
            flat,
            split_last,
            P(),
            P(),
        ),
        out_specs=(split_last, split_last),
        check_vma=False,
    )
```

time: 196 us -> 82.5 us (0.42)
  local copies, waits for them, and re-layouts: 53 us -> 7.17 us
  waiting for transfers between devices: 34.8 us -> 13.7 us
  matrix products: 17.8 us -> 0 us
  other arithmetic: 17 us -> 0 us
  between operations: 14.5 us -> 0.85 us
  Pallas kernels: 0 us -> 10.9 us
  blocking collectives: 17.2 us -> 9.87 us
    reduce_scatter x1 -> x0, waiting for transfers between devices: 32.1 us -> none  [per_device(): lax.psum_scatter(partial_sums, 'gy', scatter_dimension=1, tiled=True)]
    dot_general x12 -> x0, matrix products: 17.8 us -> none  [the longest x1 4.93 us: per_device(): jnp.einsum('qk,kgs->qgs', linear_flux_matrix, stiffness_matrix, precision...]
    all_gather x1 -> x0, blocking collectives: 17.2 us -> none  [per_device(): everything = lax.all_gather(coarse, 'gy', axis=1, tiled=True)]
    concatenate x2 -> x0, local copies, waits for them, and re-layouts: 12.2 us -> none  [padded_2(): value = jnp.concatenate([before, value, after], axis=dim)]
    ppermute x4 -> x0, local copies, waits for them, and re-layouts: 11.3 us -> none  [the longest x2 5.7 us: padded_2(): after = lax.ppermute(first, axis, down)]
    convert_element_type x8 -> x0, local copies, waits for them, and re-layouts: 11 us -> none  [the longest x4 6 us: per_device(): nearby[face_no].astype(jnp.float32) - owned[face_no].astype(jnp.float32)]
    pallas_call x0 -> x9, Pallas kernels: none -> 10.9 us  [call(): pl.pallas_call(kernel, out_shape=outs, in_specs=[SMEM if i in smem else V...]
    all_to_all x0 -> x1, blocking collectives: none -> 9.87 us  [per_device(): blocks = lax.all_to_all(blocks, 'gy', 0, 0, tiled=True)]
  transfers between devices with their start and end apart: 9 -> 9, of which waited for: 3 -> 3; matrix products, arithmetic and copies ran while one was open for 17% -> 0% of each run, Pallas kernels for 0% -> 7%
where the time goes in v1:
time: 82.5 us; the launch traced here: 81.7 us
  starting transfers between devices  39.2 us (48%)
  waiting for transfers between devices  13.7 us (17%)
  Pallas kernels  10.9 us (13%)
  blocking collectives  9.87 us (12%)
  local copies, waits for them, and re-layouts  7.17 us (9%)
  between operations  0.85 us (1%)
    ppermute x8, starting transfers between devices, shifted(): lax.ppermute(value, axis, [(i, (i + by) % size) for i in range(size)])  32.6 us
    pallas_call x9, Pallas kernels, call(): pl.pallas_call(kernel, out_shape=outs, in_specs=[SMEM if i in smem else V...  10.9 us
    ppermute x8, waiting for transfers between devices, shifted(): lax.ppermute(value, axis, [(i, (i + by) % size) for i in range(size)])  10.1 us
    all_to_all x1, blocking collectives, per_device(): blocks = lax.all_to_all(blocks, 'gy', 0, 0, tiled=True)  9.87 us
    unnamed x34, local copies, waits for them, and re-layouts  7.17 us
    all_to_all x1, starting transfers between devices, per_device(): blocks = lax.all_to_all(blocks, 'gy', 0, 0, tiled=True)  6.61 us
    all_to_all x1, waiting for transfers between devices, per_device(): blocks = lax.all_to_all(blocks, 'gy', 0, 0, tiled=True)  3.61 us
  transfers between devices with their start and end apart: 9, of which 3 were waited for; matrix products, arithmetic and copies ran while one was open for 0% of the time, Pallas kernels for 7%

profile of v1, /device:TPU:1, one launch (start us, length us, event | category | flops | bytes accessed | tf_op | source)
XLA Modules:
  0.0 81.7 jit_solution(8900101957561655298)
XLA Ops:
  0.6 0.0 copy-start.1
  0.6 1.1 %copy-done.1 = bf16[6,125,512]{2,1,0:T(8,128)(2,1)S(1)} copy-done((bf16[6,125,512]{2,1,0:T(8,128)(2,1)S(1)}, bf16[6,125,512]{2,1,0:T(8,128)(2,1)}, u32[]{:S(2)}) %copy-start.1) | copy-done | bytes 768024
  1.8 0.0 copy-start.5
  1.8 0.8 copy-done.5
  2.5 0.0 copy-start.2
  2.5 0.0 copy-start.11
  2.5 0.0 copy-start.13
  2.5 0.0 copy-start.14
  2.5 0.0 copy-start.15
  2.5 0.3 shard_map.167
  2.9 2.6 %collective-permute-start.2 = (bf16[6,32,512]{2,1,0:T(8,128)(2,1)S(1)}, bf16[6,32,512]{2,1,0:T(8,128)(2,1)S(1)}, u32[]{:S(2)}, u32[]{:S(2)}) collective-permute-start(bf16[6,32,512]{2,1,0:T(8,128)(2,1)S(1)} %get-tuple-element.20.o3), channel_id=1, source_target_pairs={{0,1},{1,2},{2,3},{3,4},{4,5},{5,6},{6,7},{7,0},{8,9},{9,10},{10,1... | collective-permute-start | bytes 589832 | tf_op jit(solution)/shard_map/ppermute | solution.py:240
  5.5 7.9 %collective-permute-start.3 = (bf16[6,32,512]{2,1,0:T(8,128)(2,1)S(1)}, bf16[6,32,512]{2,1,0:T(8,128)(2,1)S(1)}, u32[]{:S(2)}, u32[]{:S(2)}) collective-permute-start(bf16[6,32,512]{2,1,0:T(8,128)(2,1)S(1)} %get-tuple-element.21.o2), channel_id=1, source_target_pairs={{0,7},{1,0},{2,1},{3,2},{4,3},{5,4},{6,5},{7,6},{8,15},{9,8},{10,9... | collective-permute-start | bytes 589832 | tf_op jit(solution)/shard_map/ppermute | solution.py:240
  13.5 1.9 %collective-permute-start = (bf16[6,32,256]{2,1,0:T(8,128)(2,1)S(1)}, bf16[6,32,256]{2,1,0:T(8,128)(2,1)S(1)}, u32[]{:S(2)}, u32[]{:S(2)}) collective-permute-start(bf16[6,32,256]{2,1,0:T(8,128)(2,1)S(1)} %get-tuple-element.18.o1), channel_id=1, source_target_pairs={{0,8},{8,16},{16,24},{24,32},{32,40},{40,48},{48,56},{56,64},{64,7... | collective-permute-start | bytes 294920 | tf_op jit(solution)/shard_map/ppermute | solution.py:240
  15.4 9.3 %collective-permute-start.1 = (bf16[6,32,256]{2,1,0:T(8,128)(2,1)S(1)}, bf16[6,32,256]{2,1,0:T(8,128)(2,1)S(1)}, u32[]{:S(2)}, u32[]{:S(2)}) collective-permute-start(bf16[6,32,256]{2,1,0:T(8,128)(2,1)S(1)} %get-tuple-element.19.o0), channel_id=1, source_target_pairs={{0,760},{8,0},{16,8},{24,16},{32,24},{40,32},{48,40},{56,48},{64,5... | collective-permute-start | bytes 294920 | tf_op jit(solution)/shard_map/ppermute | solution.py:240
  24.6 0.0 copy-start
  24.7 1.1 %copy-done = f32[48,48,32]{1,2,0:T(8,128)S(1)} copy-done((f32[48,48,32]{1,2,0:T(8,128)S(1)}, f32[48,48,32]{1,2,0:T(8,128)}, u32[]{:S(2)}) %copy-start) | copy-done | bytes 294936
  25.8 0.0 copy-start.4
  25.8 0.8 copy-done.4
  26.6 0.0 copy-start.8
  26.6 0.7 copy-done.8
  27.3 0.6 shard_map.168
  27.9 0.0 copy-done.2
  27.9 0.0 copy-done.11
  27.9 0.0 copy-done.13
  27.9 0.0 copy-done.14
  27.9 0.0 copy-done.15
  27.9 0.0 copy-start.10
  27.9 1.1 %copy-done.10 = bf16[6,125,512]{2,1,0:T(8,128)(2,1)S(1)} copy-done((bf16[6,125,512]{2,1,0:T(8,128)(2,1)S(1)}, bf16[6,125,512]{2,1,0:T(8,128)(2,1)}, u32[]{:S(2)}) %copy-start.10) | copy-done | bytes 768024
  29.1 0.0 copy-start.12
  29.1 0.8 copy-done.12
  29.8 0.0 copy-start.16
  29.8 0.8 copy-done.16
  30.6 0.0 copy-start.6
  30.6 0.0 copy-start.7
  30.6 3.5 %shard_map.169 = (f32[6,125,512]{2,1,0:T(8,128)S(1)}, f32[48,512]{1,0:T(8,128)S(1)}) custom-call(f32[6,6]{1,0:T(8,128)S(1)} %copy-done.13, bf16[6,125,512]{2,1,0:T(8,128)(2,1)S(1)} %copy-done.2, bf16[6,125,512]{2,1,0:T(8,128)(2,1)S(1)} %copy-done.10, bf16[125,125]{1,0:T(8,128)(2,1)S(1)} %copy-done.11, bf16[125,125]{1,0:T(8,128)(2,1)S(1)} %copy-done.12, ...), custom_call_target="tpu_custom_call" | custom-call | flops 1000000000 | bytes 4000000 | tf_op jit(solution)/shard_map/pallas_call | solution.py:47
  34.1 0.0 copy-start.3
  34.1 0.0 collective-permute-done.n0
  34.1 0.0 collective-permute-done.1.n1
  34.1 0.0 collective-permute-done.2.n2
  34.1 0.0 collective-permute-done.3.n3
  34.1 0.0 copy-done.6
  34.1 0.0 copy-done.7
  34.1 0.5 shard_map.170
  34.6 9.9 %all_to_all.10.blocks = f32[8,16,128]{2,1,0:T(8,128)S(1)} all-to-all(f32[8,16,128]{2,1,0:T(8,128)S(1)} %shard_map.170), channel_id=1, replica_groups=mesh['gx'=96,'gy'=8] {'gy'}, dimensions={0} | all-to-all | bytes 131072 | tf_op jit(solution)/shard_map/all_to_all | solution.py:314
  44.5 0.2 shard_map.171
  44.7 3.6 %collective-permute-start.5 = (f32[16,128]{1,0:T(8,128)S(1)}, f32[16,128]{1,0:T(8,128)S(1)}, u32[]{:S(2)}, u32[]{:S(2)}) collective-permute-start(f32[16,128]{1,0:T(8,128)S(1)} %get-tuple-element.31.before), channel_id=1, source_target_pairs={{0,760},{8,0},{16,8},{24,16},{32,24},{40,32},{48,40},{56,48},{64,5... | collective-permute-start | bytes 24584 | tf_op jit(solution)/shard_map/ppermute | solution.py:240
  48.3 1.9 %collective-permute-start.4 = (f32[16,128]{1,0:T(8,128)S(1)}, f32[16,128]{1,0:T(8,128)S(1)}, u32[]{:S(2)}, u32[]{:S(2)}) collective-permute-start(f32[16,128]{1,0:T(8,128)S(1)} %get-tuple-element.31.before), channel_id=1, source_target_pairs={{0,8},{8,16},{16,24},{24,32},{32,40},{40,48},{48,56},{56,64},{64,7... | collective-permute-start | bytes 24584 | tf_op jit(solution)/shard_map/ppermute | solution.py:240
  50.3 0.0 collective-permute-done.5.down
  50.3 5.8 %collective-permute-done.4.up = f32[16,128]{1,0:T(8,128)S(1)} collective-permute-done((f32[16,128]{1,0:T(8,128)S(1)}, f32[16,128]{1,0:T(8,128)S(1)}, u32[]{:S(2)}, u32[]{:S(2)}) %collective-permute-start.4) | collective-permute-done | bytes 8224 | tf_op jit(solution)/shard_map/ppermute | solution.py:240
  56.1 0.0 copy-done.3
  56.1 0.3 shard_map.173.before
  56.4 1.9 %collective-permute-start.7 = (f32[16,128]{1,0:T(8,128)S(1)}, f32[16,128]{1,0:T(8,128)S(1)}, u32[]{:S(2)}, u32[]{:S(2)}) collective-permute-start(f32[16,128]{1,0:T(8,128)S(1)} %shard_map.173.before), channel_id=1, source_target_pairs={{0,760},{8,0},{16,8},{24,16},{32,24},{40,32},{48,40},{56,48},{64,5... | collective-permute-start | bytes 24584 | tf_op jit(solution)/shard_map/ppermute | solution.py:240
  58.3 3.4 %collective-permute-start.6 = (f32[16,128]{1,0:T(8,128)S(1)}, f32[16,128]{1,0:T(8,128)S(1)}, u32[]{:S(2)}, u32[]{:S(2)}) collective-permute-start(f32[16,128]{1,0:T(8,128)S(1)} %shard_map.173.before), channel_id=1, source_target_pairs={{0,8},{8,16},{16,24},{24,32},{32,40},{40,48},{48,56},{56,64},{64,7... | collective-permute-start | bytes 24584 | tf_op jit(solution)/shard_map/ppermute | solution.py:240
  61.7 0.0 collective-permute-done.7.down
  61.7 4.3 %collective-permute-done.6.up = f32[16,128]{1,0:T(8,128)S(1)} collective-permute-done((f32[16,128]{1,0:T(8,128)S(1)}, f32[16,128]{1,0:T(8,128)S(1)}, u32[]{:S(2)}, u32[]{:S(2)}) %collective-permute-start.6) | collective-permute-done | bytes 8224 | tf_op jit(solution)/shard_map/ppermute | solution.py:240
  66.0 1.0 %shard_map.174 = f32[8,16,128]{2,1,0:T(8,128)} custom-call(f32[16,128]{1,0:T(8,128)S(1)} %collective-permute-done.6.up, f32[16,128]{1,0:T(8,128)S(1)} %collective-permute-done.7.down, f32[48,128]{1,0:T(8,128)S(1)} %get-tuple-element.33.totals, f32[48,48]{1,0:T(8,128)S(1)} %copy-done.3, f32[16,128]{1,0:T(8,128)S(1)} %shard_map.173.before, ...), custom_call_target="tpu_custom_call" | custom-call | flops 100000000 | bytes 1000000 | tf_op jit(solution)/shard_map/pallas_call | solution.py:47
  67.0 6.6 %all-to-all-start.1 = ((f32[8,16,128]{2,1,0:T(8,128)}), f32[8,16,128]{2,1,0:T(8,128)S(1)}, u32[]{:S(2)}, u32[]{:S(2)}) async-start(f32[8,16,128]{2,1,0:T(8,128)} %shard_map.174), calls=%async_computation.1 | async-start | bytes 131072 | tf_op jit(solution)/shard_map/all_to_all | solution.py:339
  73.6 0.0 copy-start.9
  73.6 1.3 %shard_map.172 = bf16[6,125,512]{2,1,0:T(8,128)(2,1)} custom-call(bf16[6,32,256]{2,1,0:T(8,128)(2,1)S(1)} %collective-permute-done.n0, bf16[6,32,256]{2,1,0:T(8,128)(2,1)S(1)} %collective-permute-done.1.n1, bf16[6,32,512]{2,1,0:T(8,128)(2,1)S(1)} %collective-permute-done.2.n2, bf16[6,32,512]{2,1,0:T(8,128)(2,1)S(1)} %collective-permute-done.3.n3, ...), custom_call_target="tpu_custom_call" | custom-call | flops 1000000000 | bytes 4000000 | tf_op jit(solution)/shard_map/pallas_call | solution.py:47
  74.9 3.6 %all-to-all-done.1.blocks = f32[8,16,128]{2,1,0:T(8,128)S(1)} async-done(((f32[8,16,128]{2,1,0:T(8,128)}), f32[8,16,128]{2,1,0:T(8,128)S(1)}, u32[]{:S(2)}, u32[]{:S(2)}) %all-to-all-start.1) | async-done | bytes 65568 | tf_op jit(solution)/shard_map/all_to_all | solution.py:339
  78.5 0.0 copy-done.9
  78.5 3.2 %shard_map.175 = bf16[6,125,512]{2,1,0:T(8,128)(2,1)} custom-call(f32[8,16,128]{2,1,0:T(8,128)S(1)} %all-to-all-done.1.blocks, f32[8,125]{1,0:T(8,128)S(1)} %bitcast.13, s32[1,512]{1,0:T(1,128)S(1)} %bitcast.10, s32[1,512]{1,0:T(1,128)S(1)} %bitcast.12), custom_call_target="tpu_custom_call" | custom-call | flops 100000000 | bytes 1000000 | tf_op jit(solution)/shard_map/pallas_call | solution.py:47
Async XLA Ops:
  0.6 1.1 %copy-start.1 = (bf16[6,125,512]{2,1,0:T(8,128)(2,1)S(1)}, bf16[6,125,512]{2,1,0:T(8,128)(2,1)}, u32[]{:S(2)}) copy-start(bf16[6,125,512]{2,1,0:T(8,128)(2,1)} %state.3) | copy-start | bytes 2304004
  1.8 0.8 copy-start.5
  2.5 25.4 %copy-start.2 = (bf16[6,125,512]{2,1,0:T(8,128)(2,1)S(1)}, bf16[6,125,512]{2,1,0:T(8,128)(2,1)}, u32[]{:S(2)}) copy-start(bf16[6,125,512]{2,1,0:T(8,128)(2,1)} %state.3) | copy-start | bytes 2304004
  2.5 25.4 %copy-start.11 = (bf16[125,125]{1,0:T(8,128)(2,1)S(1)}, bf16[125,125]{1,0:T(8,128)(2,1)}, u32[]{:S(2)}) copy-start(bf16[125,125]{1,0:T(8,128)(2,1)} %volume.1) | copy-start | bytes 93754
  2.5 25.4 %copy-start.13 = (f32[6,6]{1,0:T(8,128)S(1)}, f32[6,6]{1,0:T(8,128)}, u32[]{:S(2)}) copy-start(f32[6,6]{1,0:T(8,128)} %mix.1) | copy-start | bytes 436
  2.5 25.4 %copy-start.14 = (f32[512]{0:T(512)S(1)}, f32[512]{0:T(512)}, u32[]{:S(2)}) copy-start(f32[512]{0:T(512)} %param.21) | copy-start | bytes 6148
  2.5 25.4 %copy-start.15 = (s32[512]{0:T(512)S(1)}, s32[512]{0:T(512)}, u32[]{:S(2)}) copy-start(s32[512]{0:T(512)} %param.23) | copy-start | bytes 6148
  2.9 31.2 %collective-permute-start.2 = (bf16[6,32,512]{2,1,0:T(8,128)(2,1)S(1)}, bf16[6,32,512]{2,1,0:T(8,128)(2,1)S(1)}, u32[]{:S(2)}, u32[]{:S(2)}) collective-permute-start(bf16[6,32,512]{2,1,0:T(8,128)(2,1)S(1)} %get-tuple-element.20.o3), channel_id=1, source_target_pairs={{0,1},{1,2},{2,3},{3,4},{4,5},{5,6},{6,7},{7,0},{8,9},{9,10},{10,1... | collective-permute-start | bytes 589832 | tf_op jit(solution)/shard_map/ppermute | solution.py:240
  5.5 28.6 %collective-permute-start.3 = (bf16[6,32,512]{2,1,0:T(8,128)(2,1)S(1)}, bf16[6,32,512]{2,1,0:T(8,128)(2,1)S(1)}, u32[]{:S(2)}, u32[]{:S(2)}) collective-permute-start(bf16[6,32,512]{2,1,0:T(8,128)(2,1)S(1)} %get-tuple-element.21.o2), channel_id=1, source_target_pairs={{0,7},{1,0},{2,1},{3,2},{4,3},{5,4},{6,5},{7,6},{8,15},{9,8},{10,9... | collective-permute-start | bytes 589832 | tf_op jit(solution)/shard_map/ppermute | solution.py:240
  13.5 20.6 %collective-permute-start = (bf16[6,32,256]{2,1,0:T(8,128)(2,1)S(1)}, bf16[6,32,256]{2,1,0:T(8,128)(2,1)S(1)}, u32[]{:S(2)}, u32[]{:S(2)}) collective-permute-start(bf16[6,32,256]{2,1,0:T(8,128)(2,1)S(1)} %get-tuple-element.18.o1), channel_id=1, source_target_pairs={{0,8},{8,16},{16,24},{24,32},{32,40},{40,48},{48,56},{56,64},{64,7... | collective-permute-start | bytes 294920 | tf_op jit(solution)/shard_map/ppermute | solution.py:240
  15.4 18.7 %collective-permute-start.1 = (bf16[6,32,256]{2,1,0:T(8,128)(2,1)S(1)}, bf16[6,32,256]{2,1,0:T(8,128)(2,1)S(1)}, u32[]{:S(2)}, u32[]{:S(2)}) collective-permute-start(bf16[6,32,256]{2,1,0:T(8,128)(2,1)S(1)} %get-tuple-element.19.o0), channel_id=1, source_target_pairs={{0,760},{8,0},{16,8},{24,16},{32,24},{40,32},{48,40},{56,48},{64,5... | collective-permute-start | bytes 294920 | tf_op jit(solution)/shard_map/ppermute | solution.py:240
  24.6 1.1 %copy-start = (f32[48,48,32]{1,2,0:T(8,128)S(1)}, f32[48,48,32]{1,2,0:T(8,128)}, u32[]{:S(2)}) copy-start(f32[48,48,32]{1,2,0:T(8,128)} %param.27) | copy-start | bytes 884740
  25.8 0.8 copy-start.4
  26.6 0.7 copy-start.8
  27.9 1.1 %copy-start.10 = (bf16[6,125,512]{2,1,0:T(8,128)(2,1)S(1)}, bf16[6,125,512]{2,1,0:T(8,128)(2,1)}, u32[]{:S(2)}) copy-start(bf16[6,125,512]{2,1,0:T(8,128)(2,1)} %forcing.1) | copy-start | bytes 2304004
  29.1 0.8 copy-start.12
  29.8 0.8 copy-start.16
  30.6 3.5 %copy-start.6 = (s32[512,1]{0,1:T(1,128)S(1)}, s32[512,1]{0,1:T(1,128)}, u32[]{:S(2)}) copy-start(s32[512,1]{0,1:T(1,128)} %param.25) | copy-start | bytes 6148
  30.6 3.5 %copy-start.7 = (s32[512]{0:T(512)S(1)}, s32[512]{0:T(512)}, u32[]{:S(2)}) copy-start(s32[512]{0:T(512)} %param.26) | copy-start | bytes 6148
  34.1 22.0 %copy-start.3 = (f32[48,48]{1,0:T(8,128)S(1)}, f32[48,48]{1,0:T(8,128)}, u32[]{:S(2)}) copy-start(f32[48,48]{1,0:T(8,128)} %coupling.3) | copy-start | bytes 27652
  44.7 5.6 %collective-permute-start.5 = (f32[16,128]{1,0:T(8,128)S(1)}, f32[16,128]{1,0:T(8,128)S(1)}, u32[]{:S(2)}, u32[]{:S(2)}) collective-permute-start(f32[16,128]{1,0:T(8,128)S(1)} %get-tuple-element.31.before), channel_id=1, source_target_pairs={{0,760},{8,0},{16,8},{24,16},{32,24},{40,32},{48,40},{56,48},{64,5... | collective-permute-start | bytes 24584 | tf_op jit(solution)/shard_map/ppermute | solution.py:240
  48.3 7.7 %collective-permute-start.4 = (f32[16,128]{1,0:T(8,128)S(1)}, f32[16,128]{1,0:T(8,128)S(1)}, u32[]{:S(2)}, u32[]{:S(2)}) collective-permute-start(f32[16,128]{1,0:T(8,128)S(1)} %get-tuple-element.31.before), channel_id=1, source_target_pairs={{0,8},{8,16},{16,24},{24,32},{32,40},{40,48},{48,56},{56,64},{64,7... | collective-permute-start | bytes 24584 | tf_op jit(solution)/shard_map/ppermute | solution.py:240
  56.4 5.3 %collective-permute-start.7 = (f32[16,128]{1,0:T(8,128)S(1)}, f32[16,128]{1,0:T(8,128)S(1)}, u32[]{:S(2)}, u32[]{:S(2)}) collective-permute-start(f32[16,128]{1,0:T(8,128)S(1)} %shard_map.173.before), channel_id=1, source_target_pairs={{0,760},{8,0},{16,8},{24,16},{32,24},{40,32},{48,40},{56,48},{64,5... | collective-permute-start | bytes 24584 | tf_op jit(solution)/shard_map/ppermute | solution.py:240
  58.3 7.7 %collective-permute-start.6 = (f32[16,128]{1,0:T(8,128)S(1)}, f32[16,128]{1,0:T(8,128)S(1)}, u32[]{:S(2)}, u32[]{:S(2)}) collective-permute-start(f32[16,128]{1,0:T(8,128)S(1)} %shard_map.173.before), channel_id=1, source_target_pairs={{0,8},{8,16},{16,24},{24,32},{32,40},{40,48},{48,56},{56,64},{64,7... | collective-permute-start | bytes 24584 | tf_op jit(solution)/shard_map/ppermute | solution.py:240
  67.0 11.5 %all-to-all-start.1 = ((f32[8,16,128]{2,1,0:T(8,128)}), f32[8,16,128]{2,1,0:T(8,128)S(1)}, u32[]{:S(2)}, u32[]{:S(2)}) async-start(f32[8,16,128]{2,1,0:T(8,128)} %shard_map.174), calls=%async_computation.1 | async-start | bytes 131072 | tf_op jit(solution)/shard_map/all_to_all | solution.py:339
  73.6 4.9 %copy-start.9 = (f32[125,8]{0,1:T(8,128)S(1)}, f32[125,8]{0,1:T(8,128)}, u32[]{:S(2)}) copy-start(f32[125,8]{0,1:T(8,128)} %param.29) | copy-start | bytes 12004

commit v2 on v1

v2 whole, which is shorter than its diff:
```python
import jax
import jax.numpy as jnp
from jax import lax
from jax.experimental import pallas as pl
from jax.experimental.pallas import tpu as pltpu
from jax.sharding import PartitionSpec as P

NV = 6
NN = 125
NF = 25
FR = 32
ASLOT = 32
MEMBERS = 8
RELAX = 0.7
WALL = 2.0
BF = jnp.bfloat16
F32 = jnp.float32
TOP = lax.Precision.HIGHEST
VMEM = pl.BlockSpec(memory_space=pltpu.VMEM)
ANY = pl.BlockSpec(memory_space=pl.ANY)
HBM = pl.BlockSpec(memory_space=pltpu.HBM)
SMEM = pl.BlockSpec(memory_space=pltpu.SMEM)


def picker(faces, columns=NN):
    place = lax.broadcasted_iota(jnp.int32, (FR, columns), 0)
    node = lax.broadcasted_iota(jnp.int32, (FR, columns), 1)
    p, line = (node * 41) >> 10, (node * 205) >> 10
    q, r = line - 5 * p, node - 5 * line
    rows = []
    for face in faces:
        end = 4 * (face % 2)
        held, index = ((p, 5 * q + r), (q, 5 * p + r), (r, 5 * p + q))[face // 2]
        rows.append(((held == end) & (index == place) & (place < NF)).astype(F32))
    return jnp.concatenate(rows, axis=0).astype(BF)


def dot(a, b, **kw):
    return jnp.dot(a, b, preferred_element_type=F32, **kw)


def split(x):
    high = x.astype(BF)
    return high, (x - high.astype(F32)).astype(BF)


def call(kernel, outs, *args, scratch=(), smem=(), loose=(), hbm_out=(), flops=1000, nbytes=1000):
    flat, tree = jax.tree.flatten(outs)
    return pl.pallas_call(
        kernel,
        out_shape=outs,
        in_specs=[SMEM if i in smem else ANY if i in loose else VMEM for i in range(len(args))],
        out_specs=jax.tree.unflatten(tree, [HBM if i in hbm_out else VMEM for i in range(len(flat))]),
        scratch_shapes=list(scratch),
        compiler_params=pltpu.CompilerParams(vmem_limit_bytes=24 * 2**20),
        cost_estimate=pl.CostEstimate(flops=flops, bytes_accessed=nbytes, transcendentals=0),
    )(*args)


def is_odd():
    return lax.axis_index("gx") % 2 == 1


def faces_kernel(state, low_y, high_y, near_x, far_x):
    half = state.shape[2] // 2
    pick = picker((0, 1, 2, 3))
    odd = is_odd()
    for v in range(NV):
        found = dot(pick, state[v])
        low, high = found[:FR, :half], found[FR : 2 * FR, half:]
        far_x[v] = jnp.where(odd, high, low).astype(BF)
        near_x[v] = jnp.where(odd, low, high).astype(BF)
        low_y[v] = found[2 * FR : 3 * FR].astype(BF)
        high_y[v] = found[3 * FR :].astype(BF)


def halves(x):
    return [part.astype(F32) for part in split(x)]


def transposed_lifts(lift_t):
    gap = jnp.zeros((FR - NF, NN), F32)
    lifts = [jnp.concatenate([lift_t[f].astype(F32), gap], axis=0).T for f in range(6)]
    return jnp.concatenate(lifts, axis=1).astype(BF)


def weights_kernel(volume, viscous, lift_t, restrict, state_side, forcing_side, lift_side):
    both = jnp.concatenate(halves(restrict[...]), axis=0).astype(BF)

    def restricted(matrix):
        parts = dot(both, matrix)
        return halves(parts[:8] + parts[8:])

    lift_side[...] = jnp.concatenate(restricted(transposed_lifts(lift_t)), axis=0).astype(BF)
    forcing_side[...] = both
    parts = restricted(volume[...]) + restricted(viscous[...]) + halves(restrict[...])
    state_side[...] = jnp.concatenate([picker((0, 1, 4, 5)).astype(F32), *parts], axis=0).astype(BF)


def inverse_kernel(inverse, coupling, coarse_side):
    lanes = coarse_side.shape[2]
    rows, modes = inverse.shape[0] // 3, inverse.shape[2]
    blank = jnp.zeros((lanes - 3 * ASLOT, modes), F32)
    for r in range(rows):
        stacked = jnp.concatenate([inverse[r], inverse[rows + r], inverse[2 * rows + r], blank], axis=0)
        coarse_side[r] = RELAX * stacked.T
    coarse_side[rows] = jnp.concatenate([coupling[...], jnp.zeros((modes, lanes - modes), F32)], axis=1)


def restricted_kernel(mix, forcing, state, viscosity, flags, state_side, forcing_side, near, restricted):
    lanes = state.shape[2]
    half = lanes // 2
    place = lax.broadcasted_iota(jnp.int32, (FR, lanes), 1) % half
    visc = viscosity[...]
    fluxes, local = [], []
    for v in range(NV):
        found = dot(state_side[...], state[v])
        given = dot(forcing_side[...], forcing[v])
        t0, t1, t4, t5 = (found[FR * k : FR * (k + 1)] for k in range(4))
        across = t0[:, half:] - t1[:, :half]
        below = jnp.where(place == 0, 0.0, pltpu.roll(t5, 1, 1))
        above = jnp.where(place == half - 1, 0.0, pltpu.roll(t4, lanes - 1, 1))
        near[v, :FR] = jnp.concatenate([across, -across], axis=1).astype(BF)
        near[v, FR : 2 * FR] = (below - t4).astype(BF)
        near[v, 2 * FR :] = (above - t5).astype(BF)
        first = 4 * FR
        rows = [found[first + 16 * k : first + 16 * k + 8] + found[first + 16 * k + 8 : first + 16 * k + 16] for k in range(3)]
        total = given[:8] + given[8:] - visc * rows[1]
        if v == NV - 1:
            total = total - (WALL * flags[...].astype(F32)) * rows[2]
        fluxes.append(rows[0])
        local.append(total)
    for q in range(NV):
        total = local[q]
        for k in range(NV):
            total = total - mix[q, k] * fluxes[k]
        restricted[8 * q : 8 * q + 8] = total


def products_kernel(mix, forcing, state, volume, viscous, viscosity, flags, partial, flux):
    for v in range(NV):
        u = state[v]
        flux[v, :NN] = dot(volume[...], u)
        total = forcing[v].astype(F32) - viscosity[...] * dot(viscous[...], u)
        if v == NV - 1:
            total = total - (WALL * flags[...].astype(F32)) * u.astype(F32)
        partial[v] = total
    for q in range(NV):
        for low in range(0, NN, 16):
            rows = slice(low, min(low + 16, NN))
            total = partial[q, rows]
            for k in range(NV):
                total = total - mix[q, k] * flux[k, rows]
            partial[q, rows] = total


def residual_kernel(partial, jumps, lift_t, residual, out, sems):
    lifts = transposed_lifts(lift_t)
    sends = []
    for v in range(NV):
        out[v] = (partial[v] + dot(lifts, jumps[v])).astype(BF)
        sends.append(pltpu.make_async_copy(out.at[v], residual.at[v], sems.at[v]))
        sends[-1].start()
    for copy in sends:
        copy.wait()


def keys_of(owner, slot):
    return owner[...] * ASLOT + slot[...]


def one_hot(keys):
    groups = MEMBERS * ASLOT
    return (lax.broadcasted_iota(jnp.int32, (groups, keys.shape[1]), 0) == keys).astype(F32).astype(BF)


def sums_kernel(n1, n0, n2, n3, o2, o3, o1, o0, near, lift_side, restricted, owner, slot, blocks, jumps):
    half = owner.shape[1] // 2

    odd = is_odd()

    def difference(a, b):
        return a.astype(F32) - b.astype(F32)

    highs, lows = [], []
    for v in range(NV):
        far, close = difference(n0[v], o0[v]), difference(n1[v], o1[v])
        jumps[v, :FR, :half] = jnp.where(odd, close, far).astype(BF)
        jumps[v, :FR, half:] = near[v, :FR, half:]
        jumps[v, FR : 2 * FR, :half] = near[v, :FR, :half]
        jumps[v, FR : 2 * FR, half:] = jnp.where(odd, far, close).astype(BF)
        jumps[v, 2 * FR : 3 * FR] = difference(n2[v], o2[v]).astype(BF)
        jumps[v, 3 * FR : 4 * FR] = difference(n3[v], o3[v]).astype(BF)
        jumps[v, 4 * FR :] = near[v, FR:]
        both = dot(lift_side[...], jumps[v])
        high, low = halves(restricted[8 * v : 8 * v + 8] + both[:8] + both[8:])
        highs.append(high)
        lows.append(low)
    stacked = jnp.concatenate(highs + lows, axis=0).astype(BF)
    spread = one_hot(keys_of(owner, slot))
    both = lax.dot_general(stacked, spread, (((1,), (1,)), ((), ())), preferred_element_type=F32)
    sums = both[: 8 * NV] + both[8 * NV :]
    group = lax.broadcasted_iota(jnp.int32, (16, 128), 1) // ASLOT
    for m in range(MEMBERS):
        block = jnp.zeros((16, 128), F32)
        for k in range(3):
            piece = sums[16 * k : 16 * k + 16, (m // 4) * 128 : (m // 4 + 1) * 128]
            turn = ((k - m % 4) * ASLOT) % 128
            piece = pltpu.roll(piece, turn, 1) if turn else piece
            block = jnp.where(group == k, piece, block)
        blocks[m] = block


def opened(packed):
    group = lax.broadcasted_iota(jnp.int32, (16, 128), 1) // ASLOT
    rows = []
    for k in range(3):
        only = jnp.where(group == k, packed, 0.0)
        two = only + pltpu.roll(only, 32, 1)
        rows.append(two + pltpu.roll(two, 64, 1))
    return jnp.concatenate(rows, axis=0)


def solve(coarse_side, source, out):
    for r in range(16):
        out[r : r + 1] = jnp.sum(coarse_side[r] * source, axis=0, keepdims=True)


def first_kernel(blocks, coarse_side, _, totals, coarse):
    packed = jnp.sum(blocks[...], axis=0)
    source = opened(packed)
    totals[...] = source
    solve(coarse_side, source, coarse)


def sweep_kernel(up, down, totals, before, coarse_side, coarse):
    beside = opened(up[...] + down[...])
    coupling = coarse_side[16][:, : beside.shape[0]]
    source = totals[...] - dot(coupling, beside, precision=TOP)
    solve(coarse_side, source, coarse)
    coarse[...] = (1.0 - RELAX) * before[...] + coarse[...]


def last_sweep_kernel(up, down, totals, before, coarse_side, blocks, scratch):
    sweep_kernel(up, down, totals, before, coarse_side, scratch)
    for m in range(MEMBERS):
        blocks[m] = scratch[...]


def correction_kernel(blocks, prolong_t, owner, slot, correction, wide, out, sems):
    high, low = (x.astype(F32) for x in split(prolong_t[...]))
    weights = jnp.concatenate([high, low, high], axis=0)
    gap = jnp.zeros((weights.shape[0], wide.shape[0] // NV - NN), F32)
    weights = jnp.concatenate([weights, gap], axis=1).T.astype(BF)
    select = one_hot(keys_of(owner, slot))
    group = lax.broadcasted_iota(jnp.int32, (8, 128), 1) // ASLOT
    step = wide.shape[0] // NV
    for v in range(NV):
        k, rows = v // 2, slice(8 * (v % 2), 8 * (v % 2) + 8)
        parts = []
        for h in range(MEMBERS // 4):
            value = jnp.zeros((8, 128), F32)
            for w in range(4):
                turn = ((w - k) * ASLOT) % 128
                piece = blocks[4 * h + w, rows]
                piece = pltpu.roll(piece, turn, 1) if turn else piece
                value = jnp.where(group == w, piece, value)
            parts.append(value)
        high, low = (x.astype(F32) for x in split(jnp.concatenate(parts, axis=1)))
        values = jnp.concatenate([high, high, low], axis=0).astype(BF)
        wide[step * v : step * (v + 1)] = dot(weights, values).astype(BF)
    sends = []
    for first in range(0, NV, 2):
        found = dot(wide[step * first : step * (first + 2)], select)
        for v in (first, first + 1):
            out[v] = found[step * (v - first) : step * (v - first) + NN].astype(BF)
            sends.append(pltpu.make_async_copy(out.at[v], correction.at[v], sems.at[v]))
            sends[-1].start()
    for copy in sends:
        copy.wait()


def shifted(value, axis, by):
    size = lax.axis_size(axis)
    return lax.ppermute(value, axis, [(i, (i + by) % size) for i in range(size)])


def swapped(value, start):
    size = lax.axis_size("gx")
    return lax.ppermute(value, "gx", [(i, (i + (1 if i % 2 == start else -1)) % size) for i in range(size)])


def struct(shape, dtype):
    return jax.ShapeDtypeStruct(shape, dtype)


def per_device(
    state,
    forcing,
    volume_flux_matrix,
    viscous_matrix,
    linear_flux_matrix,
    viscosity,
    lift,
    wall_flags,
    restriction_weight,
    owner,
    slot,
    coarse_inverse,
    coupling,
    prolongation_weight,
):
    elems = state.shape[2]
    half = elems // 2
    owner, slot = owner.reshape(1, elems), slot.reshape(1, elems)
    viscosity, flags = viscosity.reshape(1, elems), wall_flags.reshape(1, elems)
    x_face, y_face = struct((NV, FR, half), BF), struct((NV, FR, elems), BF)
    field = struct((NV, NN, elems), BF)
    own = call(faces_kernel, (y_face, y_face, x_face, x_face), state, flops=2 * 10**10)
    far_x, near_x = swapped(own[3], 1), swapped(own[2], 0)
    restrict, inverse, _ = lax.optimization_barrier(
        (restriction_weight, jnp.transpose(coarse_inverse, (0, 2, 1)), own[0])
    )
    coarse_side = call(inverse_kernel, struct((17, 48, 128), F32), inverse, coupling)
    near = (near_x, far_x, shifted(own[1], "gy", 1), shifted(own[0], "gy", -1))
    lift_t = jnp.transpose(lift, (0, 2, 1))
    state_side, forcing_side, lift_side = call(
        weights_kernel,
        (struct((4 * FR + 48, NN), BF), struct((16, NN), BF), struct((16, 6 * FR), BF)),
        volume_flux_matrix,
        viscous_matrix,
        lift_t,
        restrict,
    )
    inner, restricted = call(
        restricted_kernel,
        (struct((NV, 3 * FR, elems), BF), struct((48, elems), F32)),
        linear_flux_matrix,
        forcing,
        state,
        viscosity,
        flags,
        state_side,
        forcing_side,
        smem=(0,),
    )
    restricted, coarse_side = lax.optimization_barrier((restricted, coarse_side))
    blocks, jumps = call(
        sums_kernel,
        (struct((MEMBERS, 16, 128), F32), struct((NV, 6 * FR, elems), BF)),
        *near,
        *own,
        inner,
        lift_side,
        restricted,
        owner,
        slot,
    )
    viscous_matrix, _ = lax.optimization_barrier((viscous_matrix, blocks))
    partial = call(
        products_kernel,
        struct((NV, NN, elems), F32),
        linear_flux_matrix,
        forcing,
        state,
        volume_flux_matrix,
        viscous_matrix,
        viscosity,
        flags,
        scratch=[pltpu.VMEM((NV, 128, elems), F32)],
        smem=(0,),
    )
    blocks = lax.all_to_all(blocks, "gy", 0, 0, tiled=True)
    totals, coarse = call(
        first_kernel,
        (struct((48, 128), F32), struct((16, 128), F32)),
        blocks,
        coarse_side,
        partial,
        loose=(2,),
    )
    up, down = swapped(coarse, 0), swapped(coarse, 1)
    coarse = call(sweep_kernel, struct((16, 128), F32), up, down, totals, coarse, coarse_side)
    up, down = swapped(coarse, 0), swapped(coarse, 1)
    blocks = call(
        last_sweep_kernel,
        struct((MEMBERS, 16, 128), F32),
        up,
        down,
        totals,
        coarse,
        coarse_side,
        scratch=[pltpu.VMEM((16, 128), F32)],
    )
    partial, _ = lax.optimization_barrier((partial, blocks))
    residual = call(
        residual_kernel,
        field,
        partial,
        jumps,
        lift_t,
        hbm_out=(0,),
        scratch=[pltpu.VMEM((NV, NN, elems), BF), pltpu.SemaphoreType.DMA((NV,))],
    )
    blocks = lax.all_to_all(blocks, "gy", 0, 0, tiled=True)
    correction = call(
        correction_kernel,
        field,
        blocks,
        jnp.transpose(prolongation_weight),
        owner,
        slot,
        hbm_out=(0,),
        scratch=[
            pltpu.VMEM((128 * NV, MEMBERS * ASLOT), BF),
            pltpu.VMEM((NV, NN, elems), BF),
            pltpu.SemaphoreType.DMA((NV,)),
        ],
    )
    return residual, correction


def solution(mesh):
    split_last = P(None, None, ("gx", "gy"))
    flat = P(("gx", "gy"))
    return jax.shard_map(
        per_device,
        mesh=mesh,
        in_specs=(
            split_last,
            split_last,
            P(),
            P(),
            P(),
            flat,
            P(),
            flat,
            P(),
            P(("gx", "gy"), None),
            flat,
            split_last,
            P(),
            P(),
        ),
        out_specs=(split_last, split_last),
        check_vma=False,
    )
```

time: 82.5 us -> 73.6 us (0.89)
  blocking collectives: 9.87 us -> 0 us
  starting transfers between devices: 39.2 us -> 48.9 us
  local copies, waits for them, and re-layouts: 7.17 us -> 3.36 us
  waiting for transfers between devices: 13.7 us -> 10.2 us
  Pallas kernels: 10.9 us -> 9.57 us
    ppermute x0 -> x6, starting transfers between devices: none -> 25.6 us  [swapped(): lax.ppermute(value, 'gx', [(i, (i + (1 if i % 2 == start else -1)) % size...]
    ppermute x8 -> x2, starting transfers between devices: 32.6 us -> 10.5 us  [shifted(): lax.ppermute(value, axis, [(i, (i + by) % size) for i in range(size)])]
    ppermute x8 -> x2, waiting for transfers between devices: 10.1 us -> 0.01 us  [shifted(): lax.ppermute(value, axis, [(i, (i + by) % size) for i in range(size)])]
    all_to_all x1 -> x0, blocking collectives: 9.87 us -> none  [per_device(): blocks = lax.all_to_all(blocks, 'gy', 0, 0, tiled=True)]
    all_to_all x1 -> x2, starting transfers between devices: 6.61 us -> 12.8 us  [per_device(): blocks = lax.all_to_all(blocks, 'gy', 0, 0, tiled=True)]
    ppermute x0 -> x6, waiting for transfers between devices: none -> 4.93 us  [swapped(): lax.ppermute(value, 'gx', [(i, (i + (1 if i % 2 == start else -1)) % size...]
    unnamed x34 -> x36, local copies, waits for them, and re-layouts: 7.17 us -> 3.36 us
    all_to_all x1 -> x2, waiting for transfers between devices: 3.61 us -> 5.28 us  [per_device(): blocks = lax.all_to_all(blocks, 'gy', 0, 0, tiled=True)]
  transfers between devices with their start and end apart: 9 -> 10, of which waited for: 3 -> 4; matrix products, arithmetic and copies ran while one was open for 0% -> 0% of each run, Pallas kernels for 7% -> 7%
where the time goes in v2:
time: 73.6 us; the launch traced here: 73 us
  starting transfers between devices  48.9 us (66%)
  waiting for transfers between devices  10.2 us (14%)
  Pallas kernels  9.57 us (13%)
  local copies, waits for them, and re-layouts  3.36 us (5%)
  between operations  0.97 us (1%)
    ppermute x6, starting transfers between devices, swapped(): lax.ppermute(value, 'gx', [(i, (i + (1 if i % 2 == start else -1)) % size...  25.6 us
    all_to_all x2, starting transfers between devices, per_device(): blocks = lax.all_to_all(blocks, 'gy', 0, 0, tiled=True)  12.8 us
    ppermute x2, starting transfers between devices, shifted(): lax.ppermute(value, axis, [(i, (i + by) % size) for i in range(size)])  10.5 us
    pallas_call x11, Pallas kernels, call(): pl.pallas_call(kernel, out_shape=outs, in_specs=[SMEM if i in smem else A...  9.57 us
    all_to_all x2, waiting for transfers between devices, per_device(): blocks = lax.all_to_all(blocks, 'gy', 0, 0, tiled=True)  5.28 us
    ppermute x6, waiting for transfers between devices, swapped(): lax.ppermute(value, 'gx', [(i, (i + (1 if i % 2 == start else -1)) % size...  4.93 us
    unnamed x36, local copies, waits for them, and re-layouts  3.36 us
  transfers between devices with their start and end apart: 10, of which 4 were waited for; matrix products, arithmetic and copies ran while one was open for 0% of the time, Pallas kernels for 7%

profile of v2, /device:TPU:1, one launch (start us, length us, event | category | flops | bytes accessed | tf_op | source)
XLA Modules:
  0.0 73.0 jit_solution(424230122069978966)
XLA Ops:
  0.6 0.0 copy-start.1
  0.6 1.1 %copy-done.1 = bf16[6,125,512]{2,1,0:T(8,128)(2,1)S(1)} copy-done((bf16[6,125,512]{2,1,0:T(8,128)(2,1)S(1)}, bf16[6,125,512]{2,1,0:T(8,128)(2,1)}, u32[]{:S(2)}) %copy-start.1) | copy-done | bytes 768024
  1.8 0.0 copy-start.6
  1.8 0.0 copy-start.10
  1.8 0.0 copy-start.7
  1.8 0.0 copy-start.8
  1.8 0.0 copy-start.9
  1.8 0.0 copy-start.17
  1.8 0.0 copy-start.2
  1.8 0.0 copy-start.11
  1.8 0.0 copy-start.12
  1.8 0.0 copy-start.13
  1.8 0.4 shard_map.149
  2.2 0.0 copy-start
  2.2 0.0 copy-start.14
  2.2 0.0 copy-start.15
  2.2 2.6 %collective-permute-start.2 = (bf16[6,32,512]{2,1,0:T(8,128)(2,1)S(1)}, bf16[6,32,512]{2,1,0:T(8,128)(2,1)S(1)}, u32[]{:S(2)}, u32[]{:S(2)}) collective-permute-start(bf16[6,32,512]{2,1,0:T(8,128)(2,1)S(1)} %get-tuple-element.23.o3), channel_id=1, source_target_pairs={{0,1},{1,2},{2,3},{3,4},{4,5},{5,6},{6,7},{7,0},{8,9},{9,10},{10,1... | collective-permute-start | bytes 589832 | tf_op jit(solution)/shard_map/ppermute | solution.py:285
  4.8 7.9 %collective-permute-start.3 = (bf16[6,32,512]{2,1,0:T(8,128)(2,1)S(1)}, bf16[6,32,512]{2,1,0:T(8,128)(2,1)S(1)}, u32[]{:S(2)}, u32[]{:S(2)}) collective-permute-start(bf16[6,32,512]{2,1,0:T(8,128)(2,1)S(1)} %get-tuple-element.24.o2), channel_id=1, source_target_pairs={{0,7},{1,0},{2,1},{3,2},{4,3},{5,4},{6,5},{7,6},{8,15},{9,8},{10,9... | collective-permute-start | bytes 589832 | tf_op jit(solution)/shard_map/ppermute | solution.py:285
  12.8 1.9 %collective-permute-start = (bf16[6,32,256]{2,1,0:T(8,128)(2,1)S(1)}, bf16[6,32,256]{2,1,0:T(8,128)(2,1)S(1)}, u32[]{:S(2)}, u32[]{:S(2)}) collective-permute-start(bf16[6,32,256]{2,1,0:T(8,128)(2,1)S(1)} %get-tuple-element.21.o1), channel_id=1, source_target_pairs={{0,8},{8,0},{16,24},{24,16},{32,40},{40,32},{48,56},{56,48},{64,72... | collective-permute-start | bytes 294920 | tf_op jit(solution)/shard_map/ppermute | solution.py:290
  14.7 9.5 %collective-permute-start.1 = (bf16[6,32,256]{2,1,0:T(8,128)(2,1)S(1)}, bf16[6,32,256]{2,1,0:T(8,128)(2,1)S(1)}, u32[]{:S(2)}, u32[]{:S(2)}) collective-permute-start(bf16[6,32,256]{2,1,0:T(8,128)(2,1)S(1)} %get-tuple-element.22.o0), channel_id=1, source_target_pairs={{0,760},{8,16},{16,8},{24,32},{32,24},{40,48},{48,40},{56,64},{64,... | collective-permute-start | bytes 294920 | tf_op jit(solution)/shard_map/ppermute | solution.py:290
  24.2 0.0 copy-done.6
  24.3 0.0 copy-done.10
  24.3 0.3 shard_map.152.coarse_side
  24.5 0.0 copy-done.7
  24.5 0.0 copy-done.8
  24.5 0.0 copy-done.9
  24.6 0.0 copy-done.17
  24.6 0.4 shard_map.150
  24.9 0.0 copy-done.2
  24.9 0.0 copy-done.11
  25.0 0.0 copy-done.12
  25.0 0.0 copy-done.13
  25.0 0.0 copy-done
  25.0 1.3 %shard_map.151 = (bf16[6,96,512]{2,1,0:T(8,128)(2,1)S(1)}, f32[48,512]{1,0:T(8,128)S(1)}) custom-call(f32[6,6]{1,0:T(8,128)S(1)} %copy-done.11, bf16[6,125,512]{2,1,0:T(8,128)(2,1)S(1)} %copy-done, bf16[6,125,512]{2,1,0:T(8,128)(2,1)S(1)} %copy-done.2, f32[1,512]{1,0:T(1,128)S(1)} %bitcast.10, s32[1,512]{1,0:T(1,128)S(1)} %bitcast.12, ...), custom_call_target="tpu_custom_call" | custom-call | flops 1000 | bytes 1000 | tf_op jit(solution)/shard_map/pallas_call | solution.py:49
  26.3 0.0 collective-permute-done.n1
  26.3 0.0 collective-permute-done.1.n0
  26.3 0.0 collective-permute-done.2.n2
  26.3 0.0 collective-permute-done.3.n3
  26.3 0.0 copy-done.14
  26.3 0.0 copy-done.15
  26.3 1.2 %shard_map.153 = (f32[8,16,128]{2,1,0:T(8,128)}, bf16[6,192,512]{2,1,0:T(8,128)(2,1)S(1)}) custom-call(bf16[6,32,256]{2,1,0:T(8,128)(2,1)S(1)} %collective-permute-done.n1, bf16[6,32,256]{2,1,0:T(8,128)(2,1)S(1)} %collective-permute-done.1.n0, bf16[6,32,512]{2,1,0:T(8,128)(2,1)S(1)} %collective-permute-done.2.n2, ...), custom_call_target="tpu_custom_call" | custom-call | flops 1000 | bytes 1000 | tf_op jit(solution)/shard_map/pallas_call | solution.py:49
  27.5 1.0 %copy-done.4 = bf16[6,192,512]{2,1,0:T(8,128)(2,1)} copy-done((bf16[6,192,512]{2,1,0:T(8,128)(2,1)}, bf16[6,192,512]{2,1,0:T(8,128)(2,1)S(1)}, u32[]{:S(2)}) %copy-start.4) | copy-done | bytes 1179672
  28.6 6.2 %all-to-all-start = ((f32[8,16,128]{2,1,0:T(8,128)}), f32[8,16,128]{2,1,0:T(8,128)S(1)}, u32[]{:S(2)}, u32[]{:S(2)}) async-start(f32[8,16,128]{2,1,0:T(8,128)} %get-tuple-element.33), calls=%async_computation | async-start | bytes 131072 | tf_op jit(solution)/shard_map/all_to_all | solution.py:373
  34.8 1.1 %copy-done.3 = bf16[6,125,512]{2,1,0:T(8,128)(2,1)S(1)} copy-done((bf16[6,125,512]{2,1,0:T(8,128)(2,1)S(1)}, bf16[6,125,512]{2,1,0:T(8,128)(2,1)}, u32[]{:S(2)}) %copy-start.3) | copy-done | bytes 768024
  35.9 2.0 %shard_map.154._.partial = f32[6,125,512]{2,1,0:T(8,128)S(1)} custom-call(f32[6,6]{1,0:T(8,128)S(1)} %copy-done.11, bf16[6,125,512]{2,1,0:T(8,128)(2,1)S(1)} %copy-done, bf16[6,125,512]{2,1,0:T(8,128)(2,1)S(1)} %copy-done.3, bf16[125,125]{1,0:T(8,128)(2,1)S(1)} %copy-done.8, bf16[125,125]{1,0:T(8,128)(2,1)S(1)} %copy-done.9, f32[1,512]{1,0:T(1,128)S(1)} %bitcast.11, ...), custom_call_target="tpu_custom_call" | custom-call | flops 1000 | bytes 1000 | tf_op jit(solution)/shard_map/pallas_call | solution.py:49
  37.9 0.0 copy-start.5
  37.9 1.7 %all-to-all-done.blocks = f32[8,16,128]{2,1,0:T(8,128)S(1)} async-done(((f32[8,16,128]{2,1,0:T(8,128)}), f32[8,16,128]{2,1,0:T(8,128)S(1)}, u32[]{:S(2)}, u32[]{:S(2)}) %all-to-all-start) | async-done | bytes 65568 | tf_op jit(solution)/shard_map/all_to_all | solution.py:373
  39.7 0.2 shard_map.155
  39.8 7.0 %collective-permute-start.5 = (f32[16,128]{1,0:T(8,128)S(1)}, f32[16,128]{1,0:T(8,128)S(1)}, u32[]{:S(2)}, u32[]{:S(2)}) collective-permute-start(f32[16,128]{1,0:T(8,128)S(1)} %get-tuple-element.36.before), channel_id=1, source_target_pairs={{0,760},{8,16},{16,8},{24,32},{32,24},{40,48},{48,40},{56,64},{64,... | collective-permute-start | bytes 24584 | tf_op jit(solution)/shard_map/ppermute | solution.py:290
  46.8 1.9 %collective-permute-start.4 = (f32[16,128]{1,0:T(8,128)S(1)}, f32[16,128]{1,0:T(8,128)S(1)}, u32[]{:S(2)}, u32[]{:S(2)}) collective-permute-start(f32[16,128]{1,0:T(8,128)S(1)} %get-tuple-element.36.before), channel_id=1, source_target_pairs={{0,8},{8,0},{16,24},{24,16},{32,40},{40,32},{48,56},{56,48},{64,72... | collective-permute-start | bytes 24584 | tf_op jit(solution)/shard_map/ppermute | solution.py:290
  48.7 0.0 collective-permute-done.5.down
  48.8 2.5 %collective-permute-done.4.up = f32[16,128]{1,0:T(8,128)S(1)} collective-permute-done((f32[16,128]{1,0:T(8,128)S(1)}, f32[16,128]{1,0:T(8,128)S(1)}, u32[]{:S(2)}, u32[]{:S(2)}) %collective-permute-start.4) | collective-permute-done | bytes 8224 | tf_op jit(solution)/shard_map/ppermute | solution.py:290
  51.2 0.3 shard_map.156.before
  51.5 3.3 %collective-permute-start.7 = (f32[16,128]{1,0:T(8,128)S(1)}, f32[16,128]{1,0:T(8,128)S(1)}, u32[]{:S(2)}, u32[]{:S(2)}) collective-permute-start(f32[16,128]{1,0:T(8,128)S(1)} %shard_map.156.before), channel_id=1, source_target_pairs={{0,760},{8,16},{16,8},{24,32},{32,24},{40,48},{48,40},{56,64},{64,... | collective-permute-start | bytes 24584 | tf_op jit(solution)/shard_map/ppermute | solution.py:290
  54.9 1.9 %collective-permute-start.6 = (f32[16,128]{1,0:T(8,128)S(1)}, f32[16,128]{1,0:T(8,128)S(1)}, u32[]{:S(2)}, u32[]{:S(2)}) collective-permute-start(f32[16,128]{1,0:T(8,128)S(1)} %shard_map.156.before), channel_id=1, source_target_pairs={{0,8},{8,0},{16,24},{24,16},{32,40},{40,32},{48,56},{56,48},{64,72... | collective-permute-start | bytes 24584 | tf_op jit(solution)/shard_map/ppermute | solution.py:290
  56.8 2.5 %collective-permute-done.7.down = f32[16,128]{1,0:T(8,128)S(1)} collective-permute-done((f32[16,128]{1,0:T(8,128)S(1)}, f32[16,128]{1,0:T(8,128)S(1)}, u32[]{:S(2)}, u32[]{:S(2)}) %collective-permute-start.7) | collective-permute-done | bytes 8224 | tf_op jit(solution)/shard_map/ppermute | solution.py:290
  59.3 0.0 collective-permute-done.6.up
  59.3 1.0 %shard_map.157 = f32[8,16,128]{2,1,0:T(8,128)} custom-call(f32[16,128]{1,0:T(8,128)S(1)} %collective-permute-done.6.up, f32[16,128]{1,0:T(8,128)S(1)} %collective-permute-done.7.down, f32[48,128]{1,0:T(8,128)S(1)} %get-tuple-element.37.totals, f32[16,128]{1,0:T(8,128)S(1)} %shard_map.156.before, f32[17,48,128]{2,1,0:T(8,128)S(1)} %shard_map.152.coarse_side), custom_call_target="tpu_custom_call" | custom-call | flops 1000 | bytes 1000 | tf_op jit(solution)/shard_map/pallas_call | solution.py:49
  60.2 6.6 %all-to-all-start.1 = ((f32[8,16,128]{2,1,0:T(8,128)}), f32[8,16,128]{2,1,0:T(8,128)S(1)}, u32[]{:S(2)}, u32[]{:S(2)}) async-start(f32[8,16,128]{2,1,0:T(8,128)} %shard_map.157), calls=%async_computation.1 | async-start | bytes 131072 | tf_op jit(solution)/shard_map/all_to_all | solution.py:405
  66.9 0.0 copy-done.5
  66.9 1.3 %shard_map.158 = bf16[6,125,512]{2,1,0:T(8,128)(2,1)} custom-call(f32[6,125,512]{2,1,0:T(8,128)S(1)} %shard_map.154._.partial, bf16[6,192,512]{2,1,0:T(8,128)(2,1)S(1)} %copy-done.5, bf16[6,25,125]{2,1,0:T(8,128)(2,1)S(1)} %bitcast.9), custom_call_target="tpu_custom_call" | custom-call | flops 1000 | bytes 1000 | tf_op jit(solution)/shard_map/pallas_call | solution.py:49
  68.2 3.6 %all-to-all-done.1.blocks = f32[8,16,128]{2,1,0:T(8,128)S(1)} async-done(((f32[8,16,128]{2,1,0:T(8,128)}), f32[8,16,128]{2,1,0:T(8,128)S(1)}, u32[]{:S(2)}, u32[]{:S(2)}) %all-to-all-start.1) | async-done | bytes 65568 | tf_op jit(solution)/shard_map/all_to_all | solution.py:405
  71.7 0.0 copy-done.16
  71.7 1.3 %shard_map.159 = bf16[6,125,512]{2,1,0:T(8,128)(2,1)} custom-call(f32[8,16,128]{2,1,0:T(8,128)S(1)} %all-to-all-done.1.blocks, f32[8,125]{1,0:T(8,128)S(1)} %bitcast.18, s32[1,512]{1,0:T(1,128)S(1)} %bitcast.15, s32[1,512]{1,0:T(1,128)S(1)} %bitcast.17), custom_call_target="tpu_custom_call" | custom-call | flops 1000 | bytes 1000 | tf_op jit(solution)/shard_map/pallas_call | solution.py:49
  (3 shorter events, 0.0 us)
Async XLA Ops:
  0.6 1.1 %copy-start.1 = (bf16[6,125,512]{2,1,0:T(8,128)(2,1)S(1)}, bf16[6,125,512]{2,1,0:T(8,128)(2,1)}, u32[]{:S(2)}) copy-start(bf16[6,125,512]{2,1,0:T(8,128)(2,1)} %state.5) | copy-start | bytes 2304004
  1.8 22.5 %copy-start.6 = (f32[48,48,32]{1,2,0:T(8,128)S(1)}, f32[48,48,32]{1,2,0:T(8,128)}, u32[]{:S(2)}) copy-start(f32[48,48,32]{1,2,0:T(8,128)} %param.25) | copy-start | bytes 884740
  1.8 22.5 %copy-start.10 = (f32[48,48]{1,0:T(8,128)S(1)}, f32[48,48]{1,0:T(8,128)}, u32[]{:S(2)}) copy-start(f32[48,48]{1,0:T(8,128)} %coupling.1) | copy-start | bytes 27652
  1.8 22.8 %copy-start.7 = (bf16[6,125,25]{1,2,0:T(8,128)(2,1)S(1)}, bf16[6,125,25]{1,2,0:T(8,128)(2,1)}, u32[]{:S(2)}) copy-start(bf16[6,125,25]{1,2,0:T(8,128)(2,1)} %param.20) | copy-start | bytes 112504
  1.8 22.8 %copy-start.8 = (bf16[125,125]{1,0:T(8,128)(2,1)S(1)}, bf16[125,125]{1,0:T(8,128)(2,1)}, u32[]{:S(2)}) copy-start(bf16[125,125]{1,0:T(8,128)(2,1)} %volume.3) | copy-start | bytes 93754
  1.8 22.8 %copy-start.9 = (bf16[125,125]{1,0:T(8,128)(2,1)S(1)}, bf16[125,125]{1,0:T(8,128)(2,1)}, u32[]{:S(2)}) copy-start(bf16[125,125]{1,0:T(8,128)(2,1)} %viscous.2) | copy-start | bytes 93754
  1.8 22.8 %copy-start.17 = (f32[8,125]{1,0:T(8,128)S(1)}, f32[8,125]{1,0:T(8,128)}, u32[]{:S(2)}) copy-start(f32[8,125]{1,0:T(8,128)} %restrict) | copy-start | bytes 12004
  1.8 23.1 %copy-start.2 = (bf16[6,125,512]{2,1,0:T(8,128)(2,1)S(1)}, bf16[6,125,512]{2,1,0:T(8,128)(2,1)}, u32[]{:S(2)}) copy-start(bf16[6,125,512]{2,1,0:T(8,128)(2,1)} %state.5) | copy-start | bytes 2304004
  1.8 23.1 %copy-start.11 = (f32[6,6]{1,0:T(8,128)S(1)}, f32[6,6]{1,0:T(8,128)}, u32[]{:S(2)}) copy-start(f32[6,6]{1,0:T(8,128)} %mix.3) | copy-start | bytes 436
  1.8 23.1 %copy-start.12 = (f32[512]{0:T(512)S(1)}, f32[512]{0:T(512)}, u32[]{:S(2)}) copy-start(f32[512]{0:T(512)} %param.19) | copy-start | bytes 6148
  1.8 23.1 %copy-start.13 = (s32[512]{0:T(512)S(1)}, s32[512]{0:T(512)}, u32[]{:S(2)}) copy-start(s32[512]{0:T(512)} %param.21) | copy-start | bytes 6148
  2.2 22.8 %copy-start = (bf16[6,125,512]{2,1,0:T(8,128)(2,1)S(1)}, bf16[6,125,512]{2,1,0:T(8,128)(2,1)}, u32[]{:S(2)}) copy-start(bf16[6,125,512]{2,1,0:T(8,128)(2,1)} %forcing.3) | copy-start | bytes 2304004
  2.2 24.1 %copy-start.14 = (s32[512,1]{0,1:T(1,128)S(1)}, s32[512,1]{0,1:T(1,128)}, u32[]{:S(2)}) copy-start(s32[512,1]{0,1:T(1,128)} %param.23) | copy-start | bytes 6148
  2.2 24.1 %copy-start.15 = (s32[512]{0:T(512)S(1)}, s32[512]{0:T(512)}, u32[]{:S(2)}) copy-start(s32[512]{0:T(512)} %param.24) | copy-start | bytes 6148
  2.2 24.0 %collective-permute-start.2 = (bf16[6,32,512]{2,1,0:T(8,128)(2,1)S(1)}, bf16[6,32,512]{2,1,0:T(8,128)(2,1)S(1)}, u32[]{:S(2)}, u32[]{:S(2)}) collective-permute-start(bf16[6,32,512]{2,1,0:T(8,128)(2,1)S(1)} %get-tuple-element.23.o3), channel_id=1, source_target_pairs={{0,1},{1,2},{2,3},{3,4},{4,5},{5,6},{6,7},{7,0},{8,9},{9,10},{10,1... | collective-permute-start | bytes 589832 | tf_op jit(solution)/shard_map/ppermute | solution.py:285
  4.8 21.4 %collective-permute-start.3 = (bf16[6,32,512]{2,1,0:T(8,128)(2,1)S(1)}, bf16[6,32,512]{2,1,0:T(8,128)(2,1)S(1)}, u32[]{:S(2)}, u32[]{:S(2)}) collective-permute-start(bf16[6,32,512]{2,1,0:T(8,128)(2,1)S(1)} %get-tuple-element.24.o2), channel_id=1, source_target_pairs={{0,7},{1,0},{2,1},{3,2},{4,3},{5,4},{6,5},{7,6},{8,15},{9,8},{10,9... | collective-permute-start | bytes 589832 | tf_op jit(solution)/shard_map/ppermute | solution.py:285
  12.8 13.5 %collective-permute-start = (bf16[6,32,256]{2,1,0:T(8,128)(2,1)S(1)}, bf16[6,32,256]{2,1,0:T(8,128)(2,1)S(1)}, u32[]{:S(2)}, u32[]{:S(2)}) collective-permute-start(bf16[6,32,256]{2,1,0:T(8,128)(2,1)S(1)} %get-tuple-element.21.o1), channel_id=1, source_target_pairs={{0,8},{8,0},{16,24},{24,16},{32,40},{40,32},{48,56},{56,48},{64,72... | collective-permute-start | bytes 294920 | tf_op jit(solution)/shard_map/ppermute | solution.py:290
  14.7 11.6 %collective-permute-start.1 = (bf16[6,32,256]{2,1,0:T(8,128)(2,1)S(1)}, bf16[6,32,256]{2,1,0:T(8,128)(2,1)S(1)}, u32[]{:S(2)}, u32[]{:S(2)}) collective-permute-start(bf16[6,32,256]{2,1,0:T(8,128)(2,1)S(1)} %get-tuple-element.22.o0), channel_id=1, source_target_pairs={{0,760},{8,16},{16,8},{24,32},{32,24},{40,48},{48,40},{56,64},{64,... | collective-permute-start | bytes 294920 | tf_op jit(solution)/shard_map/ppermute | solution.py:290
  27.5 1.0 %copy-start.4 = (bf16[6,192,512]{2,1,0:T(8,128)(2,1)}, bf16[6,192,512]{2,1,0:T(8,128)(2,1)S(1)}, u32[]{:S(2)}) copy-start(bf16[6,192,512]{2,1,0:T(8,128)(2,1)S(1)} %get-tuple-element.39.jumps) | copy-start | bytes 3538948
  28.6 11.1 %all-to-all-start = ((f32[8,16,128]{2,1,0:T(8,128)}), f32[8,16,128]{2,1,0:T(8,128)S(1)}, u32[]{:S(2)}, u32[]{:S(2)}) async-start(f32[8,16,128]{2,1,0:T(8,128)} %get-tuple-element.33), calls=%async_computation | async-start | bytes 131072 | tf_op jit(solution)/shard_map/all_to_all | solution.py:373
  34.8 1.1 %copy-start.3 = (bf16[6,125,512]{2,1,0:T(8,128)(2,1)S(1)}, bf16[6,125,512]{2,1,0:T(8,128)(2,1)}, u32[]{:S(2)}) copy-start(bf16[6,125,512]{2,1,0:T(8,128)(2,1)} %state.5) | copy-start | bytes 2304004
  37.9 28.9 %copy-start.5 = (bf16[6,192,512]{2,1,0:T(8,128)(2,1)S(1)}, bf16[6,192,512]{2,1,0:T(8,128)(2,1)}, u32[]{:S(2)}) copy-start(bf16[6,192,512]{2,1,0:T(8,128)(2,1)} %copy-done.4) | copy-start | bytes 3538948
  39.8 8.9 %collective-permute-start.5 = (f32[16,128]{1,0:T(8,128)S(1)}, f32[16,128]{1,0:T(8,128)S(1)}, u32[]{:S(2)}, u32[]{:S(2)}) collective-permute-start(f32[16,128]{1,0:T(8,128)S(1)} %get-tuple-element.36.before), channel_id=1, source_target_pairs={{0,760},{8,16},{16,8},{24,32},{32,24},{40,48},{48,40},{56,64},{64,... | collective-permute-start | bytes 24584 | tf_op jit(solution)/shard_map/ppermute | solution.py:290
  46.8 4.4 %collective-permute-start.4 = (f32[16,128]{1,0:T(8,128)S(1)}, f32[16,128]{1,0:T(8,128)S(1)}, u32[]{:S(2)}, u32[]{:S(2)}) collective-permute-start(f32[16,128]{1,0:T(8,128)S(1)} %get-tuple-element.36.before), channel_id=1, source_target_pairs={{0,8},{8,0},{16,24},{24,16},{32,40},{40,32},{48,56},{56,48},{64,72... | collective-permute-start | bytes 24584 | tf_op jit(solution)/shard_map/ppermute | solution.py:290
  51.5 7.7 %collective-permute-start.7 = (f32[16,128]{1,0:T(8,128)S(1)}, f32[16,128]{1,0:T(8,128)S(1)}, u32[]{:S(2)}, u32[]{:S(2)}) collective-permute-start(f32[16,128]{1,0:T(8,128)S(1)} %shard_map.156.before), channel_id=1, source_target_pairs={{0,760},{8,16},{16,8},{24,32},{32,24},{40,48},{48,40},{56,64},{64,... | collective-permute-start | bytes 24584 | tf_op jit(solution)/shard_map/ppermute | solution.py:290
  54.9 4.4 %collective-permute-start.6 = (f32[16,128]{1,0:T(8,128)S(1)}, f32[16,128]{1,0:T(8,128)S(1)}, u32[]{:S(2)}, u32[]{:S(2)}) collective-permute-start(f32[16,128]{1,0:T(8,128)S(1)} %shard_map.156.before), channel_id=1, source_target_pairs={{0,8},{8,0},{16,24},{24,16},{32,40},{40,32},{48,56},{56,48},{64,72... | collective-permute-start | bytes 24584 | tf_op jit(solution)/shard_map/ppermute | solution.py:290
  60.2 11.5 %all-to-all-start.1 = ((f32[8,16,128]{2,1,0:T(8,128)}), f32[8,16,128]{2,1,0:T(8,128)S(1)}, u32[]{:S(2)}, u32[]{:S(2)}) async-start(f32[8,16,128]{2,1,0:T(8,128)} %shard_map.157), calls=%async_computation.1 | async-start | bytes 131072 | tf_op jit(solution)/shard_map/all_to_all | solution.py:405
  66.9 4.9 %copy-start.16 = (f32[125,8]{0,1:T(8,128)S(1)}, f32[125,8]{0,1:T(8,128)}, u32[]{:S(2)}) copy-start(f32[125,8]{0,1:T(8,128)} %param.27) | copy-start | bytes 12004

commit v3 on v2

--- a/solution.py
+++ b/solution.py
@@ -17,7 +17,6 @@
 F32 = jnp.float32
 TOP = lax.Precision.HIGHEST
 VMEM = pl.BlockSpec(memory_space=pltpu.VMEM)
-ANY = pl.BlockSpec(memory_space=pl.ANY)
 HBM = pl.BlockSpec(memory_space=pltpu.HBM)
 SMEM = pl.BlockSpec(memory_space=pltpu.SMEM)
 
@@ -44,12 +43,12 @@
     return high, (x - high.astype(F32)).astype(BF)
 
 
-def call(kernel, outs, *args, scratch=(), smem=(), loose=(), hbm_out=(), flops=1000, nbytes=1000):
+def call(kernel, outs, *args, scratch=(), smem=(), hbm_out=(), flops=1000, nbytes=1000):
     flat, tree = jax.tree.flatten(outs)
     return pl.pallas_call(
         kernel,
         out_shape=outs,
-        in_specs=[SMEM if i in smem else ANY if i in loose else VMEM for i in range(len(args))],
+        in_specs=[SMEM if i in smem else VMEM for i in range(len(args))],
         out_specs=jax.tree.unflatten(tree, [HBM if i in hbm_out else VMEM for i in range(len(flat))]),
         scratch_shapes=list(scratch),
         compiler_params=pltpu.CompilerParams(vmem_limit_bytes=24 * 2**20),
@@ -137,30 +136,28 @@
         restricted[8 * q : 8 * q + 8] = total
 
 
-def products_kernel(mix, forcing, state, volume, viscous, viscosity, flags, partial, flux):
+def residual_kernel(
+    mix, forcing, state, volume, viscous, viscosity, flags, lift_t, jumps, residual, done, flux, local, out, sems
+):
+    lifts = transposed_lifts(lift_t)
     for v in range(NV):
         u = state[v]
         flux[v, :NN] = dot(volume[...], u)
-        total = forcing[v].astype(F32) - viscosity[...] * dot(viscous[...], u)
+        total = forcing[v].astype(F32) - viscosity[...] * dot(viscous[...], u) + dot(lifts, jumps[v])
         if v == NV - 1:
             total = total - (WALL * flags[...].astype(F32)) * u.astype(F32)
-        partial[v] = total
+        local[v] = total
+    sends = []
     for q in range(NV):
         for low in range(0, NN, 16):
             rows = slice(low, min(low + 16, NN))
-            total = partial[q, rows]
+            total = local[q, rows]
             for k in range(NV):
                 total = total - mix[q, k] * flux[k, rows]
-            partial[q, rows] = total
-
-
-def residual_kernel(partial, jumps, lift_t, residual, out, sems):
-    lifts = transposed_lifts(lift_t)
-    sends = []
-    for v in range(NV):
-        out[v] = (partial[v] + dot(lifts, jumps[v])).astype(BF)
-        sends.append(pltpu.make_async_copy(out.at[v], residual.at[v], sems.at[v]))
+            out[q, rows] = total.astype(BF)
+        sends.append(pltpu.make_async_copy(out.at[q], residual.at[q], sems.at[q]))
         sends[-1].start()
+    done[...] = jnp.zeros_like(done)
     for copy in sends:
         copy.wait()
 
@@ -357,9 +354,9 @@
         slot,
     )
     viscous_matrix, _ = lax.optimization_barrier((viscous_matrix, blocks))
-    partial = call(
-        products_kernel,
-        struct((NV, NN, elems), F32),
+    residual, done = call(
+        residual_kernel,
+        (field, struct((8, 128), F32)),
         linear_flux_matrix,
         forcing,
         state,
@@ -367,8 +364,16 @@
         viscous_matrix,
         viscosity,
         flags,
-        scratch=[pltpu.VMEM((NV, 128, elems), F32)],
+        lift_t,
+        jumps,
         smem=(0,),
+        hbm_out=(0,),
+        scratch=[
+            pltpu.VMEM((NV, 128, elems), F32),
+            pltpu.VMEM((NV, NN, elems), F32),
+            pltpu.VMEM((NV, NN, elems), BF),
+            pltpu.SemaphoreType.DMA((NV,)),
+        ],
     )
     blocks = lax.all_to_all(blocks, "gy", 0, 0, tiled=True)
     totals, coarse = call(
@@ -376,11 +381,12 @@
         (struct((48, 128), F32), struct((16, 128), F32)),
         blocks,
         coarse_side,
-        partial,
-        loose=(2,),
+        done,
     )
     up, down = swapped(coarse, 0), swapped(coarse, 1)
-    coarse = call(sweep_kernel, struct((16, 128), F32), up, down, totals, coarse, coarse_side)
+    coarse = call(
+        sweep_kernel, struct((16, 128), F32), up, down, totals, coarse, coarse_side, flops=5 * 10**9
+    )
     up, down = swapped(coarse, 0), swapped(coarse, 1)
     blocks = call(
         last_sweep_kernel,
@@ -391,16 +397,6 @@
         coarse,
         coarse_side,
         scratch=[pltpu.VMEM((16, 128), F32)],
-    )
-    partial, _ = lax.optimization_barrier((partial, blocks))
-    residual = call(
-        residual_kernel,
-        field,
-        partial,
-        jumps,
-        lift_t,
-        hbm_out=(0,),
-        scratch=[pltpu.VMEM((NV, NN, elems), BF), pltpu.SemaphoreType.DMA((NV,))],
     )
     blocks = lax.all_to_all(blocks, "gy", 0, 0, tiled=True)
     correction = call(

time: 73.6 us -> 70.9 us (0.963)
  blocking collectives: 0 us -> 10.6 us
  starting transfers between devices: 48.9 us -> 42.3 us
  waiting for transfers between devices: 10.2 us -> 6.68 us
  local copies, waits for them, and re-layouts: 3.36 us -> 1.2 us
  Pallas kernels: 9.57 us -> 8.74 us
    all_to_all x0 -> x1, blocking collectives: none -> 10.6 us  [per_device(): blocks = lax.all_to_all(blocks, 'gy', 0, 0, tiled=True)]
    all_to_all x2 -> x1, starting transfers between devices: 12.8 us -> 6.18 us  [per_device(): blocks = lax.all_to_all(blocks, 'gy', 0, 0, tiled=True)]
    all_to_all x2 -> x1, waiting for transfers between devices: 5.28 us -> 1.74 us  [per_device(): blocks = lax.all_to_all(blocks, 'gy', 0, 0, tiled=True)]
    unnamed x36 -> x30, local copies, waits for them, and re-layouts: 3.36 us -> 1.2 us
    pallas_call x11 -> x10, Pallas kernels: 9.57 us -> 8.74 us  [call(): pl.pallas_call(kernel, out_shape=outs, in_specs=[SMEM if i in smem else V...]
  transfers between devices with their start and end apart: 10 -> 9, of which waited for: 4 -> 3; matrix products, arithmetic and copies ran while one was open for 0% -> 0% of each run, Pallas kernels for 7% -> 7%
where the time goes in v3:
time: 70.9 us; the launch traced here: 70.4 us
  starting transfers between devices  42.3 us (60%)
  blocking collectives  10.6 us (15%)
  Pallas kernels  8.74 us (12%)
  waiting for transfers between devices  6.68 us (9%)
  local copies, waits for them, and re-layouts  1.2 us (2%)
  between operations  0.96 us (1%)
    ppermute x6, starting transfers between devices, swapped(): lax.ppermute(value, 'gx', [(i, (i + (1 if i % 2 == start else -1)) % size...  25.6 us
    all_to_all x1, blocking collectives, per_device(): blocks = lax.all_to_all(blocks, 'gy', 0, 0, tiled=True)  10.6 us
    ppermute x2, starting transfers between devices, shifted(): lax.ppermute(value, axis, [(i, (i + by) % size) for i in range(size)])  10.6 us
    pallas_call x10, Pallas kernels, call(): pl.pallas_call(kernel, out_shape=outs, in_specs=[SMEM if i in smem else V...  8.74 us
    all_to_all x1, starting transfers between devices, per_device(): blocks = lax.all_to_all(blocks, 'gy', 0, 0, tiled=True)  6.18 us
    ppermute x6, waiting for transfers between devices, swapped(): lax.ppermute(value, 'gx', [(i, (i + (1 if i % 2 == start else -1)) % size...  4.93 us
    all_to_all x1, waiting for transfers between devices, per_device(): blocks = lax.all_to_all(blocks, 'gy', 0, 0, tiled=True)  1.74 us
  transfers between devices with their start and end apart: 9, of which 3 were waited for; matrix products, arithmetic and copies ran while one was open for 0% of the time, Pallas kernels for 7%

profile of v3, /device:TPU:1, one launch (start us, length us, event | category | flops | bytes accessed | tf_op | source)
XLA Modules:
  0.0 70.4 jit_solution(17449190604485865482)
XLA Ops:
  0.6 0.0 copy-start.1
  0.6 1.1 %copy-done.1 = bf16[6,125,512]{2,1,0:T(8,128)(2,1)S(1)} copy-done((bf16[6,125,512]{2,1,0:T(8,128)(2,1)S(1)}, bf16[6,125,512]{2,1,0:T(8,128)(2,1)}, u32[]{:S(2)}) %copy-start.1) | copy-done | bytes 768024
  1.8 0.0 copy-start.3
  1.8 0.0 copy-start.7
  1.8 0.0 copy-start.2
  1.8 0.3 shard_map.149
  2.1 0.0 copy-start.4
  2.1 0.0 copy-start.5
  2.1 0.0 copy-start.6
  2.2 0.0 copy-start.14
  2.2 0.0 copy-start
  2.2 0.0 copy-start.8
  2.2 0.0 copy-start.11
  2.2 0.0 copy-start.12
  2.2 2.6 %collective-permute-start.2 = (bf16[6,32,512]{2,1,0:T(8,128)(2,1)S(1)}, bf16[6,32,512]{2,1,0:T(8,128)(2,1)S(1)}, u32[]{:S(2)}, u32[]{:S(2)}) collective-permute-start(bf16[6,32,512]{2,1,0:T(8,128)(2,1)S(1)} %get-tuple-element.24.o3), channel_id=1, source_target_pairs={{0,1},{1,2},{2,3},{3,4},{4,5},{5,6},{6,7},{7,0},{8,9},{9,10},{10,1... | collective-permute-start | bytes 589832 | tf_op jit(solution)/shard_map/ppermute | solution.py:282
  4.8 7.9 %collective-permute-start.3 = (bf16[6,32,512]{2,1,0:T(8,128)(2,1)S(1)}, bf16[6,32,512]{2,1,0:T(8,128)(2,1)S(1)}, u32[]{:S(2)}, u32[]{:S(2)}) collective-permute-start(bf16[6,32,512]{2,1,0:T(8,128)(2,1)S(1)} %get-tuple-element.25.o2), channel_id=1, source_target_pairs={{0,7},{1,0},{2,1},{3,2},{4,3},{5,4},{6,5},{7,6},{8,15},{9,8},{10,9... | collective-permute-start | bytes 589832 | tf_op jit(solution)/shard_map/ppermute | solution.py:282
  12.8 1.9 %collective-permute-start = (bf16[6,32,256]{2,1,0:T(8,128)(2,1)S(1)}, bf16[6,32,256]{2,1,0:T(8,128)(2,1)S(1)}, u32[]{:S(2)}, u32[]{:S(2)}) collective-permute-start(bf16[6,32,256]{2,1,0:T(8,128)(2,1)S(1)} %get-tuple-element.22.o1), channel_id=1, source_target_pairs={{0,8},{8,0},{16,24},{24,16},{32,40},{40,32},{48,56},{56,48},{64,72... | collective-permute-start | bytes 294920 | tf_op jit(solution)/shard_map/ppermute | solution.py:287
  14.7 9.5 %collective-permute-start.1 = (bf16[6,32,256]{2,1,0:T(8,128)(2,1)S(1)}, bf16[6,32,256]{2,1,0:T(8,128)(2,1)S(1)}, u32[]{:S(2)}, u32[]{:S(2)}) collective-permute-start(bf16[6,32,256]{2,1,0:T(8,128)(2,1)S(1)} %get-tuple-element.23.o0), channel_id=1, source_target_pairs={{0,760},{8,16},{16,8},{24,32},{32,24},{40,48},{48,40},{56,64},{64,... | collective-permute-start | bytes 294920 | tf_op jit(solution)/shard_map/ppermute | solution.py:287
  24.2 0.0 copy-done.3
  24.2 0.0 copy-done.7
  24.3 0.3 shard_map.152.coarse_side
  24.5 0.0 copy-start.9
  24.5 0.0 copy-start.10
  24.5 0.0 copy-done.4
  24.5 0.0 copy-done.5
  24.6 0.0 copy-done.6
  24.6 0.0 copy-done.14
  24.6 0.4 shard_map.150
  24.9 0.0 copy-done.2
  24.9 0.0 copy-done
  25.0 0.0 copy-done.8
  25.0 0.0 copy-done.11
  25.0 0.0 copy-done.12
  25.0 1.3 %shard_map.151 = (bf16[6,96,512]{2,1,0:T(8,128)(2,1)S(1)}, f32[48,512]{1,0:T(8,128)S(1)}) custom-call(f32[6,6]{1,0:T(8,128)S(1)} %copy-done.8, bf16[6,125,512]{2,1,0:T(8,128)(2,1)S(1)} %copy-done, bf16[6,125,512]{2,1,0:T(8,128)(2,1)S(1)} %copy-done.2, f32[1,512]{1,0:T(1,128)S(1)} %bitcast.14, s32[1,512]{1,0:T(1,128)S(1)} %bitcast.16, ...), custom_call_target="tpu_custom_call" | custom-call | flops 1000 | bytes 1000 | tf_op jit(solution)/shard_map/pallas_call | solution.py:48
  26.3 0.0 collective-permute-done.n1
  26.3 0.0 collective-permute-done.1.n0
  26.3 0.0 collective-permute-done.2.n2
  26.3 0.0 collective-permute-done.3.n3
  26.3 0.0 copy-done.9
  26.3 0.0 copy-done.10
  26.3 1.2 %shard_map.153 = (f32[8,16,128]{2,1,0:T(8,128)}, bf16[6,192,512]{2,1,0:T(8,128)(2,1)S(1)}) custom-call(bf16[6,32,256]{2,1,0:T(8,128)(2,1)S(1)} %collective-permute-done.n1, bf16[6,32,256]{2,1,0:T(8,128)(2,1)S(1)} %collective-permute-done.1.n0, bf16[6,32,512]{2,1,0:T(8,128)(2,1)S(1)} %collective-permute-done.2.n2, ...), custom_call_target="tpu_custom_call" | custom-call | flops 1000 | bytes 1000 | tf_op jit(solution)/shard_map/pallas_call | solution.py:48
  27.5 6.2 %all-to-all-start = ((f32[8,16,128]{2,1,0:T(8,128)}), f32[8,16,128]{2,1,0:T(8,128)S(1)}, u32[]{:S(2)}, u32[]{:S(2)}) async-start(f32[8,16,128]{2,1,0:T(8,128)} %get-tuple-element.34), calls=%async_computation | async-start | bytes 131072 | tf_op jit(solution)/shard_map/all_to_all | solution.py:378
  33.7 3.1 %shard_map.154 = (bf16[6,125,512]{2,1,0:T(8,128)(2,1)}, f32[8,128]{1,0:T(8,128)S(1)}) custom-call(f32[6,6]{1,0:T(8,128)S(1)} %copy-done.8, bf16[6,125,512]{2,1,0:T(8,128)(2,1)S(1)} %copy-done, bf16[6,125,512]{2,1,0:T(8,128)(2,1)S(1)} %copy-done.2, bf16[125,125]{1,0:T(8,128)(2,1)S(1)} %copy-done.5, bf16[125,125]{1,0:T(8,128)(2,1)S(1)} %copy-done.6, ...), custom_call_target="tpu_custom_call" | custom-call | flops 1000 | bytes 1000 | tf_op jit(solution)/shard_map/pallas_call | solution.py:48
  36.8 1.7 %all-to-all-done.blocks = f32[8,16,128]{2,1,0:T(8,128)S(1)} async-done(((f32[8,16,128]{2,1,0:T(8,128)}), f32[8,16,128]{2,1,0:T(8,128)S(1)}, u32[]{:S(2)}, u32[]{:S(2)}) %all-to-all-start) | async-done | bytes 65568 | tf_op jit(solution)/shard_map/all_to_all | solution.py:378
  38.6 0.2 shard_map.155
  38.8 7.0 %collective-permute-start.5 = (f32[16,128]{1,0:T(8,128)S(1)}, f32[16,128]{1,0:T(8,128)S(1)}, u32[]{:S(2)}, u32[]{:S(2)}) collective-permute-start(f32[16,128]{1,0:T(8,128)S(1)} %get-tuple-element.40.before), channel_id=1, source_target_pairs={{0,760},{8,16},{16,8},{24,32},{32,24},{40,48},{48,40},{56,64},{64,... | collective-permute-start | bytes 24584 | tf_op jit(solution)/shard_map/ppermute | solution.py:287
  45.8 1.9 %collective-permute-start.4 = (f32[16,128]{1,0:T(8,128)S(1)}, f32[16,128]{1,0:T(8,128)S(1)}, u32[]{:S(2)}, u32[]{:S(2)}) collective-permute-start(f32[16,128]{1,0:T(8,128)S(1)} %get-tuple-element.40.before), channel_id=1, source_target_pairs={{0,8},{8,0},{16,24},{24,16},{32,40},{40,32},{48,56},{56,48},{64,72... | collective-permute-start | bytes 24584 | tf_op jit(solution)/shard_map/ppermute | solution.py:287
  47.7 0.0 collective-permute-done.5.down
  47.7 2.5 %collective-permute-done.4.up = f32[16,128]{1,0:T(8,128)S(1)} collective-permute-done((f32[16,128]{1,0:T(8,128)S(1)}, f32[16,128]{1,0:T(8,128)S(1)}, u32[]{:S(2)}, u32[]{:S(2)}) %collective-permute-start.4) | collective-permute-done | bytes 8224 | tf_op jit(solution)/shard_map/ppermute | solution.py:287
  50.1 0.0 copy-start.13
  50.2 0.3 shard_map.156.before
  50.5 3.3 %collective-permute-start.7 = (f32[16,128]{1,0:T(8,128)S(1)}, f32[16,128]{1,0:T(8,128)S(1)}, u32[]{:S(2)}, u32[]{:S(2)}) collective-permute-start(f32[16,128]{1,0:T(8,128)S(1)} %shard_map.156.before), channel_id=1, source_target_pairs={{0,760},{8,16},{16,8},{24,32},{32,24},{40,48},{48,40},{56,64},{64,... | collective-permute-start | bytes 24584 | tf_op jit(solution)/shard_map/ppermute | solution.py:287
  53.8 1.9 %collective-permute-start.6 = (f32[16,128]{1,0:T(8,128)S(1)}, f32[16,128]{1,0:T(8,128)S(1)}, u32[]{:S(2)}, u32[]{:S(2)}) collective-permute-start(f32[16,128]{1,0:T(8,128)S(1)} %shard_map.156.before), channel_id=1, source_target_pairs={{0,8},{8,0},{16,24},{24,16},{32,40},{40,32},{48,56},{56,48},{64,72... | collective-permute-start | bytes 24584 | tf_op jit(solution)/shard_map/ppermute | solution.py:287
  55.7 2.5 %collective-permute-done.7.down = f32[16,128]{1,0:T(8,128)S(1)} collective-permute-done((f32[16,128]{1,0:T(8,128)S(1)}, f32[16,128]{1,0:T(8,128)S(1)}, u32[]{:S(2)}, u32[]{:S(2)}) %collective-permute-start.7) | collective-permute-done | bytes 8224 | tf_op jit(solution)/shard_map/ppermute | solution.py:287
  58.2 0.0 collective-permute-done.6.up
  58.2 0.3 shard_map.157
  58.6 10.6 %all_to_all.10.blocks = f32[8,16,128]{2,1,0:T(8,128)S(1)} all-to-all(f32[8,16,128]{2,1,0:T(8,128)S(1)} %shard_map.157), channel_id=1, replica_groups=mesh['gx'=96,'gy'=8] {'gy'}, dimensions={0} | all-to-all | bytes 131072 | tf_op jit(solution)/shard_map/all_to_all | solution.py:401
  69.1 0.0 copy-done.13
  69.1 1.3 %shard_map.158 = bf16[6,125,512]{2,1,0:T(8,128)(2,1)} custom-call(f32[8,16,128]{2,1,0:T(8,128)S(1)} %all_to_all.10.blocks, f32[8,125]{1,0:T(8,128)S(1)} %bitcast.18, s32[1,512]{1,0:T(1,128)S(1)} %bitcast.11, s32[1,512]{1,0:T(1,128)S(1)} %bitcast.13), custom_call_target="tpu_custom_call" | custom-call | flops 1000 | bytes 1000 | tf_op jit(solution)/shard_map/pallas_call | solution.py:48
Async XLA Ops:
  0.6 1.1 %copy-start.1 = (bf16[6,125,512]{2,1,0:T(8,128)(2,1)S(1)}, bf16[6,125,512]{2,1,0:T(8,128)(2,1)}, u32[]{:S(2)}) copy-start(bf16[6,125,512]{2,1,0:T(8,128)(2,1)} %state.5) | copy-start | bytes 2304004
  1.8 22.5 %copy-start.3 = (f32[48,48,32]{1,2,0:T(8,128)S(1)}, f32[48,48,32]{1,2,0:T(8,128)}, u32[]{:S(2)}) copy-start(f32[48,48,32]{1,2,0:T(8,128)} %param.25) | copy-start | bytes 884740
  1.8 22.5 %copy-start.7 = (f32[48,48]{1,0:T(8,128)S(1)}, f32[48,48]{1,0:T(8,128)}, u32[]{:S(2)}) copy-start(f32[48,48]{1,0:T(8,128)} %coupling.1) | copy-start | bytes 27652
  1.8 23.2 %copy-start.2 = (bf16[6,125,512]{2,1,0:T(8,128)(2,1)S(1)}, bf16[6,125,512]{2,1,0:T(8,128)(2,1)}, u32[]{:S(2)}) copy-start(bf16[6,125,512]{2,1,0:T(8,128)(2,1)} %state.5) | copy-start | bytes 2304004
  2.1 22.4 %copy-start.4 = (bf16[6,125,25]{1,2,0:T(8,128)(2,1)S(1)}, bf16[6,125,25]{1,2,0:T(8,128)(2,1)}, u32[]{:S(2)}) copy-start(bf16[6,125,25]{1,2,0:T(8,128)(2,1)} %param.20) | copy-start | bytes 112504
  2.1 22.4 %copy-start.5 = (bf16[125,125]{1,0:T(8,128)(2,1)S(1)}, bf16[125,125]{1,0:T(8,128)(2,1)}, u32[]{:S(2)}) copy-start(bf16[125,125]{1,0:T(8,128)(2,1)} %volume.3) | copy-start | bytes 93754
  2.1 22.4 %copy-start.6 = (bf16[125,125]{1,0:T(8,128)(2,1)S(1)}, bf16[125,125]{1,0:T(8,128)(2,1)}, u32[]{:S(2)}) copy-start(bf16[125,125]{1,0:T(8,128)(2,1)} %viscous.2) | copy-start | bytes 93754
  2.2 22.4 %copy-start.14 = (f32[8,125]{1,0:T(8,128)S(1)}, f32[8,125]{1,0:T(8,128)}, u32[]{:S(2)}) copy-start(f32[8,125]{1,0:T(8,128)} %restrict) | copy-start | bytes 12004
  2.2 22.8 %copy-start = (bf16[6,125,512]{2,1,0:T(8,128)(2,1)S(1)}, bf16[6,125,512]{2,1,0:T(8,128)(2,1)}, u32[]{:S(2)}) copy-start(bf16[6,125,512]{2,1,0:T(8,128)(2,1)} %forcing.3) | copy-start | bytes 2304004
  2.2 22.8 %copy-start.8 = (f32[6,6]{1,0:T(8,128)S(1)}, f32[6,6]{1,0:T(8,128)}, u32[]{:S(2)}) copy-start(f32[6,6]{1,0:T(8,128)} %mix.3) | copy-start | bytes 436
  2.2 22.8 %copy-start.11 = (f32[512]{0:T(512)S(1)}, f32[512]{0:T(512)}, u32[]{:S(2)}) copy-start(f32[512]{0:T(512)} %param.19) | copy-start | bytes 6148
  2.2 22.8 %copy-start.12 = (s32[512]{0:T(512)S(1)}, s32[512]{0:T(512)}, u32[]{:S(2)}) copy-start(s32[512]{0:T(512)} %param.21) | copy-start | bytes 6148
  2.2 24.1 %collective-permute-start.2 = (bf16[6,32,512]{2,1,0:T(8,128)(2,1)S(1)}, bf16[6,32,512]{2,1,0:T(8,128)(2,1)S(1)}, u32[]{:S(2)}, u32[]{:S(2)}) collective-permute-start(bf16[6,32,512]{2,1,0:T(8,128)(2,1)S(1)} %get-tuple-element.24.o3), channel_id=1, source_target_pairs={{0,1},{1,2},{2,3},{3,4},{4,5},{5,6},{6,7},{7,0},{8,9},{9,10},{10,1... | collective-permute-start | bytes 589832 | tf_op jit(solution)/shard_map/ppermute | solution.py:282
  4.8 21.5 %collective-permute-start.3 = (bf16[6,32,512]{2,1,0:T(8,128)(2,1)S(1)}, bf16[6,32,512]{2,1,0:T(8,128)(2,1)S(1)}, u32[]{:S(2)}, u32[]{:S(2)}) collective-permute-start(bf16[6,32,512]{2,1,0:T(8,128)(2,1)S(1)} %get-tuple-element.25.o2), channel_id=1, source_target_pairs={{0,7},{1,0},{2,1},{3,2},{4,3},{5,4},{6,5},{7,6},{8,15},{9,8},{10,9... | collective-permute-start | bytes 589832 | tf_op jit(solution)/shard_map/ppermute | solution.py:282
  12.8 13.5 %collective-permute-start = (bf16[6,32,256]{2,1,0:T(8,128)(2,1)S(1)}, bf16[6,32,256]{2,1,0:T(8,128)(2,1)S(1)}, u32[]{:S(2)}, u32[]{:S(2)}) collective-permute-start(bf16[6,32,256]{2,1,0:T(8,128)(2,1)S(1)} %get-tuple-element.22.o1), channel_id=1, source_target_pairs={{0,8},{8,0},{16,24},{24,16},{32,40},{40,32},{48,56},{56,48},{64,72... | collective-permute-start | bytes 294920 | tf_op jit(solution)/shard_map/ppermute | solution.py:287
  14.7 11.6 %collective-permute-start.1 = (bf16[6,32,256]{2,1,0:T(8,128)(2,1)S(1)}, bf16[6,32,256]{2,1,0:T(8,128)(2,1)S(1)}, u32[]{:S(2)}, u32[]{:S(2)}) collective-permute-start(bf16[6,32,256]{2,1,0:T(8,128)(2,1)S(1)} %get-tuple-element.23.o0), channel_id=1, source_target_pairs={{0,760},{8,16},{16,8},{24,32},{32,24},{40,48},{48,40},{56,64},{64,... | collective-permute-start | bytes 294920 | tf_op jit(solution)/shard_map/ppermute | solution.py:287
  24.5 1.8 %copy-start.9 = (s32[512,1]{0,1:T(1,128)S(1)}, s32[512,1]{0,1:T(1,128)}, u32[]{:S(2)}) copy-start(s32[512,1]{0,1:T(1,128)} %param.23) | copy-start | bytes 6148
  24.5 1.8 %copy-start.10 = (s32[512]{0:T(512)S(1)}, s32[512]{0:T(512)}, u32[]{:S(2)}) copy-start(s32[512]{0:T(512)} %param.24) | copy-start | bytes 6148
  27.5 11.0 %all-to-all-start = ((f32[8,16,128]{2,1,0:T(8,128)}), f32[8,16,128]{2,1,0:T(8,128)S(1)}, u32[]{:S(2)}, u32[]{:S(2)}) async-start(f32[8,16,128]{2,1,0:T(8,128)} %get-tuple-element.34), calls=%async_computation | async-start | bytes 131072 | tf_op jit(solution)/shard_map/all_to_all | solution.py:378
  38.8 8.9 %collective-permute-start.5 = (f32[16,128]{1,0:T(8,128)S(1)}, f32[16,128]{1,0:T(8,128)S(1)}, u32[]{:S(2)}, u32[]{:S(2)}) collective-permute-start(f32[16,128]{1,0:T(8,128)S(1)} %get-tuple-element.40.before), channel_id=1, source_target_pairs={{0,760},{8,16},{16,8},{24,32},{32,24},{40,48},{48,40},{56,64},{64,... | collective-permute-start | bytes 24584 | tf_op jit(solution)/shard_map/ppermute | solution.py:287
  45.8 4.4 %collective-permute-start.4 = (f32[16,128]{1,0:T(8,128)S(1)}, f32[16,128]{1,0:T(8,128)S(1)}, u32[]{:S(2)}, u32[]{:S(2)}) collective-permute-start(f32[16,128]{1,0:T(8,128)S(1)} %get-tuple-element.40.before), channel_id=1, source_target_pairs={{0,8},{8,0},{16,24},{24,16},{32,40},{40,32},{48,56},{56,48},{64,72... | collective-permute-start | bytes 24584 | tf_op jit(solution)/shard_map/ppermute | solution.py:287
  50.1 19.0 %copy-start.13 = (f32[125,8]{0,1:T(8,128)S(1)}, f32[125,8]{0,1:T(8,128)}, u32[]{:S(2)}) copy-start(f32[125,8]{0,1:T(8,128)} %param.27) | copy-start | bytes 12004
  50.5 7.7 %collective-permute-start.7 = (f32[16,128]{1,0:T(8,128)S(1)}, f32[16,128]{1,0:T(8,128)S(1)}, u32[]{:S(2)}, u32[]{:S(2)}) collective-permute-start(f32[16,128]{1,0:T(8,128)S(1)} %shard_map.156.before), channel_id=1, source_target_pairs={{0,760},{8,16},{16,8},{24,32},{32,24},{40,48},{48,40},{56,64},{64,... | collective-permute-start | bytes 24584 | tf_op jit(solution)/shard_map/ppermute | solution.py:287
  53.8 4.4 %collective-permute-start.6 = (f32[16,128]{1,0:T(8,128)S(1)}, f32[16,128]{1,0:T(8,128)S(1)}, u32[]{:S(2)}, u32[]{:S(2)}) collective-permute-start(f32[16,128]{1,0:T(8,128)S(1)} %shard_map.156.before), channel_id=1, source_target_pairs={{0,8},{8,0},{16,24},{24,16},{32,40},{40,32},{48,56},{56,48},{64,72... | collective-permute-start | bytes 24584 | tf_op jit(solution)/shard_map/ppermute | solution.py:287

commit v4 on v3

--- a/solution.py
+++ b/solution.py
@@ -136,9 +136,7 @@
         restricted[8 * q : 8 * q + 8] = total
 
 
-def residual_kernel(
-    mix, forcing, state, volume, viscous, viscosity, flags, lift_t, jumps, residual, done, flux, local, out, sems
-):
+def products_kernel(forcing, state, volume, viscous, viscosity, flags, lift_t, jumps, flux, local, done):
     lifts = transposed_lifts(lift_t)
     for v in range(NV):
         u = state[v]
@@ -147,6 +145,10 @@
         if v == NV - 1:
             total = total - (WALL * flags[...].astype(F32)) * u.astype(F32)
         local[v] = total
+    done[...] = jnp.zeros_like(done)
+
+
+def mixed_kernel(mix, flux, local, residual, done, out, sems):
     sends = []
     for q in range(NV):
         for low in range(0, NN, 16):
@@ -223,14 +225,14 @@
         out[r : r + 1] = jnp.sum(coarse_side[r] * source, axis=0, keepdims=True)
 
 
-def first_kernel(blocks, coarse_side, _, totals, coarse):
+def first_kernel(blocks, coarse_side, totals, coarse):
     packed = jnp.sum(blocks[...], axis=0)
     source = opened(packed)
     totals[...] = source
     solve(coarse_side, source, coarse)
 
 
-def sweep_kernel(up, down, totals, before, coarse_side, coarse):
+def sweep_kernel(up, down, totals, before, coarse_side, _, coarse):
     beside = opened(up[...] + down[...])
     coupling = coarse_side[16][:, : beside.shape[0]]
     source = totals[...] - dot(coupling, beside, precision=TOP)
@@ -238,8 +240,8 @@
     coarse[...] = (1.0 - RELAX) * before[...] + coarse[...]
 
 
-def last_sweep_kernel(up, down, totals, before, coarse_side, blocks, scratch):
-    sweep_kernel(up, down, totals, before, coarse_side, scratch)
+def last_sweep_kernel(up, down, totals, before, coarse_side, _, blocks, scratch):
+    sweep_kernel(up, down, totals, before, coarse_side, _, scratch)
     for m in range(MEMBERS):
         blocks[m] = scratch[...]
 
@@ -353,49 +355,49 @@
         owner,
         slot,
     )
-    viscous_matrix, _ = lax.optimization_barrier((viscous_matrix, blocks))
-    residual, done = call(
-        residual_kernel,
-        (field, struct((8, 128), F32)),
-        linear_flux_matrix,
+    blocks = lax.all_to_all(blocks, "gy", 0, 0, tiled=True)
+    totals, coarse = call(
+        first_kernel, (struct((48, 128), F32), struct((16, 128), F32)), blocks, coarse_side
+    )
+    far_c, near_c = swapped(coarse, 1), swapped(coarse, 0)
+    mark = struct((8, 128), F32)
+    lift_after, _ = lax.optimization_barrier((lift_t, coarse))
+    flux, local, done = call(
+        products_kernel,
+        (struct((NV, 128, elems), F32), struct((NV, NN, elems), F32), mark),
         forcing,
         state,
         volume_flux_matrix,
         viscous_matrix,
         viscosity,
         flags,
-        lift_t,
+        lift_after,
         jumps,
+    )
+    coarse = call(
+        sweep_kernel, struct((16, 128), F32), far_c, near_c, totals, coarse, coarse_side, done
+    )
+    far_c, near_c = swapped(coarse, 1), swapped(coarse, 0)
+    local, _ = lax.optimization_barrier((local, coarse))
+    residual, done = call(
+        mixed_kernel,
+        (field, mark),
+        linear_flux_matrix,
+        flux,
+        local,
         smem=(0,),
         hbm_out=(0,),
-        scratch=[
-            pltpu.VMEM((NV, 128, elems), F32),
-            pltpu.VMEM((NV, NN, elems), F32),
-            pltpu.VMEM((NV, NN, elems), BF),
-            pltpu.SemaphoreType.DMA((NV,)),
-        ],
-    )
-    blocks = lax.all_to_all(blocks, "gy", 0, 0, tiled=True)
-    totals, coarse = call(
-        first_kernel,
-        (struct((48, 128), F32), struct((16, 128), F32)),
-        blocks,
-        coarse_side,
-        done,
-    )
-    up, down = swapped(coarse, 0), swapped(coarse, 1)
-    coarse = call(
-        sweep_kernel, struct((16, 128), F32), up, down, totals, coarse, coarse_side, flops=5 * 10**9
-    )
-    up, down = swapped(coarse, 0), swapped(coarse, 1)
+        scratch=[pltpu.VMEM((NV, NN, elems), BF), pltpu.SemaphoreType.DMA((NV,))],
+    )
     blocks = call(
         last_sweep_kernel,
         struct((MEMBERS, 16, 128), F32),
-        up,
-        down,
+        far_c,
+        near_c,
         totals,
         coarse,
         coarse_side,
+        done,
         scratch=[pltpu.VMEM((16, 128), F32)],
     )
     blocks = lax.all_to_all(blocks, "gy", 0, 0, tiled=True)

time: 70.9 us -> 69.4 us (0.979)
  blocking collectives: 10.6 us -> 21 us
  starting transfers between devices: 42.3 us -> 36.1 us
  waiting for transfers between devices: 6.68 us -> 1.93 us
  Pallas kernels: 8.74 us -> 7.94 us
    all_to_all x1 -> x2, blocking collectives: 10.6 us -> 21 us  [per_device(): blocks = lax.all_to_all(blocks, 'gy', 0, 0, tiled=True)]
    all_to_all x1 -> x0, starting transfers between devices: 6.18 us -> none  [per_device(): blocks = lax.all_to_all(blocks, 'gy', 0, 0, tiled=True)]
    ppermute x6, waiting for transfers between devices: 4.93 us -> 1.92 us  [swapped(): lax.ppermute(value, 'gx', [(i, (i + (1 if i % 2 == start else -1)) % size...]
    all_to_all x1 -> x0, waiting for transfers between devices: 1.74 us -> none  [per_device(): blocks = lax.all_to_all(blocks, 'gy', 0, 0, tiled=True)]
    pallas_call x10 -> x11, Pallas kernels: 8.74 us -> 7.94 us  [call(): pl.pallas_call(kernel, out_shape=outs, in_specs=[SMEM if i in smem else V...]
  transfers between devices with their start and end apart: 9 -> 8, of which waited for: 3 -> 2; matrix products, arithmetic and copies ran while one was open for 0% -> 0% of each run, Pallas kernels for 7% -> 7%
where the time goes in v4:
time: 69.4 us; the launch traced here: 69.1 us
  starting transfers between devices  36.1 us (52%)
  blocking collectives  21 us (30%)
  Pallas kernels  7.94 us (11%)
  waiting for transfers between devices  1.93 us (3%)
  local copies, waits for them, and re-layouts  1.19 us (2%)
  between operations  0.98 us (1%)
    ppermute x6, starting transfers between devices, swapped(): lax.ppermute(value, 'gx', [(i, (i + (1 if i % 2 == start else -1)) % size...  25.5 us
    all_to_all x2, blocking collectives, per_device(): blocks = lax.all_to_all(blocks, 'gy', 0, 0, tiled=True)  21 us
    ppermute x2, starting transfers between devices, shifted(): lax.ppermute(value, axis, [(i, (i + by) % size) for i in range(size)])  10.5 us
    pallas_call x11, Pallas kernels, call(): pl.pallas_call(kernel, out_shape=outs, in_specs=[SMEM if i in smem else V...  7.94 us
    ppermute x6, waiting for transfers between devices, swapped(): lax.ppermute(value, 'gx', [(i, (i + (1 if i % 2 == start else -1)) % size...  1.92 us
  transfers between devices with their start and end apart: 8, of which 2 were waited for; matrix products, arithmetic and copies ran while one was open for 0% of the time, Pallas kernels for 7%

profile of v4, /device:TPU:1, one launch (start us, length us, event | category | flops | bytes accessed | tf_op | source)
XLA Modules:
  0.0 69.1 jit_solution(15608129368726698638)
XLA Ops:
  0.6 0.0 copy-start.1
  0.6 1.1 %copy-done.1 = bf16[6,125,512]{2,1,0:T(8,128)(2,1)S(1)} copy-done((bf16[6,125,512]{2,1,0:T(8,128)(2,1)S(1)}, bf16[6,125,512]{2,1,0:T(8,128)(2,1)}, u32[]{:S(2)}) %copy-start.1) | copy-done | bytes 768024
  1.8 0.0 copy-start.3
  1.8 0.0 copy-start.7
  1.8 0.0 copy-start.4
  1.8 0.0 copy-start.5
  1.8 0.0 copy-start.6
  1.8 0.0 copy-start.14
  1.8 0.0 copy-start.2
  1.8 0.0 copy-start.8
  1.8 0.0 copy-start.11
  1.8 0.0 copy-start.12
  1.8 0.3 shard_map.149
  2.2 0.0 copy-start
  2.2 0.0 copy-start.9
  2.2 0.0 copy-start.10
  2.2 10.5 %collective-permute-start.3 = (bf16[6,32,512]{2,1,0:T(8,128)(2,1)S(1)}, bf16[6,32,512]{2,1,0:T(8,128)(2,1)S(1)}, u32[]{:S(2)}, u32[]{:S(2)}) collective-permute-start(bf16[6,32,512]{2,1,0:T(8,128)(2,1)S(1)} %get-tuple-element.29.o2), channel_id=1, source_target_pairs={{0,7},{1,0},{2,1},{3,2},{4,3},{5,4},{6,5},{7,6},{8,15},{9,8},{10,9... | collective-permute-start | bytes 589832 | tf_op jit(solution)/shard_map/ppermute | solution.py:284
  12.8 0.0 collective-permute-start.2
  12.8 1.9 %collective-permute-start = (bf16[6,32,256]{2,1,0:T(8,128)(2,1)S(1)}, bf16[6,32,256]{2,1,0:T(8,128)(2,1)S(1)}, u32[]{:S(2)}, u32[]{:S(2)}) collective-permute-start(bf16[6,32,256]{2,1,0:T(8,128)(2,1)S(1)} %get-tuple-element.26.o1), channel_id=1, source_target_pairs={{0,8},{8,0},{16,24},{24,16},{32,40},{40,32},{48,56},{56,48},{64,72... | collective-permute-start | bytes 294920 | tf_op jit(solution)/shard_map/ppermute | solution.py:289
  14.7 9.6 %collective-permute-start.1 = (bf16[6,32,256]{2,1,0:T(8,128)(2,1)S(1)}, bf16[6,32,256]{2,1,0:T(8,128)(2,1)S(1)}, u32[]{:S(2)}, u32[]{:S(2)}) collective-permute-start(bf16[6,32,256]{2,1,0:T(8,128)(2,1)S(1)} %get-tuple-element.27.o0), channel_id=1, source_target_pairs={{0,760},{8,16},{16,8},{24,32},{32,24},{40,48},{48,40},{56,64},{64,... | collective-permute-start | bytes 294920 | tf_op jit(solution)/shard_map/ppermute | solution.py:289
  24.3 0.0 copy-done.3
  24.3 0.0 copy-done.7
  24.3 0.3 shard_map.152.coarse_side
  24.5 0.0 copy-done.4
  24.6 0.0 copy-done.5
  24.6 0.0 copy-done.6
  24.6 0.0 copy-done.14
  24.6 0.4 shard_map.150
  24.9 0.0 copy-done.2
  25.0 0.0 copy-done.8
  25.0 0.0 copy-done.11
  25.0 0.0 copy-done.12
  25.0 0.0 copy-done
  25.0 1.3 %shard_map.151 = (bf16[6,96,512]{2,1,0:T(8,128)(2,1)S(1)}, f32[48,512]{1,0:T(8,128)S(1)}) custom-call(f32[6,6]{1,0:T(8,128)S(1)} %copy-done.8, bf16[6,125,512]{2,1,0:T(8,128)(2,1)S(1)} %copy-done, bf16[6,125,512]{2,1,0:T(8,128)(2,1)S(1)} %copy-done.2, f32[1,512]{1,0:T(1,128)S(1)} %bitcast.14, s32[1,512]{1,0:T(1,128)S(1)} %bitcast.16, ...), custom_call_target="tpu_custom_call" | custom-call | flops 1000 | bytes 1000 | tf_op jit(solution)/shard_map/pallas_call | solution.py:48
  26.3 0.0 collective-permute-done.n1
  26.3 0.0 collective-permute-done.1.n0
  26.3 0.0 collective-permute-done.3.n3
  26.3 0.0 collective-permute-done.2.n2
  26.3 0.0 copy-done.9
  26.3 0.0 copy-done.10
  26.3 0.6 shard_map.153
  26.9 10.4 %all_to_all.10.blocks = f32[8,16,128]{2,1,0:T(8,128)S(1)} all-to-all(f32[8,16,128]{2,1,0:T(8,128)S(1)} %get-tuple-element.38), channel_id=1, replica_groups=mesh['gx'=96,'gy'=8] {'gy'}, dimensions={0} | all-to-all | bytes 131072 | tf_op jit(solution)/shard_map/all_to_all | solution.py:358
  37.3 0.2 shard_map.154
  37.5 6.9 %collective-permute-start.4 = (f32[16,128]{1,0:T(8,128)S(1)}, f32[16,128]{1,0:T(8,128)S(1)}, u32[]{:S(2)}, u32[]{:S(2)}) collective-permute-start(f32[16,128]{1,0:T(8,128)S(1)} %get-tuple-element.40.before), channel_id=1, source_target_pairs={{0,760},{8,16},{16,8},{24,32},{32,24},{40,48},{48,40},{56,64},{64,... | collective-permute-start | bytes 24584 | tf_op jit(solution)/shard_map/ppermute | solution.py:289
  44.4 1.9 %collective-permute-start.5 = (f32[16,128]{1,0:T(8,128)S(1)}, f32[16,128]{1,0:T(8,128)S(1)}, u32[]{:S(2)}, u32[]{:S(2)}) collective-permute-start(f32[16,128]{1,0:T(8,128)S(1)} %get-tuple-element.40.before), channel_id=1, source_target_pairs={{0,8},{8,0},{16,24},{24,16},{32,40},{40,32},{48,56},{56,48},{64,72... | collective-permute-start | bytes 24584 | tf_op jit(solution)/shard_map/ppermute | solution.py:289
  46.3 0.9 %shard_map.155 = (f32[6,128,512]{2,1,0:T(8,128)S(1)}, f32[6,125,512]{2,1,0:T(8,128)S(1)}, f32[8,128]{1,0:T(8,128)S(1)}) custom-call(bf16[6,125,512]{2,1,0:T(8,128)(2,1)S(1)} %copy-done, bf16[6,125,512]{2,1,0:T(8,128)(2,1)S(1)} %copy-done.2, bf16[125,125]{1,0:T(8,128)(2,1)S(1)} %copy-done.5, bf16[125,125]{1,0:T(8,128)(2,1)S(1)} %copy-done.6, ...), custom_call_target="tpu_custom_call" | custom-call | flops 1000 | bytes 1000 | tf_op jit(solution)/shard_map/pallas_call | solution.py:48
  47.2 0.0 collective-permute-done.4.up
  47.3 1.5 %collective-permute-done.5.down = f32[16,128]{1,0:T(8,128)S(1)} collective-permute-done((f32[16,128]{1,0:T(8,128)S(1)}, f32[16,128]{1,0:T(8,128)S(1)}, u32[]{:S(2)}, u32[]{:S(2)}) %collective-permute-start.5) | collective-permute-done | bytes 8224 | tf_op jit(solution)/shard_map/ppermute | solution.py:289
  48.8 0.3 shard_map.156.before
  49.1 3.3 %collective-permute-start.6 = (f32[16,128]{1,0:T(8,128)S(1)}, f32[16,128]{1,0:T(8,128)S(1)}, u32[]{:S(2)}, u32[]{:S(2)}) collective-permute-start(f32[16,128]{1,0:T(8,128)S(1)} %shard_map.156.before), channel_id=1, source_target_pairs={{0,760},{8,16},{16,8},{24,32},{32,24},{40,48},{48,40},{56,64},{64,... | collective-permute-start | bytes 24584 | tf_op jit(solution)/shard_map/ppermute | solution.py:289
  52.4 1.9 %collective-permute-start.7 = (f32[16,128]{1,0:T(8,128)S(1)}, f32[16,128]{1,0:T(8,128)S(1)}, u32[]{:S(2)}, u32[]{:S(2)}) collective-permute-start(f32[16,128]{1,0:T(8,128)S(1)} %shard_map.156.before), channel_id=1, source_target_pairs={{0,8},{8,0},{16,24},{24,16},{32,40},{40,32},{48,56},{56,48},{64,72... | collective-permute-start | bytes 24584 | tf_op jit(solution)/shard_map/ppermute | solution.py:289
  54.4 0.0 copy-start.13
  54.4 2.0 %shard_map.157 = (bf16[6,125,512]{2,1,0:T(8,128)(2,1)}, f32[8,128]{1,0:T(8,128)S(1)}) custom-call(f32[6,6]{1,0:T(8,128)S(1)} %copy-done.8, f32[6,128,512]{2,1,0:T(8,128)S(1)} %get-tuple-element.43.flux, f32[6,125,512]{2,1,0:T(8,128)S(1)} %get-tuple-element.47.local), custom_call_target="tpu_custom_call" | custom-call | flops 1000 | bytes 1000 | tf_op jit(solution)/shard_map/pallas_call | solution.py:48
  56.4 0.4 collective-permute-done.6.up
  56.8 0.0 collective-permute-done.7.down
  56.8 0.3 shard_map.158
  57.2 10.6 %all_to_all.11.blocks = f32[8,16,128]{2,1,0:T(8,128)S(1)} all-to-all(f32[8,16,128]{2,1,0:T(8,128)S(1)} %shard_map.158), channel_id=1, replica_groups=mesh['gx'=96,'gy'=8] {'gy'}, dimensions={0} | all-to-all | bytes 131072 | tf_op jit(solution)/shard_map/all_to_all | solution.py:403
  67.7 0.0 copy-done.13
  67.7 1.3 %shard_map.159 = bf16[6,125,512]{2,1,0:T(8,128)(2,1)} custom-call(f32[8,16,128]{2,1,0:T(8,128)S(1)} %all_to_all.11.blocks, f32[8,125]{1,0:T(8,128)S(1)} %bitcast.18, s32[1,512]{1,0:T(1,128)S(1)} %bitcast.11, s32[1,512]{1,0:T(1,128)S(1)} %bitcast.13), custom_call_target="tpu_custom_call" | custom-call | flops 1000 | bytes 1000 | tf_op jit(solution)/shard_map/pallas_call | solution.py:48
Async XLA Ops:
  0.6 1.1 %copy-start.1 = (bf16[6,125,512]{2,1,0:T(8,128)(2,1)S(1)}, bf16[6,125,512]{2,1,0:T(8,128)(2,1)}, u32[]{:S(2)}) copy-start(bf16[6,125,512]{2,1,0:T(8,128)(2,1)} %state.5) | copy-start | bytes 2304004
  1.8 22.5 %copy-start.3 = (f32[48,48,32]{1,2,0:T(8,128)S(1)}, f32[48,48,32]{1,2,0:T(8,128)}, u32[]{:S(2)}) copy-start(f32[48,48,32]{1,2,0:T(8,128)} %param.25) | copy-start | bytes 884740
  1.8 22.5 %copy-start.7 = (f32[48,48]{1,0:T(8,128)S(1)}, f32[48,48]{1,0:T(8,128)}, u32[]{:S(2)}) copy-start(f32[48,48]{1,0:T(8,128)} %coupling.1) | copy-start | bytes 27652
  1.8 22.8 %copy-start.4 = (bf16[6,125,25]{1,2,0:T(8,128)(2,1)S(1)}, bf16[6,125,25]{1,2,0:T(8,128)(2,1)}, u32[]{:S(2)}) copy-start(bf16[6,125,25]{1,2,0:T(8,128)(2,1)} %param.20) | copy-start | bytes 112504
  1.8 22.8 %copy-start.5 = (bf16[125,125]{1,0:T(8,128)(2,1)S(1)}, bf16[125,125]{1,0:T(8,128)(2,1)}, u32[]{:S(2)}) copy-start(bf16[125,125]{1,0:T(8,128)(2,1)} %volume.3) | copy-start | bytes 93754
  1.8 22.8 %copy-start.6 = (bf16[125,125]{1,0:T(8,128)(2,1)S(1)}, bf16[125,125]{1,0:T(8,128)(2,1)}, u32[]{:S(2)}) copy-start(bf16[125,125]{1,0:T(8,128)(2,1)} %viscous.3) | copy-start | bytes 93754
  1.8 22.8 %copy-start.14 = (f32[8,125]{1,0:T(8,128)S(1)}, f32[8,125]{1,0:T(8,128)}, u32[]{:S(2)}) copy-start(f32[8,125]{1,0:T(8,128)} %restrict) | copy-start | bytes 12004
  1.8 23.2 %copy-start.2 = (bf16[6,125,512]{2,1,0:T(8,128)(2,1)S(1)}, bf16[6,125,512]{2,1,0:T(8,128)(2,1)}, u32[]{:S(2)}) copy-start(bf16[6,125,512]{2,1,0:T(8,128)(2,1)} %state.5) | copy-start | bytes 2304004
  1.8 23.2 %copy-start.8 = (f32[6,6]{1,0:T(8,128)S(1)}, f32[6,6]{1,0:T(8,128)}, u32[]{:S(2)}) copy-start(f32[6,6]{1,0:T(8,128)} %mix.3) | copy-start | bytes 436
  1.8 23.2 %copy-start.11 = (f32[512]{0:T(512)S(1)}, f32[512]{0:T(512)}, u32[]{:S(2)}) copy-start(f32[512]{0:T(512)} %param.19) | copy-start | bytes 6148
  1.8 23.2 %copy-start.12 = (s32[512]{0:T(512)S(1)}, s32[512]{0:T(512)}, u32[]{:S(2)}) copy-start(s32[512]{0:T(512)} %param.21) | copy-start | bytes 6148
  2.2 22.8 %copy-start = (bf16[6,125,512]{2,1,0:T(8,128)(2,1)S(1)}, bf16[6,125,512]{2,1,0:T(8,128)(2,1)}, u32[]{:S(2)}) copy-start(bf16[6,125,512]{2,1,0:T(8,128)(2,1)} %forcing.3) | copy-start | bytes 2304004
  2.2 24.1 %copy-start.9 = (s32[512,1]{0,1:T(1,128)S(1)}, s32[512,1]{0,1:T(1,128)}, u32[]{:S(2)}) copy-start(s32[512,1]{0,1:T(1,128)} %param.23) | copy-start | bytes 6148
  2.2 24.1 %copy-start.10 = (s32[512]{0:T(512)S(1)}, s32[512]{0:T(512)}, u32[]{:S(2)}) copy-start(s32[512]{0:T(512)} %param.24) | copy-start | bytes 6148
  2.2 24.1 %collective-permute-start.3 = (bf16[6,32,512]{2,1,0:T(8,128)(2,1)S(1)}, bf16[6,32,512]{2,1,0:T(8,128)(2,1)S(1)}, u32[]{:S(2)}, u32[]{:S(2)}) collective-permute-start(bf16[6,32,512]{2,1,0:T(8,128)(2,1)S(1)} %get-tuple-element.29.o2), channel_id=1, source_target_pairs={{0,7},{1,0},{2,1},{3,2},{4,3},{5,4},{6,5},{7,6},{8,15},{9,8},{10,9... | collective-permute-start | bytes 589832 | tf_op jit(solution)/shard_map/ppermute | solution.py:284
  12.8 13.5 %collective-permute-start.2 = (bf16[6,32,512]{2,1,0:T(8,128)(2,1)S(1)}, bf16[6,32,512]{2,1,0:T(8,128)(2,1)S(1)}, u32[]{:S(2)}, u32[]{:S(2)}) collective-permute-start(bf16[6,32,512]{2,1,0:T(8,128)(2,1)S(1)} %get-tuple-element.28.o3), channel_id=1, source_target_pairs={{0,1},{1,2},{2,3},{3,4},{4,5},{5,6},{6,7},{7,0},{8,9},{9,10},{10,1... | collective-permute-start | bytes 589832 | tf_op jit(solution)/shard_map/ppermute | solution.py:284
  12.8 13.5 %collective-permute-start = (bf16[6,32,256]{2,1,0:T(8,128)(2,1)S(1)}, bf16[6,32,256]{2,1,0:T(8,128)(2,1)S(1)}, u32[]{:S(2)}, u32[]{:S(2)}) collective-permute-start(bf16[6,32,256]{2,1,0:T(8,128)(2,1)S(1)} %get-tuple-element.26.o1), channel_id=1, source_target_pairs={{0,8},{8,0},{16,24},{24,16},{32,40},{40,32},{48,56},{56,48},{64,72... | collective-permute-start | bytes 294920 | tf_op jit(solution)/shard_map/ppermute | solution.py:289
  14.7 11.6 %collective-permute-start.1 = (bf16[6,32,256]{2,1,0:T(8,128)(2,1)S(1)}, bf16[6,32,256]{2,1,0:T(8,128)(2,1)S(1)}, u32[]{:S(2)}, u32[]{:S(2)}) collective-permute-start(bf16[6,32,256]{2,1,0:T(8,128)(2,1)S(1)} %get-tuple-element.27.o0), channel_id=1, source_target_pairs={{0,760},{8,16},{16,8},{24,32},{32,24},{40,48},{48,40},{56,64},{64,... | collective-permute-start | bytes 294920 | tf_op jit(solution)/shard_map/ppermute | solution.py:289
  37.5 9.8 %collective-permute-start.4 = (f32[16,128]{1,0:T(8,128)S(1)}, f32[16,128]{1,0:T(8,128)S(1)}, u32[]{:S(2)}, u32[]{:S(2)}) collective-permute-start(f32[16,128]{1,0:T(8,128)S(1)} %get-tuple-element.40.before), channel_id=1, source_target_pairs={{0,760},{8,16},{16,8},{24,32},{32,24},{40,48},{48,40},{56,64},{64,... | collective-permute-start | bytes 24584 | tf_op jit(solution)/shard_map/ppermute | solution.py:289
  44.4 4.4 %collective-permute-start.5 = (f32[16,128]{1,0:T(8,128)S(1)}, f32[16,128]{1,0:T(8,128)S(1)}, u32[]{:S(2)}, u32[]{:S(2)}) collective-permute-start(f32[16,128]{1,0:T(8,128)S(1)} %get-tuple-element.40.before), channel_id=1, source_target_pairs={{0,8},{8,0},{16,24},{24,16},{32,40},{40,32},{48,56},{56,48},{64,72... | collective-permute-start | bytes 24584 | tf_op jit(solution)/shard_map/ppermute | solution.py:289
  49.1 7.7 %collective-permute-start.6 = (f32[16,128]{1,0:T(8,128)S(1)}, f32[16,128]{1,0:T(8,128)S(1)}, u32[]{:S(2)}, u32[]{:S(2)}) collective-permute-start(f32[16,128]{1,0:T(8,128)S(1)} %shard_map.156.before), channel_id=1, source_target_pairs={{0,760},{8,16},{16,8},{24,32},{32,24},{40,48},{48,40},{56,64},{64,... | collective-permute-start | bytes 24584 | tf_op jit(solution)/shard_map/ppermute | solution.py:289
  52.4 4.4 %collective-permute-start.7 = (f32[16,128]{1,0:T(8,128)S(1)}, f32[16,128]{1,0:T(8,128)S(1)}, u32[]{:S(2)}, u32[]{:S(2)}) collective-permute-start(f32[16,128]{1,0:T(8,128)S(1)} %shard_map.156.before), channel_id=1, source_target_pairs={{0,8},{8,0},{16,24},{24,16},{32,40},{40,32},{48,56},{56,48},{64,72... | collective-permute-start | bytes 24584 | tf_op jit(solution)/shard_map/ppermute | solution.py:289
  54.4 13.4 %copy-start.13 = (f32[125,8]{0,1:T(8,128)S(1)}, f32[125,8]{0,1:T(8,128)}, u32[]{:S(2)}) copy-start(f32[125,8]{0,1:T(8,128)} %param.27) | copy-start | bytes 12004

commit v5 on v4

--- a/solution.py
+++ b/solution.py
@@ -148,7 +148,8 @@
     done[...] = jnp.zeros_like(done)
 
 
-def mixed_kernel(mix, flux, local, residual, done, out, sems):
+def mixed_kernel(mix, flux, local, owner, slot, residual, done, select, out, sems):
+    select[...] = one_hot(keys_of(owner, slot))
     sends = []
     for q in range(NV):
         for low in range(0, NN, 16):
@@ -246,12 +247,11 @@
         blocks[m] = scratch[...]
 
 
-def correction_kernel(blocks, prolong_t, owner, slot, correction, wide, out, sems):
+def correction_kernel(blocks, prolong_t, select, correction, wide, out, sems):
     high, low = (x.astype(F32) for x in split(prolong_t[...]))
     weights = jnp.concatenate([high, low, high], axis=0)
     gap = jnp.zeros((weights.shape[0], wide.shape[0] // NV - NN), F32)
     weights = jnp.concatenate([weights, gap], axis=1).T.astype(BF)
-    select = one_hot(keys_of(owner, slot))
     group = lax.broadcasted_iota(jnp.int32, (8, 128), 1) // ASLOT
     step = wide.shape[0] // NV
     for v in range(NV):
@@ -270,7 +270,7 @@
         wide[step * v : step * (v + 1)] = dot(weights, values).astype(BF)
     sends = []
     for first in range(0, NV, 2):
-        found = dot(wide[step * first : step * (first + 2)], select)
+        found = dot(wide[step * first : step * (first + 2)], select[...])
         for v in (first, first + 1):
             out[v] = found[step * (v - first) : step * (v - first) + NN].astype(BF)
             sends.append(pltpu.make_async_copy(out.at[v], correction.at[v], sems.at[v]))
@@ -379,12 +379,14 @@
     )
     far_c, near_c = swapped(coarse, 1), swapped(coarse, 0)
     local, _ = lax.optimization_barrier((local, coarse))
-    residual, done = call(
+    residual, done, select = call(
         mixed_kernel,
-        (field, mark),
+        (field, mark, struct((MEMBERS * ASLOT, elems), BF)),
         linear_flux_matrix,
         flux,
         local,
+        owner,
+        slot,
         smem=(0,),
         hbm_out=(0,),
         scratch=[pltpu.VMEM((NV, NN, elems), BF), pltpu.SemaphoreType.DMA((NV,))],
@@ -406,8 +408,7 @@
         field,
         blocks,
         jnp.transpose(prolongation_weight),
-        owner,
-        slot,
+        select,
         hbm_out=(0,),
         scratch=[
             pltpu.VMEM((128 * NV, MEMBERS * ASLOT), BF),

time: 69.4 us -> 69.4 us (level)
  no operation moved by 1% of the time
where the time goes in v5:
time: 69.4 us; the launch traced here: 69.1 us
  starting transfers between devices  36.1 us (52%)
  blocking collectives  21 us (30%)
  Pallas kernels  7.96 us (11%)
  waiting for transfers between devices  1.9 us (3%)
  local copies, waits for them, and re-layouts  1.19 us (2%)
  between operations  0.98 us (1%)
    ppermute x6, starting transfers between devices, swapped(): lax.ppermute(value, 'gx', [(i, (i + (1 if i % 2 == start else -1)) % size...  25.5 us
    all_to_all x2, blocking collectives, per_device(): blocks = lax.all_to_all(blocks, 'gy', 0, 0, tiled=True)  21 us
    ppermute x2, starting transfers between devices, shifted(): lax.ppermute(value, axis, [(i, (i + by) % size) for i in range(size)])  10.5 us
    pallas_call x11, Pallas kernels, call(): pl.pallas_call(kernel, out_shape=outs, in_specs=[SMEM if i in smem else V...  7.96 us
    ppermute x6, waiting for transfers between devices, swapped(): lax.ppermute(value, 'gx', [(i, (i + (1 if i % 2 == start else -1)) % size...  1.9 us
  transfers between devices with their start and end apart: 8, of which 2 were waited for; matrix products, arithmetic and copies ran while one was open for 0% of the time, Pallas kernels for 7%

profile of v5, /device:TPU:1, one launch (start us, length us, event | category | flops | bytes accessed | tf_op | source)
XLA Modules:
  0.0 69.1 jit_solution(17081416954576592631)
XLA Ops:
  0.6 0.0 copy-start.1
  0.6 1.1 %copy-done.1 = bf16[6,125,512]{2,1,0:T(8,128)(2,1)S(1)} copy-done((bf16[6,125,512]{2,1,0:T(8,128)(2,1)S(1)}, bf16[6,125,512]{2,1,0:T(8,128)(2,1)}, u32[]{:S(2)}) %copy-start.1) | copy-done | bytes 768024
  1.8 0.0 copy-start.3
  1.8 0.0 copy-start.7
  1.8 0.0 copy-start.4
  1.8 0.0 copy-start.5
  1.8 0.0 copy-start.6
  1.8 0.0 copy-start.14
  1.8 0.0 copy-start.2
  1.8 0.0 copy-start.8
  1.8 0.0 copy-start.11
  1.8 0.0 copy-start.12
  1.8 0.3 shard_map.149
  2.2 0.0 copy-start
  2.2 0.0 copy-start.9
  2.2 0.0 copy-start.10
  2.2 10.5 %collective-permute-start.3 = (bf16[6,32,512]{2,1,0:T(8,128)(2,1)S(1)}, bf16[6,32,512]{2,1,0:T(8,128)(2,1)S(1)}, u32[]{:S(2)}, u32[]{:S(2)}) collective-permute-start(bf16[6,32,512]{2,1,0:T(8,128)(2,1)S(1)} %get-tuple-element.30.o2), channel_id=1, source_target_pairs={{0,7},{1,0},{2,1},{3,2},{4,3},{5,4},{6,5},{7,6},{8,15},{9,8},{10,9... | collective-permute-start | bytes 589832 | tf_op jit(solution)/shard_map/ppermute | solution.py:284
  12.8 0.0 collective-permute-start.2
  12.8 1.9 %collective-permute-start = (bf16[6,32,256]{2,1,0:T(8,128)(2,1)S(1)}, bf16[6,32,256]{2,1,0:T(8,128)(2,1)S(1)}, u32[]{:S(2)}, u32[]{:S(2)}) collective-permute-start(bf16[6,32,256]{2,1,0:T(8,128)(2,1)S(1)} %get-tuple-element.27.o1), channel_id=1, source_target_pairs={{0,8},{8,0},{16,24},{24,16},{32,40},{40,32},{48,56},{56,48},{64,72... | collective-permute-start | bytes 294920 | tf_op jit(solution)/shard_map/ppermute | solution.py:289
  14.7 9.6 %collective-permute-start.1 = (bf16[6,32,256]{2,1,0:T(8,128)(2,1)S(1)}, bf16[6,32,256]{2,1,0:T(8,128)(2,1)S(1)}, u32[]{:S(2)}, u32[]{:S(2)}) collective-permute-start(bf16[6,32,256]{2,1,0:T(8,128)(2,1)S(1)} %get-tuple-element.28.o0), channel_id=1, source_target_pairs={{0,760},{8,16},{16,8},{24,32},{32,24},{40,48},{48,40},{56,64},{64,... | collective-permute-start | bytes 294920 | tf_op jit(solution)/shard_map/ppermute | solution.py:289
  24.3 0.0 copy-done.3
  24.3 0.0 copy-done.7
  24.3 0.3 shard_map.152.coarse_side
  24.5 0.0 copy-done.4
  24.6 0.0 copy-done.5
  24.6 0.0 copy-done.6
  24.6 0.0 copy-done.14
  24.6 0.4 shard_map.150
  24.9 0.0 copy-done.2
  25.0 0.0 copy-done.8
  25.0 0.0 copy-done.11
  25.0 0.0 copy-done.12
  25.0 0.0 copy-done
  25.0 1.3 %shard_map.151 = (bf16[6,96,512]{2,1,0:T(8,128)(2,1)S(1)}, f32[48,512]{1,0:T(8,128)S(1)}) custom-call(f32[6,6]{1,0:T(8,128)S(1)} %copy-done.8, bf16[6,125,512]{2,1,0:T(8,128)(2,1)S(1)} %copy-done, bf16[6,125,512]{2,1,0:T(8,128)(2,1)S(1)} %copy-done.2, f32[1,512]{1,0:T(1,128)S(1)} %bitcast.14, s32[1,512]{1,0:T(1,128)S(1)} %bitcast.16, ...), custom_call_target="tpu_custom_call" | custom-call | flops 1000 | bytes 1000 | tf_op jit(solution)/shard_map/pallas_call | solution.py:48
  26.3 0.0 collective-permute-done.n1
  26.3 0.0 collective-permute-done.1.n0
  26.3 0.0 collective-permute-done.3.n3
  26.3 0.0 collective-permute-done.2.n2
  26.3 0.0 copy-done.9
  26.3 0.0 copy-done.10
  26.3 0.6 shard_map.153
  26.9 10.4 %all_to_all.10.blocks = f32[8,16,128]{2,1,0:T(8,128)S(1)} all-to-all(f32[8,16,128]{2,1,0:T(8,128)S(1)} %get-tuple-element.39), channel_id=1, replica_groups=mesh['gx'=96,'gy'=8] {'gy'}, dimensions={0} | all-to-all | bytes 131072 | tf_op jit(solution)/shard_map/all_to_all | solution.py:358
  37.3 0.2 shard_map.154
  37.5 6.9 %collective-permute-start.4 = (f32[16,128]{1,0:T(8,128)S(1)}, f32[16,128]{1,0:T(8,128)S(1)}, u32[]{:S(2)}, u32[]{:S(2)}) collective-permute-start(f32[16,128]{1,0:T(8,128)S(1)} %get-tuple-element.41.before), channel_id=1, source_target_pairs={{0,760},{8,16},{16,8},{24,32},{32,24},{40,48},{48,40},{56,64},{64,... | collective-permute-start | bytes 24584 | tf_op jit(solution)/shard_map/ppermute | solution.py:289
  44.4 1.9 %collective-permute-start.5 = (f32[16,128]{1,0:T(8,128)S(1)}, f32[16,128]{1,0:T(8,128)S(1)}, u32[]{:S(2)}, u32[]{:S(2)}) collective-permute-start(f32[16,128]{1,0:T(8,128)S(1)} %get-tuple-element.41.before), channel_id=1, source_target_pairs={{0,8},{8,0},{16,24},{24,16},{32,40},{40,32},{48,56},{56,48},{64,72... | collective-permute-start | bytes 24584 | tf_op jit(solution)/shard_map/ppermute | solution.py:289
  46.3 0.9 %shard_map.155 = (f32[6,128,512]{2,1,0:T(8,128)S(1)}, f32[6,125,512]{2,1,0:T(8,128)S(1)}, f32[8,128]{1,0:T(8,128)S(1)}) custom-call(bf16[6,125,512]{2,1,0:T(8,128)(2,1)S(1)} %copy-done, bf16[6,125,512]{2,1,0:T(8,128)(2,1)S(1)} %copy-done.2, bf16[125,125]{1,0:T(8,128)(2,1)S(1)} %copy-done.5, bf16[125,125]{1,0:T(8,128)(2,1)S(1)} %copy-done.6, ...), custom_call_target="tpu_custom_call" | custom-call | flops 1000 | bytes 1000 | tf_op jit(solution)/shard_map/pallas_call | solution.py:48
  47.2 0.0 collective-permute-done.4.up
  47.3 1.5 %collective-permute-done.5.down = f32[16,128]{1,0:T(8,128)S(1)} collective-permute-done((f32[16,128]{1,0:T(8,128)S(1)}, f32[16,128]{1,0:T(8,128)S(1)}, u32[]{:S(2)}, u32[]{:S(2)}) %collective-permute-start.5) | collective-permute-done | bytes 8224 | tf_op jit(solution)/shard_map/ppermute | solution.py:289
  48.8 0.3 shard_map.156.before
  49.1 3.3 %collective-permute-start.6 = (f32[16,128]{1,0:T(8,128)S(1)}, f32[16,128]{1,0:T(8,128)S(1)}, u32[]{:S(2)}, u32[]{:S(2)}) collective-permute-start(f32[16,128]{1,0:T(8,128)S(1)} %shard_map.156.before), channel_id=1, source_target_pairs={{0,760},{8,16},{16,8},{24,32},{32,24},{40,48},{48,40},{56,64},{64,... | collective-permute-start | bytes 24584 | tf_op jit(solution)/shard_map/ppermute | solution.py:289
  52.4 1.9 %collective-permute-start.7 = (f32[16,128]{1,0:T(8,128)S(1)}, f32[16,128]{1,0:T(8,128)S(1)}, u32[]{:S(2)}, u32[]{:S(2)}) collective-permute-start(f32[16,128]{1,0:T(8,128)S(1)} %shard_map.156.before), channel_id=1, source_target_pairs={{0,8},{8,0},{16,24},{24,16},{32,40},{40,32},{48,56},{56,48},{64,72... | collective-permute-start | bytes 24584 | tf_op jit(solution)/shard_map/ppermute | solution.py:289
  54.4 0.0 copy-start.13
  54.4 2.1 %shard_map.157 = (bf16[6,125,512]{2,1,0:T(8,128)(2,1)}, f32[8,128]{1,0:T(8,128)S(1)}, bf16[256,512]{1,0:T(8,128)(2,1)S(1)}) custom-call(f32[6,6]{1,0:T(8,128)S(1)} %copy-done.8, f32[6,128,512]{2,1,0:T(8,128)S(1)} %get-tuple-element.44.flux, f32[6,125,512]{2,1,0:T(8,128)S(1)} %get-tuple-element.48.local, s32[1,512]{1,0:T(1,128)S(1)} %bitcast.11, ...), custom_call_target="tpu_custom_call" | custom-call | flops 1000 | bytes 1000 | tf_op jit(solution)/shard_map/pallas_call | solution.py:48
  56.4 0.4 collective-permute-done.6.up
  56.8 0.0 collective-permute-done.7.down
  56.8 0.3 shard_map.158
  57.2 10.6 %all_to_all.11.blocks = f32[8,16,128]{2,1,0:T(8,128)S(1)} all-to-all(f32[8,16,128]{2,1,0:T(8,128)S(1)} %shard_map.158), channel_id=1, replica_groups=mesh['gx'=96,'gy'=8] {'gy'}, dimensions={0} | all-to-all | bytes 131072 | tf_op jit(solution)/shard_map/all_to_all | solution.py:405
  67.7 0.0 copy-done.13
  67.7 1.3 %shard_map.159 = bf16[6,125,512]{2,1,0:T(8,128)(2,1)} custom-call(f32[8,16,128]{2,1,0:T(8,128)S(1)} %all_to_all.11.blocks, f32[8,125]{1,0:T(8,128)S(1)} %bitcast.18, bf16[256,512]{1,0:T(8,128)(2,1)S(1)} %get-tuple-element.51.select), custom_call_target="tpu_custom_call" | custom-call | flops 1000 | bytes 1000 | tf_op jit(solution)/shard_map/pallas_call | solution.py:48
Async XLA Ops:
  0.6 1.1 %copy-start.1 = (bf16[6,125,512]{2,1,0:T(8,128)(2,1)S(1)}, bf16[6,125,512]{2,1,0:T(8,128)(2,1)}, u32[]{:S(2)}) copy-start(bf16[6,125,512]{2,1,0:T(8,128)(2,1)} %state.5) | copy-start | bytes 2304004
  1.8 22.5 %copy-start.3 = (f32[48,48,32]{1,2,0:T(8,128)S(1)}, f32[48,48,32]{1,2,0:T(8,128)}, u32[]{:S(2)}) copy-start(f32[48,48,32]{1,2,0:T(8,128)} %param.25) | copy-start | bytes 884740
  1.8 22.5 %copy-start.7 = (f32[48,48]{1,0:T(8,128)S(1)}, f32[48,48]{1,0:T(8,128)}, u32[]{:S(2)}) copy-start(f32[48,48]{1,0:T(8,128)} %coupling.1) | copy-start | bytes 27652
  1.8 22.8 %copy-start.4 = (bf16[6,125,25]{1,2,0:T(8,128)(2,1)S(1)}, bf16[6,125,25]{1,2,0:T(8,128)(2,1)}, u32[]{:S(2)}) copy-start(bf16[6,125,25]{1,2,0:T(8,128)(2,1)} %param.20) | copy-start | bytes 112504
  1.8 22.8 %copy-start.5 = (bf16[125,125]{1,0:T(8,128)(2,1)S(1)}, bf16[125,125]{1,0:T(8,128)(2,1)}, u32[]{:S(2)}) copy-start(bf16[125,125]{1,0:T(8,128)(2,1)} %volume.3) | copy-start | bytes 93754
  1.8 22.8 %copy-start.6 = (bf16[125,125]{1,0:T(8,128)(2,1)S(1)}, bf16[125,125]{1,0:T(8,128)(2,1)}, u32[]{:S(2)}) copy-start(bf16[125,125]{1,0:T(8,128)(2,1)} %viscous.3) | copy-start | bytes 93754
  1.8 22.8 %copy-start.14 = (f32[8,125]{1,0:T(8,128)S(1)}, f32[8,125]{1,0:T(8,128)}, u32[]{:S(2)}) copy-start(f32[8,125]{1,0:T(8,128)} %restrict) | copy-start | bytes 12004
  1.8 23.2 %copy-start.2 = (bf16[6,125,512]{2,1,0:T(8,128)(2,1)S(1)}, bf16[6,125,512]{2,1,0:T(8,128)(2,1)}, u32[]{:S(2)}) copy-start(bf16[6,125,512]{2,1,0:T(8,128)(2,1)} %state.5) | copy-start | bytes 2304004
  1.8 23.2 %copy-start.8 = (f32[6,6]{1,0:T(8,128)S(1)}, f32[6,6]{1,0:T(8,128)}, u32[]{:S(2)}) copy-start(f32[6,6]{1,0:T(8,128)} %mix.3) | copy-start | bytes 436
  1.8 23.2 %copy-start.11 = (f32[512]{0:T(512)S(1)}, f32[512]{0:T(512)}, u32[]{:S(2)}) copy-start(f32[512]{0:T(512)} %param.19) | copy-start | bytes 6148
  1.8 23.2 %copy-start.12 = (s32[512]{0:T(512)S(1)}, s32[512]{0:T(512)}, u32[]{:S(2)}) copy-start(s32[512]{0:T(512)} %param.21) | copy-start | bytes 6148
  2.2 22.8 %copy-start = (bf16[6,125,512]{2,1,0:T(8,128)(2,1)S(1)}, bf16[6,125,512]{2,1,0:T(8,128)(2,1)}, u32[]{:S(2)}) copy-start(bf16[6,125,512]{2,1,0:T(8,128)(2,1)} %forcing.3) | copy-start | bytes 2304004
  2.2 24.1 %copy-start.9 = (s32[512,1]{0,1:T(1,128)S(1)}, s32[512,1]{0,1:T(1,128)}, u32[]{:S(2)}) copy-start(s32[512,1]{0,1:T(1,128)} %param.23) | copy-start | bytes 6148
  2.2 24.1 %copy-start.10 = (s32[512]{0:T(512)S(1)}, s32[512]{0:T(512)}, u32[]{:S(2)}) copy-start(s32[512]{0:T(512)} %param.24) | copy-start | bytes 6148
  2.2 24.1 %collective-permute-start.3 = (bf16[6,32,512]{2,1,0:T(8,128)(2,1)S(1)}, bf16[6,32,512]{2,1,0:T(8,128)(2,1)S(1)}, u32[]{:S(2)}, u32[]{:S(2)}) collective-permute-start(bf16[6,32,512]{2,1,0:T(8,128)(2,1)S(1)} %get-tuple-element.30.o2), channel_id=1, source_target_pairs={{0,7},{1,0},{2,1},{3,2},{4,3},{5,4},{6,5},{7,6},{8,15},{9,8},{10,9... | collective-permute-start | bytes 589832 | tf_op jit(solution)/shard_map/ppermute | solution.py:284
  12.8 13.5 %collective-permute-start.2 = (bf16[6,32,512]{2,1,0:T(8,128)(2,1)S(1)}, bf16[6,32,512]{2,1,0:T(8,128)(2,1)S(1)}, u32[]{:S(2)}, u32[]{:S(2)}) collective-permute-start(bf16[6,32,512]{2,1,0:T(8,128)(2,1)S(1)} %get-tuple-element.29.o3), channel_id=1, source_target_pairs={{0,1},{1,2},{2,3},{3,4},{4,5},{5,6},{6,7},{7,0},{8,9},{9,10},{10,1... | collective-permute-start | bytes 589832 | tf_op jit(solution)/shard_map/ppermute | solution.py:284
  12.8 13.5 %collective-permute-start = (bf16[6,32,256]{2,1,0:T(8,128)(2,1)S(1)}, bf16[6,32,256]{2,1,0:T(8,128)(2,1)S(1)}, u32[]{:S(2)}, u32[]{:S(2)}) collective-permute-start(bf16[6,32,256]{2,1,0:T(8,128)(2,1)S(1)} %get-tuple-element.27.o1), channel_id=1, source_target_pairs={{0,8},{8,0},{16,24},{24,16},{32,40},{40,32},{48,56},{56,48},{64,72... | collective-permute-start | bytes 294920 | tf_op jit(solution)/shard_map/ppermute | solution.py:289
  14.7 11.6 %collective-permute-start.1 = (bf16[6,32,256]{2,1,0:T(8,128)(2,1)S(1)}, bf16[6,32,256]{2,1,0:T(8,128)(2,1)S(1)}, u32[]{:S(2)}, u32[]{:S(2)}) collective-permute-start(bf16[6,32,256]{2,1,0:T(8,128)(2,1)S(1)} %get-tuple-element.28.o0), channel_id=1, source_target_pairs={{0,760},{8,16},{16,8},{24,32},{32,24},{40,48},{48,40},{56,64},{64,... | collective-permute-start | bytes 294920 | tf_op jit(solution)/shard_map/ppermute | solution.py:289
  37.5 9.8 %collective-permute-start.4 = (f32[16,128]{1,0:T(8,128)S(1)}, f32[16,128]{1,0:T(8,128)S(1)}, u32[]{:S(2)}, u32[]{:S(2)}) collective-permute-start(f32[16,128]{1,0:T(8,128)S(1)} %get-tuple-element.41.before), channel_id=1, source_target_pairs={{0,760},{8,16},{16,8},{24,32},{32,24},{40,48},{48,40},{56,64},{64,... | collective-permute-start | bytes 24584 | tf_op jit(solution)/shard_map/ppermute | solution.py:289
  44.4 4.4 %collective-permute-start.5 = (f32[16,128]{1,0:T(8,128)S(1)}, f32[16,128]{1,0:T(8,128)S(1)}, u32[]{:S(2)}, u32[]{:S(2)}) collective-permute-start(f32[16,128]{1,0:T(8,128)S(1)} %get-tuple-element.41.before), channel_id=1, source_target_pairs={{0,8},{8,0},{16,24},{24,16},{32,40},{40,32},{48,56},{56,48},{64,72... | collective-permute-start | bytes 24584 | tf_op jit(solution)/shard_map/ppermute | solution.py:289
  49.1 7.7 %collective-permute-start.6 = (f32[16,128]{1,0:T(8,128)S(1)}, f32[16,128]{1,0:T(8,128)S(1)}, u32[]{:S(2)}, u32[]{:S(2)}) collective-permute-start(f32[16,128]{1,0:T(8,128)S(1)} %shard_map.156.before), channel_id=1, source_target_pairs={{0,760},{8,16},{16,8},{24,32},{32,24},{40,48},{48,40},{56,64},{64,... | collective-permute-start | bytes 24584 | tf_op jit(solution)/shard_map/ppermute | solution.py:289
  52.4 4.4 %collective-permute-start.7 = (f32[16,128]{1,0:T(8,128)S(1)}, f32[16,128]{1,0:T(8,128)S(1)}, u32[]{:S(2)}, u32[]{:S(2)}) collective-permute-start(f32[16,128]{1,0:T(8,128)S(1)} %shard_map.156.before), channel_id=1, source_target_pairs={{0,8},{8,0},{16,24},{24,16},{32,40},{40,32},{48,56},{56,48},{64,72... | collective-permute-start | bytes 24584 | tf_op jit(solution)/shard_map/ppermute | solution.py:289
  54.4 13.4 %copy-start.13 = (f32[125,8]{0,1:T(8,128)S(1)}, f32[125,8]{0,1:T(8,128)}, u32[]{:S(2)}) copy-start(f32[125,8]{0,1:T(8,128)} %param.27) | copy-start | bytes 12004
